TPU v7x, 32 devices: a whole 2x2x4 slice. The times are simulated.
32 devices in a mesh: parts: 2 (over y), row: 4 (over z), col: 4 (over x, core).
Axes of the slice: x: 2, y: 2, z: 4, core: 2. Of those that a mesh axis runs over, the one named last changes fastest.
Arguments:
- features: bfloat16 [8192, 128], P(('parts', 'col', 'row')), parts along dimension 0, may hold values from -6 to 6
- block_values: bfloat16 [4096, 128, 128], P(('parts', 'row', 'col')), parts along dimension 0, may hold values from -0.25 to 0.25
- block_rows: int32 [4096], P(('parts', 'row', 'col')), parts along dimension 0, may hold values from 0 to 7
- block_cols: int32 [4096], P(('parts', 'row', 'col')), parts along dimension 0, may hold values from 0 to 7
- block_count: int32 [32], P(('parts', 'row', 'col')), parts along dimension 0, may hold values from 32 to 128, as said below
- weight: bfloat16 [128, 256], replicated, may hold values from -0.5 to 0.5
- bias: float32 [256], replicated, may hold values from -3 to 3
- cotangent: bfloat16 [8192, 256], P(('parts', 'row', 'col')), parts along dimension 0, may hold values from -6 to 6
Outputs:
- hidden: bfloat16 [8192, 256], P(('parts', 'row', 'col')), parts along dimension 0
- grad_weight: float32 [256, 256], P('parts'), parts along dimension 0
- grad_bias: float32 [512], P('parts'), parts along dimension 0
- grad_features: bfloat16 [8192, 128], P(('parts', 'col', 'row')), parts along dimension 0
There are 2 independent parts, one for each index of `parts`. A program takes and returns all parts, laid end to end along the dimension named above; an argument that names none is the same for every part. Nothing has to cross between parts.
Inputs may be any that keep to these rules, and one draw needn't show every extreme that they name: `block_count`: slot j of a device is live when j is below the device's count; some device of every partition has 128 live slots.
All inputs are finite; a program needn't handle non-finite values.
Results may differ from a plain program's by a relative error of at most 0.02.
Values may be sent and summed in bfloat16 or wider, within the bound.
No kernel may reach another device: no remote copies, remote signals or barrier semaphores. Data moves between devices by JAX's collectives and lax.ppermute only.
A program may use at most 64 MiB of HBM per device.

v0:
```python
import jax
import jax.numpy as jnp
from jax import lax
from jax.sharding import PartitionSpec as P


def pick_rows(pick_index, live_mask, source_rows):
    source_count = source_rows.shape[0]
    onehot = (
        (pick_index[:, None] == jnp.arange(source_count, dtype=jnp.int32)[None, :])
        & live_mask[:, None]
    ).astype(jnp.bfloat16)
    chosen = jnp.dot(
        onehot, source_rows.reshape(source_count, -1), preferred_element_type=jnp.float32
    ).astype(jnp.bfloat16)
    return chosen.reshape((pick_index.shape[0],) + source_rows.shape[1:])


def slot_terms(values, pick_index, live_mask, source_rows, forward_pass):
    chosen = pick_rows(pick_index, live_mask, source_rows)
    if forward_pass:
        return jnp.einsum("spq,sqf->spf", values, chosen, preferred_element_type=jnp.float32)
    return jnp.einsum("spq,spf->sqf", values, chosen, preferred_element_type=jnp.float32)


def place_terms(products, place_index, blocks):
    block_ids = jnp.arange(blocks, dtype=jnp.int32)
    onehot = (block_ids[:, None] == place_index[None, :]).astype(jnp.bfloat16)
    flat = products.reshape(products.shape[0], -1)
    upper = flat.astype(jnp.bfloat16)
    lower = (flat - upper.astype(jnp.float32)).astype(jnp.bfloat16)
    placed = jnp.dot(onehot, upper, preferred_element_type=jnp.float32)
    placed = placed + jnp.dot(onehot, lower, preferred_element_type=jnp.float32)
    return placed.reshape(blocks * products.shape[1], products.shape[2])


def on_device(features, block_values, block_rows, block_cols, block_count, weight, bias, cotangent):
    block_size = block_values.shape[1]
    slot_total = block_values.shape[0]
    live_mask = jnp.arange(slot_total, dtype=jnp.int32) < block_count[0]
    node_rows = cotangent.shape[0]
    width_in = features.shape[1]
    column_rows = lax.all_gather(features, "row", axis=0, tiled=True)
    column_blocks = column_rows.reshape(-1, block_size, width_in)
    forward_terms = slot_terms(block_values, block_cols, live_mask, column_blocks, True)
    aggregate = lax.psum_scatter(
        place_terms(
            forward_terms, block_rows, lax.axis_size("col") * node_rows // block_size
        ).astype(jnp.bfloat16),
        "col",
        scatter_dimension=0,
        tiled=True,
    ).astype(jnp.float32)
    aggregate = aggregate.astype(jnp.bfloat16)
    pre_act = jnp.dot(aggregate, weight, preferred_element_type=jnp.float32) + bias
    sigmoid_pre = jax.nn.sigmoid(pre_act)
    hidden = (pre_act * sigmoid_pre).astype(jnp.bfloat16)
    pre_grad = (
        cotangent.astype(jnp.float32) * sigmoid_pre * (1.0 + pre_act * (1.0 - sigmoid_pre))
    ).astype(jnp.bfloat16)
    grad_local = lax.dot_general(
        aggregate, pre_grad, (((0,), (0,)), ((), ())), preferred_element_type=jnp.float32
    )
    bias_local = jnp.sum(pre_grad.astype(jnp.float32), axis=0)
    grad_weight, grad_bias = lax.psum((grad_local, bias_local), ("row", "col"))
    norm_scale = float(node_rows * lax.axis_size("row") * lax.axis_size("col")) ** (-0.5)
    agg_grad = lax.dot_general(
        pre_grad, weight, (((1,), (1,)), ((), ())), preferred_element_type=jnp.float32
    ).astype(jnp.bfloat16)
    stripe_rows = lax.all_gather(agg_grad, "col", axis=0, tiled=True)
    stripe_blocks = stripe_rows.reshape(-1, block_size, width_in)
    backward_terms = slot_terms(block_values, block_rows, live_mask, stripe_blocks, False)
    grad_features = lax.psum_scatter(
        place_terms(
            backward_terms, block_cols, lax.axis_size("row") * node_rows // block_size
        ).astype(jnp.bfloat16),
        "row",
        scatter_dimension=0,
        tiled=True,
    )
    return (hidden, grad_weight * norm_scale, grad_bias * norm_scale, grad_features)


def solution(mesh):
    in_specs = (
        P(("parts", "col", "row"), None),
        P(("parts", "row", "col"), None, None),
        P(("parts", "row", "col")),
        P(("parts", "row", "col")),
        P(("parts", "row", "col")),
        P(),
        P(),
        P(("parts", "row", "col"), None),
    )
    out_specs = (
        P(("parts", "row", "col"), None),
        P("parts", None),
        P("parts"),
        P(("parts", "col", "row"), None),
    )
    return jax.shard_map(
        on_device, mesh=mesh, in_specs=in_specs, out_specs=out_specs, check_vma=False
    )
```

profile of v0, /device:TPU:0, one launch (start us, length us, event | category | flops | bytes accessed | tf_op | source)
XLA Modules:
  0.0 195.0 jit_solution(1188521184960498027)
XLA Ops:
  7.9 15.8 %all_gather.6 = bf16[1024,128]{1,0:T(8,128)(2,1)S(1)} all-gather(bf16[256,128]{1,0:T(8,128)(2,1)} %param.8), channel_id=1, replica_groups=mesh['parts'=2,'row'=4,'col'=4] {'row'}, dimensions={0}, use_global_device_ids=true | all-gather | bytes 327680 | tf_op jit(solution)/shard_map/all_gather | solution.py:43
  23.7 0.1 reshape_reshape.6
  23.8 1.9 fusion.4
  25.8 1.2 copy.20
  27.1 0.9 copy-done.2
  28.0 6.3 %convolution_bitcast_fusion.1 = f32[128,128,128]{1,2,0:T(8,128)} fusion(bf16[128,128,128]{2,1,0:T(8,128)(2,1)S(1)} %bitcast.40, bf16[128,128,128]{2,1,0:T(8,128)(2,1)S(1)} %copy-done.2), kind=kOutput, calls=%fused_computation.13 | convolution fusion | flops 536870912 | bytes 16777216 | tf_op jit(solution)/shard_map/spq,sqf->spf/dot_general | solution.py:22
  34.3 9.4 %copy.15 = f32[128,128,128]{0,2,1:T(8,128)} copy(f32[128,128,128]{1,2,0:T(8,128)} %convolution_bitcast_fusion.1) | data formatting | bytes 16777216 | tf_op jit(solution)/shard_map/spq,sqf->spf/dot_general | solution.py:22
  43.7 4.0 %fusion.3 = (bf16[128,16384]{0,1:T(8,128)(2,1)S(1)}, bf16[128,16384]{0,1:T(8,128)(2,1)S(1)}) fusion(f32[128,128,128]{0,2,1:T(8,128)} %copy.15), kind=kLoop, calls=%fused_computation.11 | loop fusion | flops 8388608 | bytes 16777216 | tf_op jit(solution)/shard_map/convert_element_type | solution.py:31
  47.8 1.2 fusion.15
  49.0 1.2 fusion
  50.2 0.8 convert_element_type.62
  51.1 21.7 %reduce-scatter.3.cloned.1.call-done = bf16[256,128]{1,0:T(8,128)(2,1)} async-done(((bf16[1024,128]{1,0:T(8,128)(2,1)}), bf16[256,128]{1,0:T(8,128)(2,1)}) %reduce-scatter.3.cloned.1.call-update) | async-done | bytes 65552 | tf_op jit(solution)/shard_map/reduce_scatter | solution.py:46
  72.8 1.8 convert_reduce_fusion
  74.5 0.2 convolution_convert_fusion.2
  74.7 1.7 fusion.20
  76.4 0.0 reduce-scatter.5.cloned.1.call-start
  76.5 6.0 %all_gather.7 = bf16[1024,128]{1,0:T(8,128)(2,1)S(1)} all-gather(bf16[256,128]{1,0:T(8,128)(2,1)S(1)} %convolution_convert_fusion.2), channel_id=1, replica_groups=mesh['parts'=2,'row'=4,'col'=4] {'col'}, dimensions={0}, use_global_device_ids=true | all-gather | bytes 327680 | tf_op jit(solution)/shard_map/all_gather | solution.py:70
  82.5 0.1 reshape_reshape.7
  82.6 1.3 fusion.5
  83.9 1.2 copy.21
  85.1 0.9 copy-done.3
  86.1 4.8 %convolution_bitcast_fusion = f32[128,128,128]{1,2,0:T(8,128)} fusion(bf16[128,128,128]{2,1,0:T(8,128)(2,1)S(1)} %bitcast.41, bf16[128,128,128]{2,1,0:T(8,128)(2,1)S(1)} %copy-done.3), kind=kOutput, calls=%fused_computation.12 | convolution fusion | flops 536870912 | bytes 16777216 | tf_op jit(solution)/shard_map/spq,spf->sqf/dot_general | solution.py:23
  90.8 9.4 %copy.17 = f32[128,128,128]{0,2,1:T(8,128)} copy(f32[128,128,128]{1,2,0:T(8,128)} %convolution_bitcast_fusion) | data formatting | bytes 16777216 | tf_op jit(solution)/shard_map/spq,spf->sqf/dot_general | solution.py:23
  100.3 4.1 %fusion.2 = (bf16[128,16384]{0,1:T(8,128)(2,1)S(1)}, bf16[128,16384]{0,1:T(8,128)(2,1)S(1)}) fusion(f32[128,128,128]{0,2,1:T(8,128)} %copy.17), kind=kLoop, calls=%fused_computation.8 | loop fusion | flops 8388608 | bytes 16777216 | tf_op jit(solution)/shard_map/convert_element_type | solution.py:31
  104.4 1.2 fusion.14
  105.5 1.2 fusion.1
  106.7 0.8 convert_element_type.73
  107.6 32.8 %psum.15 = f32[256]{0:T(256)S(1)} all-reduce(f32[256]{0:T(256)S(1)} %get-tuple-element.6), channel_id=1, replica_groups=mesh['parts'=2,'row'=4,'col'=4] {'row','col'}, use_global_device_ids=true, to_apply=%region_3.0 | all-reduce | flops 256 | bytes 2048 | tf_op jit(solution)/shard_map/psum | solution.py:65
  140.4 0.6 broadcast_multiply_fusion.1
  141.0 23.2 %all-reduce.2.cloned.1.call-done = f32[128,256]{1,0:T(8,128)} async-done(((f32[128,256]{1,0:T(8,128)}), f32[128,256]{1,0:T(8,128)}) %all-reduce.2.cloned.1.call-update) | async-done | bytes 131088 | tf_op jit(solution)/shard_map/psum | solution.py:65
  164.2 1.6 broadcast_multiply_fusion
  165.8 22.7 %reduce-scatter.5.cloned.1.call-done = bf16[256,128]{1,0:T(8,128)(2,1)} async-done(((bf16[1024,128]{1,0:T(8,128)(2,1)}), bf16[256,128]{1,0:T(8,128)(2,1)}) %reduce-scatter.5.cloned.1.call-update) | async-done | bytes 65552 | tf_op jit(solution)/shard_map/reduce_scatter | solution.py:73
  (20 shorter events, 0.2 us)
Async XLA Ops:
  7.2 65.6 %copy-start = (bf16[128,256]{1,0:T(8,128)(2,1)S(1)}, bf16[128,256]{1,0:T(8,128)(2,1)}, u32[]{:S(2)}) copy-start(bf16[128,256]{1,0:T(8,128)(2,1)} %param.13) | copy-start | bytes 196612
  7.2 65.6 %reduce-scatter.3.cloned.1.call-start = ((), (), s32[]{:S(2)}) async-start(), calls=%async_computation.2 | async-start | bytes 327680 | tf_op jit(solution)/shard_map/reduce_scatter | solution.py:46
  25.8 2.2 %copy-start.2 = (bf16[128,128,128]{2,1,0:T(8,128)(2,1)S(1)}, bf16[128,128,128]{2,1,0:T(8,128)(2,1)}, u32[]{:S(2)}) copy-start(bf16[128,128,128]{2,1,0:T(8,128)(2,1)} %param.9) | copy-start | bytes 12582916
  43.7 4.0 %copy-start.4 = (s32[128]{0:T(128)S(1)}, s32[128]{0:T(128)}, u32[]{:S(2)}) copy-start(s32[128]{0:T(128)} %param.10) | copy-start | bytes 1540
  47.8 25.0 %copy-start.6 = (bf16[256,256]{1,0:T(8,128)(2,1)S(1)}, bf16[256,256]{1,0:T(8,128)(2,1)}, u32[]{:S(2)}) copy-start(bf16[256,256]{1,0:T(8,128)(2,1)} %param.15) | copy-start | bytes 393220
  47.8 25.0 %copy-start.7 = (f32[256]{0:T(256)S(1)}, f32[256]{0:T(256)}, u32[]{:S(2)}) copy-start(f32[256]{0:T(256)} %param.14) | copy-start | bytes 3076
  51.0 113.2 %all-reduce.2.cloned.1.call-start = ((), (), s32[]{:S(2)}) async-start(), calls=%async_computation.3 | async-start | bytes 262144 | tf_op jit(solution)/shard_map/psum | solution.py:65
  76.4 112.0 %reduce-scatter.5.cloned.1.call-start = ((), (), s32[]{:S(2)}) async-start(), calls=%async_computation.4 | async-start | bytes 327680 | tf_op jit(solution)/shard_map/reduce_scatter | solution.py:73
  83.9 2.2 %copy-start.3 = (bf16[128,128,128]{2,1,0:T(8,128)(2,1)S(1)}, bf16[128,128,128]{2,1,0:T(8,128)(2,1)}, u32[]{:S(2)}) copy-start(bf16[128,128,128]{2,1,0:T(8,128)(2,1)} %param.9) | copy-start | bytes 12582916
  100.3 4.1 %copy-start.5 = (s32[128]{0:T(128)S(1)}, s32[128]{0:T(128)}, u32[]{:S(2)}) copy-start(s32[128]{0:T(128)} %param.11) | copy-start | bytes 1540
  104.4 84.1 %copy-start.1 = (bf16[128,256]{1,0:T(8,128)(2,1)S(1)}, bf16[128,256]{1,0:T(8,128)(2,1)}, u32[]{:S(2)}) copy-start(bf16[128,256]{1,0:T(8,128)(2,1)} %param.13) | copy-start | bytes 196612
Sparse Core Ops, SparseCore 0:
  51.1 21.5 reduce-scatter.2
  77.2 86.9 all-reduce.1
  167.1 21.2 reduce-scatter.4
where the time goes:
time: 196 us; the launch traced here: 195 us
  waiting for transfers between devices  67.6 us (34%)
  blocking collectives  54.6 us (28%)
  local copies, waits for them, and re-layouts  25.1 us (13%)
  matrix products  22.7 us (12%)
  between operations  14.5 us (7%)
  other arithmetic  10.2 us (5%)
    psum x1, blocking collectives, on_device(): grad_weight, grad_bias = lax.psum((grad_local, bias_local), ('row', 'col'))  32.8 us
    psum x1, waiting for transfers between devices, on_device(): grad_weight, grad_bias = lax.psum((grad_local, bias_local), ('row', 'col'))  23.2 us
    reduce_scatter x1, waiting for transfers between devices, on_device(): lax.psum_scatter(place_terms(backward_terms, block_cols, lax.axis_size('r...  22.7 us
    reduce_scatter x1, waiting for transfers between devices, on_device(): lax.psum_scatter(place_terms(forward_terms, block_rows, lax.axis_size('co...  21.7 us
    all_gather x1, blocking collectives, on_device(): column_rows = lax.all_gather(features, 'row', axis=0, tiled=True)  15.8 us
    dot_general x1, local copies, waits for them, and re-layouts, slot_terms(): jnp.einsum('spq,spf->sqf', values, chosen, preferred_element_type=jnp.flo...  9.42 us
    dot_general x1, local copies, waits for them, and re-layouts, slot_terms(): jnp.einsum('spq,sqf->spf', values, chosen, preferred_element_type=jnp.flo...  9.42 us
    convert_element_type x2, other arithmetic, place_terms(): lower = (flat - upper.astype(jnp.float32)).astype(jnp.bfloat16)  8.11 us
  transfers between devices with their start and end apart: 3, of which 3 were waited for; matrix products, arithmetic and copies ran while one was open for 13% of the time, Pallas kernels for 0%

commit v1 on v0

--- a/solution.py
+++ b/solution.py
@@ -1,7 +1,18 @@
+import functools
+
 import jax
 import jax.numpy as jnp
 from jax import lax
+from jax.experimental import pallas as pl
+from jax.experimental.pallas import tpu as pltpu
 from jax.sharding import PartitionSpec as P
+
+F32 = jnp.float32
+BF16 = jnp.bfloat16
+ROWS = 4
+COLS = 4
+WHOLE = pl.BlockSpec(memory_space=pltpu.VMEM)
+SCALARS = pl.BlockSpec(memory_space=pltpu.SMEM)
 
 
 def pick_rows(pick_index, live_mask, source_rows):
@@ -34,7 +45,7 @@
     return placed.reshape(blocks * products.shape[1], products.shape[2])
 
 
-def on_device(features, block_values, block_rows, block_cols, block_count, weight, bias, cotangent):
+def by_slots(features, block_values, block_rows, block_cols, block_count, weight, bias, cotangent):
     block_size = block_values.shape[1]
     slot_total = block_values.shape[0]
     live_mask = jnp.arange(slot_total, dtype=jnp.int32) < block_count[0]
@@ -81,6 +92,190 @@
     return (hidden, grad_weight * norm_scale, grad_bias * norm_scale, grad_features)
 
 
+def densify_kernel(chunk, row_blocks, col_blocks, rows_ref, cols_ref, count_ref, values_ref, tile_ref, acc):
+    step = pl.program_id(0)
+    block = values_ref.shape[1]
+
+    @pl.when(step == 0)
+    def _():
+        acc[...] = jnp.zeros_like(acc)
+
+    first = step * chunk
+
+    def add_slot(i, carry):
+        place = rows_ref[first + i] * col_blocks + cols_ref[first + i]
+        acc[place] = acc[place] + values_ref[i].astype(F32)
+        return carry
+
+    lax.fori_loop(0, jnp.clip(count_ref[0] - first, 0, chunk), add_slot, 0)
+
+    @pl.when(step == pl.num_programs(0) - 1)
+    def _():
+        for r in range(row_blocks):
+            for c in range(col_blocks):
+                tile_ref[pl.ds(r * block, block), pl.ds(c * block, block)] = acc[
+                    r * col_blocks + c
+                ].astype(BF16)
+
+
+def densify(values, rows, cols, count, row_blocks, col_blocks):
+    slots, block, _ = values.shape
+    chunk = 16
+    return pl.pallas_call(
+        functools.partial(densify_kernel, chunk, row_blocks, col_blocks),
+        grid=(slots // chunk,),
+        in_specs=[SCALARS] * 3
+        + [pl.BlockSpec((chunk, block, block), lambda i: (i, 0, 0))],
+        out_specs=pl.BlockSpec((row_blocks * block, col_blocks * block), lambda i: (0, 0)),
+        out_shape=jax.ShapeDtypeStruct((row_blocks * block, col_blocks * block), BF16),
+        scratch_shapes=[pltpu.VMEM((row_blocks * col_blocks, block, block), F32)],
+        cost_estimate=pl.CostEstimate(flops=slots * block * block, bytes_accessed=values.size * 2, transcendentals=0),
+        name="densify",
+    )(rows, cols, count, values)
+
+
+def forward_kernel(tile_ref, x0, x1, x2, x3, send_ref, keep_ref):
+    row = lax.axis_index("row")
+    core = lax.rem(lax.axis_index("col"), 2)
+    rows = x0.shape[0]
+
+    def part(block):
+        total = None
+        for k, x in enumerate((x0, x1, x2, x3)):
+            col_at = pl.multiple_of(jnp.bitwise_xor(row, k) * rows, rows)
+            tile = tile_ref[pl.ds(pl.multiple_of(block * rows, rows), rows), pl.ds(col_at, rows)]
+            term = jnp.dot(tile, x[...], preferred_element_type=F32)
+            total = term if total is None else total + term
+        return total
+
+    for x in range(2):
+        send_ref[pl.ds(x * rows, rows), :] = part(2 * x + 1 - core).astype(BF16)
+    for x in range(2):
+        keep_ref[pl.ds(x * rows, rows), :] = part(2 * x + core)
+
+
+def layer_kernel(keep_ref, sib_ref, far_ref, cot_ref, cot_far_ref, weight_ref, bias_ref,
+                 hidden_ref, grad_ref, gw_ref, gb_ref):
+    mine = lax.rem(lax.axis_index("col") // 2, 2)
+    rows = cot_ref.shape[0]
+    weight = weight_ref[...]
+    gw = None
+    gb = None
+    for other in range(2):
+        where = pl.multiple_of(jnp.bitwise_xor(mine, other) * rows, rows)
+        block = pl.ds(where, rows)
+        aggregate = (
+            keep_ref[block, :] + sib_ref[block, :].astype(F32) + far_ref[block, :].astype(F32)
+        ).astype(BF16)
+        pre_act = jnp.dot(aggregate, weight, preferred_element_type=F32) + bias_ref[...]
+        sigmoid_pre = jax.nn.sigmoid(pre_act)
+        if other == 0:
+            hidden_ref[...] = (pre_act * sigmoid_pre).astype(BF16)
+        cot = (cot_far_ref if other else cot_ref)[...].astype(F32)
+        pre_grad = (cot * sigmoid_pre * (1.0 + pre_act * (1.0 - sigmoid_pre))).astype(BF16)
+        grad_ref[block, :] = lax.dot_general(
+            pre_grad, weight, (((1,), (1,)), ((), ())), preferred_element_type=F32
+        ).astype(BF16)
+        term = lax.dot_general(
+            aggregate, pre_grad, (((0,), (0,)), ((), ())), preferred_element_type=F32
+        )
+        bias_term = jnp.sum(pre_grad.astype(F32), axis=0, keepdims=True)
+        gw = term if gw is None else gw + term
+        gb = bias_term if gb is None else gb + bias_term
+    gw_ref[...] = gw
+    gb_ref[...] = gb
+
+
+def backward_kernel(tile_ref, own_ref, sib_ref, keep_ref, send1, send2, send3):
+    row = lax.axis_index("row")
+    core = lax.rem(lax.axis_index("col"), 2)
+    rows = keep_ref.shape[0]
+    for k, out in ((1, send1), (2, send2), (3, send3), (0, keep_ref)):
+        col_at = pl.multiple_of(jnp.bitwise_xor(row, k) * rows, rows)
+        total = None
+        for half, ref in ((core, own_ref), (1 - core, sib_ref)):
+            for x in range(2):
+                row_at = pl.multiple_of((2 * x + half) * rows, rows)
+                tile = tile_ref[pl.ds(row_at, rows), pl.ds(col_at, rows)]
+                term = lax.dot_general(
+                    tile, ref[pl.ds(x * rows, rows), :], (((0,), (0,)), ((), ())),
+                    preferred_element_type=F32,
+                )
+                total = term if total is None else total + term
+        out[...] = total.astype(out.dtype)
+
+
+def swap(array, axis, bit):
+    size = lax.axis_size(axis)
+    return lax.ppermute(array, axis, [(i, i ^ bit) for i in range(size)])
+
+
+def dense_tile(features, block_values, block_rows, block_cols, block_count, weight, bias, cotangent):
+    block_size = block_values.shape[1]
+    node_rows = cotangent.shape[0]
+    width_in = features.shape[1]
+    hid = cotangent.shape[1]
+    row_blocks = COLS * node_rows // block_size
+    col_blocks = ROWS * node_rows // block_size
+    shards = [features] + [swap(features, "row", k) for k in (1, 2, 3)]
+    cot_far = swap(cotangent, "col", 2)
+    tile = densify(block_values, block_rows, block_cols, block_count, row_blocks, col_blocks)
+    half = jax.ShapeDtypeStruct((2 * node_rows, width_in), BF16)
+    send, keep = pl.pallas_call(
+        forward_kernel,
+        in_specs=[WHOLE] * 5,
+        out_specs=[WHOLE] * 2,
+        out_shape=[half, jax.ShapeDtypeStruct(half.shape, F32)],
+        name="forward",
+    )(tile, *shards)
+    sib = swap(send, "col", 1)
+    far = swap((keep + sib.astype(F32)).astype(BF16), "col", 2)
+    hidden, agg_grad, gw, gb = pl.pallas_call(
+        layer_kernel,
+        in_specs=[WHOLE] * 7,
+        out_specs=[WHOLE] * 4,
+        out_shape=[
+            jax.ShapeDtypeStruct((node_rows, hid), BF16),
+            half,
+            jax.ShapeDtypeStruct((width_in, hid), F32),
+            jax.ShapeDtypeStruct((1, hid), F32),
+        ],
+        name="layer",
+    )(keep, sib, far, cotangent, cot_far, weight, bias.reshape(1, hid))
+    grad_sib = swap(agg_grad, "col", 1)
+    block = jax.ShapeDtypeStruct((node_rows, width_in), BF16)
+    own, *sends = pl.pallas_call(
+        backward_kernel,
+        in_specs=[WHOLE] * 3,
+        out_specs=[WHOLE] * 4,
+        out_shape=[jax.ShapeDtypeStruct(block.shape, F32)] + [block] * 3,
+        name="backward",
+    )(tile, agg_grad, grad_sib)
+    got = [swap(part, "row", k) for k, part in zip((1, 2, 3), sends)]
+    grad_features = (own + got[0].astype(F32) + got[1].astype(F32) + got[2].astype(F32)).astype(BF16)
+
+    both = jnp.concatenate([gw, jnp.broadcast_to(gb, (16, hid))], axis=0).astype(BF16)
+    both = both.astype(F32) + swap(both, "col", 1).astype(F32)
+    mine = (lax.axis_index("col") // 2) % 2
+    part_rows = width_in // 2
+    part = lax.dynamic_slice_in_dim(both, mine * part_rows, part_rows, 0)
+    part = jnp.concatenate([part, both[width_in:]], axis=0).astype(BF16)
+    row = lax.axis_index("row")
+    parts = jnp.stack([part] + [swap(part, "row", k) for k in (1, 2, 3)])
+    total = None
+    for j in range(ROWS):
+        term = lax.dynamic_index_in_dim(parts, row ^ j, 0, keepdims=False).astype(F32)
+        total = term if total is None else total + term
+    total = total.astype(BF16)
+    total_far = swap(total, "col", 2)
+    first = jnp.where(mine == 0, total, total_far)
+    second = jnp.where(mine == 0, total_far, total)
+    norm_scale = float(node_rows * ROWS * COLS) ** (-0.5)
+    grad_weight = jnp.concatenate([first[:part_rows], second[:part_rows]], axis=0).astype(F32) * norm_scale
+    grad_bias = first[part_rows].astype(F32) * norm_scale
+    return hidden, grad_weight, grad_bias, grad_features
+
+
 def solution(mesh):
     in_specs = (
         P(("parts", "col", "row"), None),
@@ -98,6 +293,11 @@
         P("parts"),
         P(("parts", "col", "row"), None),
     )
+    small = mesh.shape["row"] == ROWS and mesh.shape["col"] == COLS
     return jax.shard_map(
-        on_device, mesh=mesh, in_specs=in_specs, out_specs=out_specs, check_vma=False
-    )
+        dense_tile if small else by_slots,
+        mesh=mesh,
+        in_specs=in_specs,
+        out_specs=out_specs,
+        check_vma=False,
+    )

time: 196 us -> 58.4 us (0.30)
  blocking collectives: 54.6 us -> 0 us
  waiting for transfers between devices: 67.6 us -> 13.1 us
  matrix products: 22.7 us -> 0 us
  local copies, waits for them, and re-layouts: 25.1 us -> 2.58 us
  starting transfers between devices: 0.12 us -> 19.3 us
  Pallas kernels: 0 us -> 15.9 us
  between operations: 14.5 us -> 1.45 us
  other arithmetic: 10.2 us -> 5.56 us
    reduce_scatter x2 -> x0, waiting for transfers between devices: 44.4 us -> none  [the longest x1 22.7 us: on_device(): lax.psum_scatter(place_terms(backward_terms, block_cols, lax.axis_size('r...]
    psum x1 -> x0, blocking collectives: 32.8 us -> none  [on_device(): grad_weight, grad_bias = lax.psum((grad_local, bias_local), ('row', 'col'))]
    psum x1 -> x0, waiting for transfers between devices: 23.2 us -> none  [on_device(): grad_weight, grad_bias = lax.psum((grad_local, bias_local), ('row', 'col'))]
    dot_general x11 -> x0, matrix products: 22.7 us -> none  [the longest x1 6.3 us: slot_terms(): jnp.einsum('spq,sqf->spf', values, chosen, preferred_element_type=jnp.flo...]
    all_gather x2 -> x0, blocking collectives: 21.8 us -> none  [the longest x1 15.8 us: on_device(): column_rows = lax.all_gather(features, 'row', axis=0, tiled=True)]
    ppermute x0 -> x15, starting transfers between devices: none -> 19.3 us  [swap(): return lax.ppermute(array, axis, [(i, i ^ bit) for i in range(size)])]
    dot_general x2 -> x0, local copies, waits for them, and re-layouts: 18.8 us -> none  [the longest x1 9.42 us: slot_terms(): jnp.einsum('spq,spf->sqf', values, chosen, preferred_element_type=jnp.flo...]
    pallas_call x0 -> x4, Pallas kernels: none -> 15.9 us  [the longest x1 7.28 us: densify(): pl.pallas_call(functools.partial(densify_kernel, chunk, row_blocks, col_b...]
  transfers between devices with their start and end apart: 3 -> 15, of which waited for: 3 -> 8; matrix products, arithmetic and copies ran while one was open for 13% -> 4% of each run, Pallas kernels for 0% -> 18%
where the time goes in v1:
time: 58.4 us; the launch traced here: 57.9 us
  starting transfers between devices  19.3 us (33%)
  Pallas kernels  15.9 us (27%)
  waiting for transfers between devices  13.1 us (22%)
  other arithmetic  5.56 us (10%)
  local copies, waits for them, and re-layouts  2.58 us (4%)
  between operations  1.45 us (2%)
    ppermute x15, starting transfers between devices, swap(): return lax.ppermute(array, axis, [(i, i ^ bit) for i in range(size)])  19.3 us
    ppermute x15, waiting for transfers between devices, swap(): return lax.ppermute(array, axis, [(i, i ^ bit) for i in range(size)])  13.1 us
    pallas_call x1, Pallas kernels, densify(): pl.pallas_call(functools.partial(densify_kernel, chunk, row_blocks, col_b...  7.28 us
    pallas_call x1, Pallas kernels, dense_tile(): pl.pallas_call(backward_kernel, in_specs=[WHOLE] * 3, out_specs=[WHOLE] *...  3.14 us
    pallas_call x1, Pallas kernels, dense_tile(): pl.pallas_call(forward_kernel, in_specs=[WHOLE] * 5, out_specs=[WHOLE] *...  3.09 us
    unnamed x16, local copies, waits for them, and re-layouts  2.55 us
    pallas_call x1, Pallas kernels, dense_tile(): pl.pallas_call(layer_kernel, in_specs=[WHOLE] * 7, out_specs=[WHOLE] * 4,...  2.4 us
    another operation x2, other arithmetic  1.61 us
  transfers between devices with their start and end apart: 15, of which 8 were waited for; matrix products, arithmetic and copies ran while one was open for 4% of the time, Pallas kernels for 18%

profile of v1, /device:TPU:0, one launch (start us, length us, event | category | flops | bytes accessed | tf_op | source)
XLA Modules:
  0.0 57.9 jit_solution(6517053719023757527)
XLA Ops:
  0.6 3.1 %collective-permute-start = (bf16[256,128]{1,0:T(8,128)(2,1)}, bf16[256,128]{1,0:T(8,128)(2,1)S(1)}, u32[]{:S(2)}, u32[]{:S(2)}) collective-permute-start(bf16[256,128]{1,0:T(8,128)(2,1)} %x0.1), channel_id=1, source_target_pairs={{0,4},{4,0},{8,12},{12,8},{1,5},{5,1},{9,13},{13,9},{2,6},{6,2},{1... | collective-permute-start | bytes 196616 | tf_op jit(solution)/shard_map/ppermute | solution.py:210
  3.7 2.6 %collective-permute-start.1 = (bf16[256,128]{1,0:T(8,128)(2,1)}, bf16[256,128]{1,0:T(8,128)(2,1)S(1)}, u32[]{:S(2)}, u32[]{:S(2)}) collective-permute-start(bf16[256,128]{1,0:T(8,128)(2,1)} %x0.1), channel_id=1, source_target_pairs={{0,8},{4,12},{8,0},{12,4},{1,9},{5,13},{9,1},{13,5},{2,10},{6,14},... | collective-permute-start | bytes 196616 | tf_op jit(solution)/shard_map/ppermute | solution.py:210
  7.0 7.3 %densify.1.tile_ref = bf16[1024,1024]{1,0:T(8,128)(2,1)} custom-call(s32[128]{0:T(128)} %rows_ref.1, s32[128]{0:T(128)} %cols_ref.1, s32[1]{0:T(128)S(6)} %copy.12.count_ref, bf16[128,128,128]{2,1,0:T(8,128)(2,1)} %values_ref.1), custom_call_target="tpu_custom_call" | custom-call | flops 2097152 | bytes 4194304 | tf_op jit(solution)/shard_map/densify/pallas_call | solution.py:124
  14.3 0.6 %copy-done.5 = bf16[256,128]{1,0:T(8,128)(2,1)} copy-done((bf16[256,128]{1,0:T(8,128)(2,1)}, bf16[256,128]{1,0:T(8,128)(2,1)S(1)}, u32[]{:S(2)}) %copy-start.5) | copy-done | bytes 65560
  14.9 0.6 %copy-done.7 = bf16[256,128]{1,0:T(8,128)(2,1)} copy-done((bf16[256,128]{1,0:T(8,128)(2,1)}, bf16[256,128]{1,0:T(8,128)(2,1)S(1)}, u32[]{:S(2)}) %copy-start.7) | copy-done | bytes 65560
  15.5 3.1 %forward.1 = (bf16[512,128]{1,0:T(8,128)(2,1)}, f32[512,128]{1,0:T(8,128)}) custom-call(bf16[1024,1024]{1,0:T(8,128)(2,1)} %densify.1.tile_ref, bf16[256,128]{1,0:T(8,128)(2,1)} %x0.1, bf16[256,128]{1,0:T(8,128)(2,1)} %copy-done.5, bf16[256,128]{1,0:T(8,128)(2,1)} %copy-done.6, bf16[256,128]{1,0:T(8,128)(2,1)} %copy-done.7), custom_call_target="tpu_custom_call" | custom-call | tf_op jit(solution)/shard_map/forward/pallas_call | solution.py:224
  18.6 1.4 %collective-permute-start.5 = (bf16[256,256]{1,0:T(8,128)(2,1)S(1)}, bf16[256,256]{1,0:T(8,128)(2,1)S(1)}, u32[]{:S(2)}, u32[]{:S(2)}) collective-permute-start(bf16[256,256]{1,0:T(8,128)(2,1)S(1)} %copy-done.2), channel_id=1, source_target_pairs={{0,2},{1,3},{2,0},{3,1},{4,6},{5,7},{6,4},{7,5},{8,10},{9,11},{10,... | collective-permute-start | bytes 393224 | tf_op jit(solution)/shard_map/ppermute | solution.py:210
  20.2 1.0 %add_convert_fusion = bf16[512,128]{1,0:T(8,128)(2,1)S(1)} fusion(f32[512,128]{1,0:T(8,128)} %get-tuple-element.14.keep_ref, bf16[512,128]{1,0:T(8,128)(2,1)S(1)} %collective-permute-done.3.sib_ref), kind=kLoop, calls=%fused_computation | loop fusion | flops 196608 | bytes 524288 | tf_op jit(solution)/shard_map/convert_element_type | solution.py:232
  21.2 1.4 %collective-permute-start.4 = (bf16[512,128]{1,0:T(8,128)(2,1)S(1)}, bf16[512,128]{1,0:T(8,128)(2,1)S(1)}, u32[]{:S(2)}, u32[]{:S(2)}) collective-permute-start(bf16[512,128]{1,0:T(8,128)(2,1)S(1)} %add_convert_fusion), channel_id=1, source_target_pairs={{0,2},{1,3},{2,0},{3,1},{4,6},{5,7},{6,4},{7,5},{8,10},{9,11},{10,... | collective-permute-start | bytes 393224 | tf_op jit(solution)/shard_map/ppermute | solution.py:210
  22.6 2.4 %collective-permute-done.5.cot_far_ref = bf16[256,256]{1,0:T(8,128)(2,1)S(1)} collective-permute-done((bf16[256,256]{1,0:T(8,128)(2,1)S(1)}, bf16[256,256]{1,0:T(8,128)(2,1)S(1)}, u32[]{:S(2)}, u32[]{:S(2)}) %collective-permute-start.5) | collective-permute-done | bytes 131104 | tf_op jit(solution)/shard_map/ppermute | solution.py:210
  25.0 2.4 %collective-permute-done.4.far_ref = bf16[512,128]{1,0:T(8,128)(2,1)S(1)} collective-permute-done((bf16[512,128]{1,0:T(8,128)(2,1)S(1)}, bf16[512,128]{1,0:T(8,128)(2,1)S(1)}, u32[]{:S(2)}, u32[]{:S(2)}) %collective-permute-start.4) | collective-permute-done | bytes 131104 | tf_op jit(solution)/shard_map/ppermute | solution.py:210
  27.3 0.6 %copy-done.4 = bf16[512,128]{1,0:T(8,128)(2,1)} copy-done((bf16[512,128]{1,0:T(8,128)(2,1)}, bf16[512,128]{1,0:T(8,128)(2,1)S(1)}, u32[]{:S(2)}) %copy-start.4) | copy-done | bytes 131096
  28.0 2.4 %layer.1 = (bf16[256,256]{1,0:T(8,128)(2,1)}, bf16[512,128]{1,0:T(8,128)(2,1)}, f32[128,256]{1,0:T(8,128)}, f32[1,256]{1,0:T(1,128)}) custom-call(f32[512,128]{1,0:T(8,128)} %get-tuple-element.14.keep_ref, bf16[512,128]{1,0:T(8,128)(2,1)} %copy-done, bf16[512,128]{1,0:T(8,128)(2,1)} %copy-done.4, bf16[256,256]{1,0:T(8,128)(2,1)} %cot_ref.1, ...), custom_call_target="tpu_custom_call" | custom-call | tf_op jit(solution)/shard_map/layer/pallas_call | solution.py:233
  30.4 0.9 %convert.20 = bf16[128,256]{1,0:T(8,128)(2,1)S(1)} convert(f32[128,256]{1,0:T(8,128)} %get-tuple-element.17) | non-fusion elementwise | flops 32768 | bytes 196608 | tf_op jit(solution)/shard_map/convert.7
  31.3 0.7 %convert_reduce_fusion = bf16[256]{0:T(256)(128)(2,1)S(1)} fusion(f32[1,256]{1,0:T(1,128)} %get-tuple-element.18), kind=kLoop, calls=%fused_computation.15 | loop fusion | flops 256 | bytes 1536 | tf_op jit(solution)/shard_map/convert.9
  32.1 0.4 collective-permute-start.11
  32.6 0.8 %collective-permute-done.6 = bf16[144,256]{1,0:T(8,128)(2,1)S(1)} collective-permute-done((bf16[144,256]{1,0:T(8,128)(2,1)S(1)}, bf16[144,256]{1,0:T(8,128)(2,1)S(1)}, u32[]{:S(2)}, u32[]{:S(2)}) %collective-permute-start.6) | collective-permute-done | bytes 73760 | tf_op jit(solution)/shard_map/ppermute | solution.py:210
  33.4 1.1 %collective-permute-start.7 = (bf16[80,256]{1,0:T(8,128)(2,1)S(1)}, bf16[80,256]{1,0:T(8,128)(2,1)S(1)}, u32[]{:S(2)}, u32[]{:S(2)}) collective-permute-start(bf16[80,256]{1,0:T(8,128)(2,1)S(1)} %pad_maximum_fusion.2), channel_id=1, source_target_pairs={{0,4},{4,0},{8,12},{12,8},{1,5},{5,1},{9,13},{13,9},{2,6},{6,2},{1... | collective-permute-start | bytes 122888 | tf_op jit(solution)/shard_map/ppermute | solution.py:210
  34.5 3.0 %collective-permute-start.8 = (bf16[80,256]{1,0:T(8,128)(2,1)S(1)}, bf16[80,256]{1,0:T(8,128)(2,1)S(1)}, u32[]{:S(2)}, u32[]{:S(2)}) collective-permute-start(bf16[80,256]{1,0:T(8,128)(2,1)S(1)} %pad_maximum_fusion.2), channel_id=1, source_target_pairs={{0,8},{4,12},{8,0},{12,4},{1,9},{5,13},{9,1},{13,5},{2,10},{6,14},... | collective-permute-start | bytes 122888 | tf_op jit(solution)/shard_map/ppermute | solution.py:210
  37.6 0.3 collective-permute-start.9
  37.9 2.4 %collective-permute-done.8 = bf16[80,256]{1,0:T(8,128)(2,1)S(1)} collective-permute-done((bf16[80,256]{1,0:T(8,128)(2,1)S(1)}, bf16[80,256]{1,0:T(8,128)(2,1)S(1)}, u32[]{:S(2)}, u32[]{:S(2)}) %collective-permute-start.8) | collective-permute-done | bytes 40992 | tf_op jit(solution)/shard_map/ppermute | solution.py:210
  40.3 3.1 %collective-permute-done.9 = bf16[80,256]{1,0:T(8,128)(2,1)S(1)} collective-permute-done((bf16[80,256]{1,0:T(8,128)(2,1)S(1)}, bf16[80,256]{1,0:T(8,128)(2,1)S(1)}, u32[]{:S(2)}, u32[]{:S(2)}) %collective-permute-start.9) | collective-permute-done | bytes 40992 | tf_op jit(solution)/shard_map/ppermute | solution.py:210
  43.4 1.5 %collective-permute-start.10 = (bf16[80,256]{1,0:T(8,128)(2,1)S(1)}, bf16[80,256]{1,0:T(8,128)(2,1)S(1)}, u32[]{:S(2)}, u32[]{:S(2)}) collective-permute-start(bf16[80,256]{1,0:T(8,128)(2,1)S(1)} %fusion), channel_id=1, source_target_pairs={{0,2},{1,3},{2,0},{3,1},{4,6},{5,7},{6,4},{7,5},{8,10},{9,11},{10,... | collective-permute-start | bytes 122888 | tf_op jit(solution)/shard_map/ppermute | solution.py:210
  44.9 0.7 %copy-done.1 = bf16[512,128]{1,0:T(8,128)(2,1)} copy-done((bf16[512,128]{1,0:T(8,128)(2,1)}, bf16[512,128]{1,0:T(8,128)(2,1)S(1)}, u32[]{:S(2)}) %copy-start.1) | copy-done | bytes 131096
  45.6 3.1 %backward.1 = (f32[256,128]{1,0:T(8,128)}, bf16[256,128]{1,0:T(8,128)(2,1)}, bf16[256,128]{1,0:T(8,128)(2,1)}, bf16[256,128]{1,0:T(8,128)(2,1)}) custom-call(bf16[1024,1024]{1,0:T(8,128)(2,1)} %densify.1.tile_ref, bf16[512,128]{1,0:T(8,128)(2,1)} %get-tuple-element.19.own_ref, bf16[512,128]{1,0:T(8,128)(2,1)} %copy-done.1), custom_call_target="tpu_custom_call" | custom-call | tf_op jit(solution)/shard_map/backward/pallas_call | solution.py:247
  48.7 1.1 %collective-permute-start.13 = (bf16[256,128]{1,0:T(8,128)(2,1)}, bf16[256,128]{1,0:T(8,128)(2,1)S(1)}, u32[]{:S(2)}, u32[]{:S(2)}) collective-permute-start(bf16[256,128]{1,0:T(8,128)(2,1)} %get-tuple-element.22), channel_id=1, source_target_pairs={{0,8},{4,12},{8,0},{12,4},{1,9},{5,13},{9,1},{13,5},{2,10},{6,14},... | collective-permute-start | bytes 196616 | tf_op jit(solution)/shard_map/ppermute | solution.py:210
  49.8 3.3 %collective-permute-start.14 = (bf16[256,128]{1,0:T(8,128)(2,1)}, bf16[256,128]{1,0:T(8,128)(2,1)S(1)}, u32[]{:S(2)}, u32[]{:S(2)}) collective-permute-start(bf16[256,128]{1,0:T(8,128)(2,1)} %get-tuple-element.23), channel_id=1, source_target_pairs={{0,12},{4,8},{8,4},{12,0},{1,13},{5,9},{9,5},{13,1},{2,14},{6,10},... | collective-permute-start | bytes 196616 | tf_op jit(solution)/shard_map/ppermute | solution.py:210
  53.1 0.6 fusion.1
  53.7 0.7 %convert_multiply_fusion = f32[128,256]{1,0:T(8,128)} fusion(bf16[64,256]{1,0:T(8,128)(2,1)S(1)} %slice_select_fusion, bf16[64,256]{1,0:T(8,128)(2,1)S(1)} %slice.17), kind=kLoop, calls=%fused_computation.4 | loop fusion | flops 163840 | bytes 196608 | tf_op jit(solution)/shard_map/mul | solution.py:274
  54.4 0.2 collective-permute-done.13
  54.6 1.8 %collective-permute-done.14 = bf16[256,128]{1,0:T(8,128)(2,1)S(1)} collective-permute-done((bf16[256,128]{1,0:T(8,128)(2,1)}, bf16[256,128]{1,0:T(8,128)(2,1)S(1)}, u32[]{:S(2)}, u32[]{:S(2)}) %collective-permute-start.14) | collective-permute-done | bytes 65568 | tf_op jit(solution)/shard_map/ppermute | solution.py:210
  56.3 1.6 %add_convert_fusion.1 = bf16[256,128]{1,0:T(8,128)(2,1)} fusion(bf16[256,128]{1,0:T(8,128)(2,1)S(1)} %collective-permute-done.14, bf16[256,128]{1,0:T(8,128)(2,1)S(1)} %collective-permute-done.13, f32[256,128]{1,0:T(8,128)} %get-tuple-element.20, bf16[256,128]{1,0:T(8,128)(2,1)S(1)} %collective-permute-done.12), kind=kLoop, calls=%fused_computation.3 | loop fusion | flops 229376 | bytes 393216 | tf_op jit(solution)/shard_map/convert_element_type | solution.py:255
  (37 shorter events, 0.4 us)
Async XLA Ops:
  0.6 13.6 %collective-permute-start = (bf16[256,128]{1,0:T(8,128)(2,1)}, bf16[256,128]{1,0:T(8,128)(2,1)S(1)}, u32[]{:S(2)}, u32[]{:S(2)}) collective-permute-start(bf16[256,128]{1,0:T(8,128)(2,1)} %x0.1), channel_id=1, source_target_pairs={{0,4},{4,0},{8,12},{12,8},{1,5},{5,1},{9,13},{13,9},{2,6},{6,2},{1... | collective-permute-start | bytes 196616 | tf_op jit(solution)/shard_map/ppermute | solution.py:210
  3.7 10.5 %collective-permute-start.1 = (bf16[256,128]{1,0:T(8,128)(2,1)}, bf16[256,128]{1,0:T(8,128)(2,1)S(1)}, u32[]{:S(2)}, u32[]{:S(2)}) collective-permute-start(bf16[256,128]{1,0:T(8,128)(2,1)} %x0.1), channel_id=1, source_target_pairs={{0,8},{4,12},{8,0},{12,4},{1,9},{5,13},{9,1},{13,5},{2,10},{6,14},... | collective-permute-start | bytes 196616 | tf_op jit(solution)/shard_map/ppermute | solution.py:210
  6.3 8.0 %collective-permute-start.2 = (bf16[256,128]{1,0:T(8,128)(2,1)}, bf16[256,128]{1,0:T(8,128)(2,1)S(1)}, u32[]{:S(2)}, u32[]{:S(2)}) collective-permute-start(bf16[256,128]{1,0:T(8,128)(2,1)} %x0.1), channel_id=1, source_target_pairs={{0,12},{4,8},{8,4},{12,0},{1,13},{5,9},{9,5},{13,1},{2,14},{6,10},... | collective-permute-start | bytes 196616 | tf_op jit(solution)/shard_map/ppermute | solution.py:210
  7.0 11.7 %copy-start.2 = (bf16[256,256]{1,0:T(8,128)(2,1)S(1)}, bf16[256,256]{1,0:T(8,128)(2,1)}, u32[]{:S(2)}) copy-start(bf16[256,256]{1,0:T(8,128)(2,1)} %cot_ref.1) | copy-start | bytes 393220
  14.3 0.6 %copy-start.5 = (bf16[256,128]{1,0:T(8,128)(2,1)}, bf16[256,128]{1,0:T(8,128)(2,1)S(1)}, u32[]{:S(2)}) copy-start(bf16[256,128]{1,0:T(8,128)(2,1)S(1)} %collective-permute-done.x1) | copy-start | bytes 196612
  14.3 0.6 %copy-start.6 = (bf16[256,128]{1,0:T(8,128)(2,1)}, bf16[256,128]{1,0:T(8,128)(2,1)S(1)}, u32[]{:S(2)}) copy-start(bf16[256,128]{1,0:T(8,128)(2,1)S(1)} %collective-permute-done.1.x2) | copy-start | bytes 196612
  14.9 0.6 %copy-start.7 = (bf16[256,128]{1,0:T(8,128)(2,1)}, bf16[256,128]{1,0:T(8,128)(2,1)S(1)}, u32[]{:S(2)}) copy-start(bf16[256,128]{1,0:T(8,128)(2,1)S(1)} %collective-permute-done.2.x3) | copy-start | bytes 196612
  18.6 1.6 %collective-permute-start.3 = (bf16[512,128]{1,0:T(8,128)(2,1)}, bf16[512,128]{1,0:T(8,128)(2,1)S(1)}, u32[]{:S(2)}, u32[]{:S(2)}) collective-permute-start(bf16[512,128]{1,0:T(8,128)(2,1)} %get-tuple-element.15), channel_id=1, source_target_pairs={{0,1},{1,0},{2,3},{3,2},{4,5},{5,4},{6,7},{7,6},{8,9},{9,8},{10,11... | collective-permute-start | bytes 393224 | tf_op jit(solution)/shard_map/ppermute | solution.py:210
  18.6 6.4 %collective-permute-start.5 = (bf16[256,256]{1,0:T(8,128)(2,1)S(1)}, bf16[256,256]{1,0:T(8,128)(2,1)S(1)}, u32[]{:S(2)}, u32[]{:S(2)}) collective-permute-start(bf16[256,256]{1,0:T(8,128)(2,1)S(1)} %copy-done.2), channel_id=1, source_target_pairs={{0,2},{1,3},{2,0},{3,1},{4,6},{5,7},{6,4},{7,5},{8,10},{9,11},{10,... | collective-permute-start | bytes 393224 | tf_op jit(solution)/shard_map/ppermute | solution.py:210
  20.2 7.2 %copy-start = (bf16[512,128]{1,0:T(8,128)(2,1)}, bf16[512,128]{1,0:T(8,128)(2,1)S(1)}, u32[]{:S(2)}) copy-start(bf16[512,128]{1,0:T(8,128)(2,1)S(1)} %collective-permute-done.3.sib_ref) | copy-start | bytes 393220
  21.2 6.1 %collective-permute-start.4 = (bf16[512,128]{1,0:T(8,128)(2,1)S(1)}, bf16[512,128]{1,0:T(8,128)(2,1)S(1)}, u32[]{:S(2)}, u32[]{:S(2)}) collective-permute-start(bf16[512,128]{1,0:T(8,128)(2,1)S(1)} %add_convert_fusion), channel_id=1, source_target_pairs={{0,2},{1,3},{2,0},{3,1},{4,6},{5,7},{6,4},{7,5},{8,10},{9,11},{10,... | collective-permute-start | bytes 393224 | tf_op jit(solution)/shard_map/ppermute | solution.py:210
  25.0 2.4 %copy-start.3 = (bf16[256,256]{1,0:T(8,128)(2,1)}, bf16[256,256]{1,0:T(8,128)(2,1)S(1)}, u32[]{:S(2)}) copy-start(bf16[256,256]{1,0:T(8,128)(2,1)S(1)} %collective-permute-done.5.cot_far_ref) | copy-start | bytes 393220
  27.3 0.6 %copy-start.4 = (bf16[512,128]{1,0:T(8,128)(2,1)}, bf16[512,128]{1,0:T(8,128)(2,1)S(1)}, u32[]{:S(2)}) copy-start(bf16[512,128]{1,0:T(8,128)(2,1)S(1)} %collective-permute-done.4.far_ref) | copy-start | bytes 393220
  32.0 1.3 %collective-permute-start.6 = (bf16[144,256]{1,0:T(8,128)(2,1)S(1)}, bf16[144,256]{1,0:T(8,128)(2,1)S(1)}, u32[]{:S(2)}, u32[]{:S(2)}) collective-permute-start(bf16[144,256]{1,0:T(8,128)(2,1)S(1)} %pad_maximum_fusion.1), channel_id=1, source_target_pairs={{0,1},{1,0},{2,3},{3,2},{4,5},{5,4},{6,7},{7,6},{8,9},{9,8},{10,11... | collective-permute-start | bytes 221192 | tf_op jit(solution)/shard_map/ppermute | solution.py:210
  32.1 12.8 %collective-permute-start.11 = (bf16[512,128]{1,0:T(8,128)(2,1)}, bf16[512,128]{1,0:T(8,128)(2,1)S(1)}, u32[]{:S(2)}, u32[]{:S(2)}) collective-permute-start(bf16[512,128]{1,0:T(8,128)(2,1)} %get-tuple-element.19.own_ref), channel_id=1, source_target_pairs={{0,1},{1,0},{2,3},{3,2},{4,5},{5,4},{6,7},{7,6},{8,9},{9,8},{10,11... | collective-permute-start | bytes 393224 | tf_op jit(solution)/shard_map/ppermute | solution.py:210
  33.4 4.5 %collective-permute-start.7 = (bf16[80,256]{1,0:T(8,128)(2,1)S(1)}, bf16[80,256]{1,0:T(8,128)(2,1)S(1)}, u32[]{:S(2)}, u32[]{:S(2)}) collective-permute-start(bf16[80,256]{1,0:T(8,128)(2,1)S(1)} %pad_maximum_fusion.2), channel_id=1, source_target_pairs={{0,4},{4,0},{8,12},{12,8},{1,5},{5,1},{9,13},{13,9},{2,6},{6,2},{1... | collective-permute-start | bytes 122888 | tf_op jit(solution)/shard_map/ppermute | solution.py:210
  34.5 5.8 %collective-permute-start.8 = (bf16[80,256]{1,0:T(8,128)(2,1)S(1)}, bf16[80,256]{1,0:T(8,128)(2,1)S(1)}, u32[]{:S(2)}, u32[]{:S(2)}) collective-permute-start(bf16[80,256]{1,0:T(8,128)(2,1)S(1)} %pad_maximum_fusion.2), channel_id=1, source_target_pairs={{0,8},{4,12},{8,0},{12,4},{1,9},{5,13},{9,1},{13,5},{2,10},{6,14},... | collective-permute-start | bytes 122888 | tf_op jit(solution)/shard_map/ppermute | solution.py:210
  37.6 5.8 %collective-permute-start.9 = (bf16[80,256]{1,0:T(8,128)(2,1)S(1)}, bf16[80,256]{1,0:T(8,128)(2,1)S(1)}, u32[]{:S(2)}, u32[]{:S(2)}) collective-permute-start(bf16[80,256]{1,0:T(8,128)(2,1)S(1)} %pad_maximum_fusion.2), channel_id=1, source_target_pairs={{0,12},{4,8},{8,4},{12,0},{1,13},{5,9},{9,5},{13,1},{2,14},{6,10},... | collective-permute-start | bytes 122888 | tf_op jit(solution)/shard_map/ppermute | solution.py:210
  43.4 9.7 %collective-permute-start.10 = (bf16[80,256]{1,0:T(8,128)(2,1)S(1)}, bf16[80,256]{1,0:T(8,128)(2,1)S(1)}, u32[]{:S(2)}, u32[]{:S(2)}) collective-permute-start(bf16[80,256]{1,0:T(8,128)(2,1)S(1)} %fusion), channel_id=1, source_target_pairs={{0,2},{1,3},{2,0},{3,1},{4,6},{5,7},{6,4},{7,5},{8,10},{9,11},{10,... | collective-permute-start | bytes 122888 | tf_op jit(solution)/shard_map/ppermute | solution.py:210
  44.9 0.7 %copy-start.1 = (bf16[512,128]{1,0:T(8,128)(2,1)}, bf16[512,128]{1,0:T(8,128)(2,1)S(1)}, u32[]{:S(2)}) copy-start(bf16[512,128]{1,0:T(8,128)(2,1)S(1)} %collective-permute-done.11.sib_ref) | copy-start | bytes 393220
  48.7 5.7 %collective-permute-start.12 = (bf16[256,128]{1,0:T(8,128)(2,1)}, bf16[256,128]{1,0:T(8,128)(2,1)S(1)}, u32[]{:S(2)}, u32[]{:S(2)}) collective-permute-start(bf16[256,128]{1,0:T(8,128)(2,1)} %get-tuple-element.21), channel_id=1, source_target_pairs={{0,4},{4,0},{8,12},{12,8},{1,5},{5,1},{9,13},{13,9},{2,6},{6,2},{1... | collective-permute-start | bytes 196616 | tf_op jit(solution)/shard_map/ppermute | solution.py:210
  48.7 5.9 %collective-permute-start.13 = (bf16[256,128]{1,0:T(8,128)(2,1)}, bf16[256,128]{1,0:T(8,128)(2,1)S(1)}, u32[]{:S(2)}, u32[]{:S(2)}) collective-permute-start(bf16[256,128]{1,0:T(8,128)(2,1)} %get-tuple-element.22), channel_id=1, source_target_pairs={{0,8},{4,12},{8,0},{12,4},{1,9},{5,13},{9,1},{13,5},{2,10},{6,14},... | collective-permute-start | bytes 196616 | tf_op jit(solution)/shard_map/ppermute | solution.py:210
  49.8 6.6 %collective-permute-start.14 = (bf16[256,128]{1,0:T(8,128)(2,1)}, bf16[256,128]{1,0:T(8,128)(2,1)S(1)}, u32[]{:S(2)}, u32[]{:S(2)}) collective-permute-start(bf16[256,128]{1,0:T(8,128)(2,1)} %get-tuple-element.23), channel_id=1, source_target_pairs={{0,12},{4,8},{8,4},{12,0},{1,13},{5,9},{9,5},{13,1},{2,14},{6,10},... | collective-permute-start | bytes 196616 | tf_op jit(solution)/shard_map/ppermute | solution.py:210

commit v2 on v1

--- a/solution.py
+++ b/solution.py
@@ -13,6 +13,8 @@
 COLS = 4
 WHOLE = pl.BlockSpec(memory_space=pltpu.VMEM)
 SCALARS = pl.BlockSpec(memory_space=pltpu.SMEM)
+LIMIT = pltpu.CompilerParams(vmem_limit_bytes=16 * 2**20)
+BIAS_ROWS = 16
 
 
 def pick_rows(pick_index, live_mask, source_rows):
@@ -92,43 +94,49 @@
     return (hidden, grad_weight * norm_scale, grad_bias * norm_scale, grad_features)
 
 
-def densify_kernel(chunk, row_blocks, col_blocks, rows_ref, cols_ref, count_ref, values_ref, tile_ref, acc):
-    step = pl.program_id(0)
-    block = values_ref.shape[1]
-
-    @pl.when(step == 0)
-    def _():
-        acc[...] = jnp.zeros_like(acc)
-
-    first = step * chunk
+def densify_kernel(chunks, row_blocks, col_blocks, rows_ref, cols_ref, count_ref, values_ref, tile_ref, held, acc, sems):
+    slots, block, _ = values_ref.shape
+    size = slots // chunks
+    copies = [
+        pltpu.make_async_copy(
+            values_ref.at[pl.ds(i * size, size)], held.at[pl.ds(i * size, size)], sems.at[i]
+        )
+        for i in range(chunks)
+    ]
+    for copy in copies:
+        copy.start()
+    acc[...] = jnp.zeros_like(acc)
+    live = count_ref[0]
 
     def add_slot(i, carry):
-        place = rows_ref[first + i] * col_blocks + cols_ref[first + i]
-        acc[place] = acc[place] + values_ref[i].astype(F32)
+        place = rows_ref[i] * col_blocks + cols_ref[i]
+        acc[place] = acc[place] + held[i].astype(F32)
         return carry
 
-    lax.fori_loop(0, jnp.clip(count_ref[0] - first, 0, chunk), add_slot, 0)
-
-    @pl.when(step == pl.num_programs(0) - 1)
-    def _():
-        for r in range(row_blocks):
-            for c in range(col_blocks):
-                tile_ref[pl.ds(r * block, block), pl.ds(c * block, block)] = acc[
-                    r * col_blocks + c
-                ].astype(BF16)
+    for i, copy in enumerate(copies):
+        copy.wait()
+        lax.fori_loop(i * size, jnp.clip(live, i * size, (i + 1) * size), add_slot, 0)
+    for r in range(row_blocks):
+        for c in range(col_blocks):
+            tile_ref[pl.ds(r * block, block), pl.ds(c * block, block)] = acc[
+                r * col_blocks + c
+            ].astype(BF16)
 
 
 def densify(values, rows, cols, count, row_blocks, col_blocks):
     slots, block, _ = values.shape
-    chunk = 16
+    chunks = 8
     return pl.pallas_call(
-        functools.partial(densify_kernel, chunk, row_blocks, col_blocks),
-        grid=(slots // chunk,),
-        in_specs=[SCALARS] * 3
-        + [pl.BlockSpec((chunk, block, block), lambda i: (i, 0, 0))],
-        out_specs=pl.BlockSpec((row_blocks * block, col_blocks * block), lambda i: (0, 0)),
+        functools.partial(densify_kernel, chunks, row_blocks, col_blocks),
+        in_specs=[SCALARS] * 3 + [pl.BlockSpec(memory_space=pltpu.HBM)],
+        out_specs=WHOLE,
         out_shape=jax.ShapeDtypeStruct((row_blocks * block, col_blocks * block), BF16),
-        scratch_shapes=[pltpu.VMEM((row_blocks * col_blocks, block, block), F32)],
+        scratch_shapes=[
+            pltpu.VMEM(values.shape, BF16),
+            pltpu.VMEM((row_blocks * col_blocks, block, block), F32),
+            pltpu.SemaphoreType.DMA((chunks,)),
+        ],
+        compiler_params=LIMIT,
         cost_estimate=pl.CostEstimate(flops=slots * block * block, bytes_accessed=values.size * 2, transcendentals=0),
         name="densify",
     )(rows, cols, count, values)
@@ -154,26 +162,26 @@
         keep_ref[pl.ds(x * rows, rows), :] = part(2 * x + core)
 
 
-def layer_kernel(keep_ref, sib_ref, far_ref, cot_ref, cot_far_ref, weight_ref, bias_ref,
-                 hidden_ref, grad_ref, gw_ref, gb_ref):
+def layer_kernel(near_ref, far_ref, cot_ref, cot_far_ref, weight_ref, bias_ref, hidden_ref, swap_ref):
     mine = lax.rem(lax.axis_index("col") // 2, 2)
-    rows = cot_ref.shape[0]
+    rows, hid = cot_ref.shape
+    width_in = near_ref.shape[1]
     weight = weight_ref[...]
     gw = None
     gb = None
-    for other in range(2):
-        where = pl.multiple_of(jnp.bitwise_xor(mine, other) * rows, rows)
-        block = pl.ds(where, rows)
-        aggregate = (
-            keep_ref[block, :] + sib_ref[block, :].astype(F32) + far_ref[block, :].astype(F32)
-        ).astype(BF16)
+    for x in range(2):
+        block = pl.ds(x * rows, rows)
+        aggregate = (near_ref[block, :].astype(F32) + far_ref[block, :].astype(F32)).astype(BF16)
         pre_act = jnp.dot(aggregate, weight, preferred_element_type=F32) + bias_ref[...]
         sigmoid_pre = jax.nn.sigmoid(pre_act)
-        if other == 0:
+
+        @pl.when(mine == x)
+        def _():
             hidden_ref[...] = (pre_act * sigmoid_pre).astype(BF16)
-        cot = (cot_far_ref if other else cot_ref)[...].astype(F32)
+
+        cot = jnp.where(mine == x, cot_ref[...], cot_far_ref[...]).astype(F32)
         pre_grad = (cot * sigmoid_pre * (1.0 + pre_act * (1.0 - sigmoid_pre))).astype(BF16)
-        grad_ref[block, :] = lax.dot_general(
+        swap_ref[block, :] = lax.dot_general(
             pre_grad, weight, (((1,), (1,)), ((), ())), preferred_element_type=F32
         ).astype(BF16)
         term = lax.dot_general(
@@ -182,8 +190,16 @@
         bias_term = jnp.sum(pre_grad.astype(F32), axis=0, keepdims=True)
         gw = term if gw is None else gw + term
         gb = bias_term if gb is None else gb + bias_term
-    gw_ref[...] = gw
-    gb_ref[...] = gb
+    at = 2 * rows
+    for j in range(hid // width_in):
+        lanes = slice(j * width_in, (j + 1) * width_in)
+        swap_ref[pl.ds(at + j * width_in, width_in), :] = gw[:, lanes].astype(BF16)
+    at = at + hid
+    swap_ref[pl.ds(at, BIAS_ROWS), :] = jnp.concatenate(
+        [gb[:, j * width_in : (j + 1) * width_in] for j in range(hid // width_in)]
+        + [jnp.zeros((BIAS_ROWS - hid // width_in, width_in), F32)],
+        axis=0,
+    ).astype(BF16)
 
 
 def backward_kernel(tile_ref, own_ref, sib_ref, keep_ref, send1, send2, send3):
@@ -202,7 +218,23 @@
                     preferred_element_type=F32,
                 )
                 total = term if total is None else total + term
-        out[...] = total.astype(out.dtype)
+        out[pl.ds(0, rows), :] = total.astype(out.dtype)
+    extra = pl.ds(2 * rows, own_ref.shape[0] - 2 * rows)
+    send1[pl.ds(rows, send1.shape[0] - rows), :] = (
+        own_ref[extra, :].astype(F32) + sib_ref[extra, :].astype(F32)
+    ).astype(BF16)
+
+
+def finish_kernel(scale, near_ref, far_ref, gw_ref, gb_ref):
+    width_in, hid = gw_ref.shape
+    for j in range(hid // width_in):
+        lanes = slice(j * width_in, (j + 1) * width_in)
+        block = pl.ds(j * width_in, width_in)
+        gw_ref[:, lanes] = (near_ref[block, :].astype(F32) + far_ref[block, :].astype(F32)) * scale
+    block = pl.ds(hid, BIAS_ROWS)
+    both = (near_ref[block, :].astype(F32) + far_ref[block, :].astype(F32)) * scale
+    for j in range(hid // width_in):
+        gb_ref[:, j * width_in : (j + 1) * width_in] = both[j : j + 1, :]
 
 
 def swap(array, axis, bit):
@@ -217,63 +249,65 @@
     hid = cotangent.shape[1]
     row_blocks = COLS * node_rows // block_size
     col_blocks = ROWS * node_rows // block_size
+    extra = hid + BIAS_ROWS
     shards = [features] + [swap(features, "row", k) for k in (1, 2, 3)]
-    cot_far = swap(cotangent, "col", 2)
+    shards, cot_far = lax.optimization_barrier((shards, swap(cotangent, "col", 2)))
     tile = densify(block_values, block_rows, block_cols, block_count, row_blocks, col_blocks)
-    half = jax.ShapeDtypeStruct((2 * node_rows, width_in), BF16)
+    half = (2 * node_rows, width_in)
     send, keep = pl.pallas_call(
         forward_kernel,
         in_specs=[WHOLE] * 5,
         out_specs=[WHOLE] * 2,
-        out_shape=[half, jax.ShapeDtypeStruct(half.shape, F32)],
+        out_shape=[jax.ShapeDtypeStruct(half, BF16), jax.ShapeDtypeStruct(half, F32)],
+        compiler_params=LIMIT,
         name="forward",
     )(tile, *shards)
-    sib = swap(send, "col", 1)
-    far = swap((keep + sib.astype(F32)).astype(BF16), "col", 2)
-    hidden, agg_grad, gw, gb = pl.pallas_call(
+    near = (keep + swap(send, "col", 1).astype(F32)).astype(BF16)
+    far = swap(near, "col", 2)
+    hidden, grads = pl.pallas_call(
         layer_kernel,
-        in_specs=[WHOLE] * 7,
-        out_specs=[WHOLE] * 4,
+        in_specs=[WHOLE] * 6,
+        out_specs=[WHOLE] * 2,
         out_shape=[
             jax.ShapeDtypeStruct((node_rows, hid), BF16),
-            half,
-            jax.ShapeDtypeStruct((width_in, hid), F32),
-            jax.ShapeDtypeStruct((1, hid), F32),
+            jax.ShapeDtypeStruct((2 * node_rows + extra, width_in), BF16),
         ],
+        compiler_params=LIMIT,
         name="layer",
-    )(keep, sib, far, cotangent, cot_far, weight, bias.reshape(1, hid))
-    grad_sib = swap(agg_grad, "col", 1)
+    )(near, far, cotangent, cot_far, weight, bias.reshape(1, hid))
     block = jax.ShapeDtypeStruct((node_rows, width_in), BF16)
     own, *sends = pl.pallas_call(
         backward_kernel,
         in_specs=[WHOLE] * 3,
         out_specs=[WHOLE] * 4,
-        out_shape=[jax.ShapeDtypeStruct(block.shape, F32)] + [block] * 3,
+        out_shape=[
+            jax.ShapeDtypeStruct(block.shape, F32),
+            jax.ShapeDtypeStruct((node_rows + extra, width_in), BF16),
+            block,
+            block,
+        ],
+        compiler_params=LIMIT,
         name="backward",
-    )(tile, agg_grad, grad_sib)
+    )(tile, grads, swap(grads, "col", 1))
     got = [swap(part, "row", k) for k, part in zip((1, 2, 3), sends)]
-    grad_features = (own + got[0].astype(F32) + got[1].astype(F32) + got[2].astype(F32)).astype(BF16)
-
-    both = jnp.concatenate([gw, jnp.broadcast_to(gb, (16, hid))], axis=0).astype(BF16)
-    both = both.astype(F32) + swap(both, "col", 1).astype(F32)
-    mine = (lax.axis_index("col") // 2) % 2
-    part_rows = width_in // 2
-    part = lax.dynamic_slice_in_dim(both, mine * part_rows, part_rows, 0)
-    part = jnp.concatenate([part, both[width_in:]], axis=0).astype(BF16)
-    row = lax.axis_index("row")
-    parts = jnp.stack([part] + [swap(part, "row", k) for k in (1, 2, 3)])
-    total = None
-    for j in range(ROWS):
-        term = lax.dynamic_index_in_dim(parts, row ^ j, 0, keepdims=False).astype(F32)
-        total = term if total is None else total + term
-    total = total.astype(BF16)
-    total_far = swap(total, "col", 2)
-    first = jnp.where(mine == 0, total, total_far)
-    second = jnp.where(mine == 0, total_far, total)
+    pair = (sends[0][node_rows:].astype(F32) + got[0][node_rows:].astype(F32)).astype(BF16)
+    pair_far = swap(pair, "row", 2)
+    grad_features = (
+        own + got[0][:node_rows].astype(F32) + got[1].astype(F32) + got[2].astype(F32)
+    ).astype(BF16)
     norm_scale = float(node_rows * ROWS * COLS) ** (-0.5)
-    grad_weight = jnp.concatenate([first[:part_rows], second[:part_rows]], axis=0).astype(F32) * norm_scale
-    grad_bias = first[part_rows].astype(F32) * norm_scale
-    return hidden, grad_weight, grad_bias, grad_features
+    grad_weight, grad_bias = pl.pallas_call(
+        functools.partial(finish_kernel, norm_scale),
+        in_specs=[WHOLE] * 2,
+        out_specs=[WHOLE] * 2,
+        out_shape=[
+            jax.ShapeDtypeStruct((width_in, hid), F32),
+            jax.ShapeDtypeStruct((1, hid), F32),
+        ],
+        compiler_params=LIMIT,
+        name="finish",
+    )(pair, pair_far)
+    return hidden, grad_weight, grad_bias.reshape(hid), grad_features
 
 
 def solution(mesh):

time: 58.4 us -> 40.5 us (0.69)
  Pallas kernels: 15.9 us -> 6.38 us
  starting transfers between devices: 19.3 us -> 13.2 us
  other arithmetic: 5.56 us -> 0.73 us
  waiting for transfers between devices: 13.1 us -> 15.1 us
  local copies, waits for them, and re-layouts: 2.58 us -> 3.51 us
    ppermute x15 -> x11, starting transfers between devices: 19.3 us -> 13.2 us  [swap(): return lax.ppermute(array, axis, [(i, i ^ bit) for i in range(size)])]
    pallas_call x2 -> x3, Pallas kernels: 9.67 us -> 4.83 us  [the longest x1 3.04 us: densify(): pl.pallas_call(functools.partial(densify_kernel, chunks, row_blocks, col_...]
    pallas_call x1, Pallas kernels: 3.09 us -> 0.71 us  [dense_tile(): pl.pallas_call(forward_kernel, in_specs=[WHOLE] * 5, out_specs=[WHOLE] *...]
    pallas_call x1, Pallas kernels: 3.14 us -> 0.85 us  [dense_tile(): pl.pallas_call(backward_kernel, in_specs=[WHOLE] * 3, out_specs=[WHOLE] *...]
    ppermute x15 -> x11, waiting for transfers between devices: 13.1 us -> 15.1 us  [swap(): return lax.ppermute(array, axis, [(i, i ^ bit) for i in range(size)])]
    convert_element_type x2 -> x3, other arithmetic: 2.6 us -> 0.73 us  [the longest x1 0.67 us: dense_tile(): grad_features = (own + got[0][:node_rows].astype(F32) + got[1].astype(F32...]
    another operation x3 -> x0, other arithmetic: 1.62 us -> none
    mul x2 -> x0, other arithmetic: 1.23 us -> none  [the longest x1 0.67 us: dense_tile(): jnp.concatenate([first[:part_rows], second[:part_rows]], axis=0).astype(F32)]
  transfers between devices with their start and end apart: 15 -> 11, of which waited for: 8 -> 6; matrix products, arithmetic and copies ran while one was open for 4% -> 2% of each run, Pallas kernels for 18% -> 8%
where the time goes in v2:
time: 40.5 us; the launch traced here: 40.3 us
  waiting for transfers between devices  15.1 us (37%)
  starting transfers between devices  13.2 us (33%)
  Pallas kernels  6.38 us (16%)
  local copies, waits for them, and re-layouts  3.51 us (9%)
  between operations  1.39 us (3%)
  other arithmetic  0.73 us (2%)
    ppermute x11, waiting for transfers between devices, swap(): return lax.ppermute(array, axis, [(i, i ^ bit) for i in range(size)])  15.1 us
    ppermute x11, starting transfers between devices, swap(): return lax.ppermute(array, axis, [(i, i ^ bit) for i in range(size)])  13.2 us
    unnamed x14, local copies, waits for them, and re-layouts  3.51 us
    pallas_call x1, Pallas kernels, densify(): pl.pallas_call(functools.partial(densify_kernel, chunks, row_blocks, col_...  3.04 us
    pallas_call x1, Pallas kernels, dense_tile(): pl.pallas_call(layer_kernel, in_specs=[WHOLE] * 6, out_specs=[WHOLE] * 2,...  1.11 us
    pallas_call x1, Pallas kernels, dense_tile(): pl.pallas_call(backward_kernel, in_specs=[WHOLE] * 3, out_specs=[WHOLE] *...  0.85 us
  transfers between devices with their start and end apart: 11, of which 6 were waited for; matrix products, arithmetic and copies ran while one was open for 2% of the time, Pallas kernels for 8%

profile of v2, /device:TPU:0, one launch (start us, length us, event | category | flops | bytes accessed | tf_op | source)
XLA Modules:
  0.0 40.3 jit_solution(16774815836354490580)
XLA Ops:
  0.6 3.0 %collective-permute-start.3 = (bf16[256,256]{1,0:T(8,128)(2,1)}, bf16[256,256]{1,0:T(8,128)(2,1)S(1)}, u32[]{:S(2)}, u32[]{:S(2)}) collective-permute-start(bf16[256,256]{1,0:T(8,128)(2,1)} %cot_ref.1), channel_id=1, source_target_pairs={{0,2},{1,3},{2,0},{3,1},{4,6},{5,7},{6,4},{7,5},{8,10},{9,11},{10,... | collective-permute-start | bytes 393224 | tf_op jit(solution)/shard_map/ppermute | solution.py:242
  3.6 2.6 %collective-permute-start.1 = (bf16[256,128]{1,0:T(8,128)(2,1)}, bf16[256,128]{1,0:T(8,128)(2,1)S(1)}, u32[]{:S(2)}, u32[]{:S(2)}) collective-permute-start(bf16[256,128]{1,0:T(8,128)(2,1)} %x0), channel_id=1, source_target_pairs={{0,8},{4,12},{8,0},{12,4},{1,9},{5,13},{9,1},{13,5},{2,10},{6,14},... | collective-permute-start | bytes 196616 | tf_op jit(solution)/shard_map/ppermute | solution.py:242
  6.2 1.6 %collective-permute-start = (bf16[256,128]{1,0:T(8,128)(2,1)}, bf16[256,128]{1,0:T(8,128)(2,1)S(1)}, u32[]{:S(2)}, u32[]{:S(2)}) collective-permute-start(bf16[256,128]{1,0:T(8,128)(2,1)} %x0), channel_id=1, source_target_pairs={{0,4},{4,0},{8,12},{12,8},{1,5},{5,1},{9,13},{13,9},{2,6},{6,2},{1... | collective-permute-start | bytes 196616 | tf_op jit(solution)/shard_map/ppermute | solution.py:242
  7.8 0.2 collective-permute-start.2
  8.7 0.0 copy-start
  8.7 2.2 %copy-done = bf16[128,128,128]{2,1,0:T(8,128)(2,1)S(1)} copy-done((bf16[128,128,128]{2,1,0:T(8,128)(2,1)S(1)}, bf16[128,128,128]{2,1,0:T(8,128)(2,1)}, u32[]{:S(2)}) %copy-start) | copy-done | bytes 4194328
  10.9 0.7 %copy-done.5 = s32[128]{0:T(128)S(1)} copy-done((s32[128]{0:T(128)S(1)}, s32[128]{0:T(128)}, u32[]{:S(2)}) %copy-start.5) | copy-done | bytes 536
  11.5 0.7 %copy-done.6 = s32[128]{0:T(128)S(1)} copy-done((s32[128]{0:T(128)S(1)}, s32[128]{0:T(128)}, u32[]{:S(2)}) %copy-start.6) | copy-done | bytes 536
  12.2 3.0 %densify.1.tile_ref = bf16[1024,1024]{1,0:T(8,128)(2,1)S(1)} custom-call(s32[128]{0:T(128)S(1)} %copy-done.5, s32[128]{0:T(128)S(1)} %copy-done.6, s32[1]{0:T(128)S(6)} %copy.12.count_ref, bf16[128,128,128]{2,1,0:T(8,128)(2,1)S(1)} %copy-done), custom_call_target="tpu_custom_call" | custom-call | flops 2097152 | bytes 4194304 | tf_op jit(solution)/shard_map/densify/pallas_call | solution.py:129
  15.2 0.0 collective-permute-done.1.x2
  15.2 0.0 collective-permute-done.x1
  15.3 0.0 collective-permute-done.2.x3
  15.3 0.0 collective-permute-done.3.cot_far_ref
  15.3 0.7 %forward.1 = (bf16[512,128]{1,0:T(8,128)(2,1)S(1)}, f32[512,128]{1,0:T(8,128)S(1)}) custom-call(bf16[1024,1024]{1,0:T(8,128)(2,1)S(1)} %densify.1.tile_ref, bf16[256,128]{1,0:T(8,128)(2,1)S(1)} %copy-done.2, bf16[256,128]{1,0:T(8,128)(2,1)S(1)} %collective-permute-done.x1, bf16[256,128]{1,0:T(8,128)(2,1)S(1)} %collective-permute-done.1.x2, ...), custom_call_target="tpu_custom_call" | custom-call | tf_op jit(solution)/shard_map/forward/pallas_call | solution.py:257
  16.0 0.1 collective-permute-start.4
  16.1 1.3 %collective-permute-done.4 = bf16[512,128]{1,0:T(8,128)(2,1)S(1)} collective-permute-done((bf16[512,128]{1,0:T(8,128)(2,1)S(1)}, bf16[512,128]{1,0:T(8,128)(2,1)S(1)}, u32[]{:S(2)}, u32[]{:S(2)}) %collective-permute-start.4) | collective-permute-done | bytes 131104 | tf_op jit(solution)/shard_map/ppermute | solution.py:242
  17.5 0.3 collective-permute-start.5
  17.8 5.3 %collective-permute-done.5.far_ref = bf16[512,128]{1,0:T(8,128)(2,1)S(1)} collective-permute-done((bf16[512,128]{1,0:T(8,128)(2,1)S(1)}, bf16[512,128]{1,0:T(8,128)(2,1)S(1)}, u32[]{:S(2)}, u32[]{:S(2)}) %collective-permute-start.5) | collective-permute-done | bytes 131104 | tf_op jit(solution)/shard_map/ppermute | solution.py:242
  23.1 1.1 %layer.1 = (bf16[256,256]{1,0:T(8,128)(2,1)}, bf16[784,128]{1,0:T(8,128)(2,1)S(1)}) custom-call(bf16[512,128]{1,0:T(8,128)(2,1)S(1)} %add_convert_fusion.near_ref, bf16[512,128]{1,0:T(8,128)(2,1)S(1)} %collective-permute-done.5.far_ref, bf16[256,256]{1,0:T(8,128)(2,1)S(1)} %copy-done.1, bf16[256,256]{1,0:T(8,128)(2,1)S(1)} %collective-permute-done.3.cot_far_ref, ...), custom_call_target="tpu_custom_call" | custom-call | tf_op jit(solution)/shard_map/layer/pallas_call | solution.py:267
  24.2 0.0 collective-permute-start.6
  24.2 1.4 %collective-permute-done.6.sib_ref = bf16[784,128]{1,0:T(8,128)(2,1)S(1)} collective-permute-done((bf16[784,128]{1,0:T(8,128)(2,1)S(1)}, bf16[784,128]{1,0:T(8,128)(2,1)S(1)}, u32[]{:S(2)}, u32[]{:S(2)}) %collective-permute-start.6) | collective-permute-done | bytes 200736 | tf_op jit(solution)/shard_map/ppermute | solution.py:242
  25.6 0.8 %backward.1 = (f32[256,128]{1,0:T(8,128)S(1)}, bf16[528,128]{1,0:T(8,128)(2,1)S(1)}, bf16[256,128]{1,0:T(8,128)(2,1)S(1)}, bf16[256,128]{1,0:T(8,128)(2,1)S(1)}) custom-call(bf16[1024,1024]{1,0:T(8,128)(2,1)S(1)} %densify.1.tile_ref, bf16[784,128]{1,0:T(8,128)(2,1)S(1)} %get-tuple-element.27.own_ref, bf16[784,128]{1,0:T(8,128)(2,1)S(1)} %collective-permute-done.6.sib_ref), custom_call_target="tpu_custom_call" | custom-call | tf_op jit(solution)/shard_map/backward/pallas_call | solution.py:279
  26.5 0.5 %collective-permute-start.7 = (bf16[528,128]{1,0:T(8,128)(2,1)S(1)}, bf16[528,128]{1,0:T(8,128)(2,1)S(1)}, u32[]{:S(2)}, u32[]{:S(2)}) collective-permute-start(bf16[528,128]{1,0:T(8,128)(2,1)S(1)} %get-tuple-element.28), channel_id=1, source_target_pairs={{0,4},{4,0},{8,12},{12,8},{1,5},{5,1},{9,13},{13,9},{2,6},{6,2},{1... | collective-permute-start | bytes 405512 | tf_op jit(solution)/shard_map/ppermute | solution.py:242
  27.0 2.7 %collective-permute-start.9 = (bf16[256,128]{1,0:T(8,128)(2,1)S(1)}, bf16[256,128]{1,0:T(8,128)(2,1)S(1)}, u32[]{:S(2)}, u32[]{:S(2)}) collective-permute-start(bf16[256,128]{1,0:T(8,128)(2,1)S(1)} %get-tuple-element.32), channel_id=1, source_target_pairs={{0,8},{4,12},{8,0},{12,4},{1,9},{5,13},{9,1},{13,5},{2,10},{6,14},... | collective-permute-start | bytes 196616 | tf_op jit(solution)/shard_map/ppermute | solution.py:242
  29.7 1.2 %collective-permute-start.10 = (bf16[256,128]{1,0:T(8,128)(2,1)S(1)}, bf16[256,128]{1,0:T(8,128)(2,1)S(1)}, u32[]{:S(2)}, u32[]{:S(2)}) collective-permute-start(bf16[256,128]{1,0:T(8,128)(2,1)S(1)} %get-tuple-element.33), channel_id=1, source_target_pairs={{0,12},{4,8},{8,4},{12,0},{1,13},{5,9},{9,5},{13,1},{2,14},{6,10},... | collective-permute-start | bytes 196616 | tf_op jit(solution)/shard_map/ppermute | solution.py:242
  30.9 2.6 %collective-permute-done.7 = bf16[528,128]{1,0:T(8,128)(2,1)S(1)} collective-permute-done((bf16[528,128]{1,0:T(8,128)(2,1)S(1)}, bf16[528,128]{1,0:T(8,128)(2,1)S(1)}, u32[]{:S(2)}, u32[]{:S(2)}) %collective-permute-start.7) | collective-permute-done | bytes 135200 | tf_op jit(solution)/shard_map/ppermute | solution.py:242
  33.6 1.0 %collective-permute-start.8 = (bf16[272,128]{1,0:T(8,128)(2,1)S(1)}, bf16[272,128]{1,0:T(8,128)(2,1)S(1)}, u32[]{:S(2)}, u32[]{:S(2)}) collective-permute-start(bf16[272,128]{1,0:T(8,128)(2,1)S(1)} %add_convert_fusion.1.near_ref), channel_id=1, source_target_pairs={{0,8},{4,12},{8,0},{12,4},{1,9},{5,13},{9,1},{13,5},{2,10},{6,14},... | collective-permute-start | bytes 208904 | tf_op jit(solution)/shard_map/ppermute | solution.py:242
  34.6 0.0 collective-permute-done.9
  34.6 1.4 %collective-permute-done.10 = bf16[256,128]{1,0:T(8,128)(2,1)S(1)} collective-permute-done((bf16[256,128]{1,0:T(8,128)(2,1)S(1)}, bf16[256,128]{1,0:T(8,128)(2,1)S(1)}, u32[]{:S(2)}, u32[]{:S(2)}) %collective-permute-start.10) | collective-permute-done | bytes 65568 | tf_op jit(solution)/shard_map/ppermute | solution.py:242
  35.9 0.7 %add_convert_fusion.2 = bf16[256,128]{1,0:T(8,128)(2,1)} fusion(bf16[256,128]{1,0:T(8,128)(2,1)S(1)} %collective-permute-done.10, bf16[256,128]{1,0:T(8,128)(2,1)S(1)} %collective-permute-done.9, f32[256,128]{1,0:T(8,128)S(1)} %get-tuple-element.31, bf16[528,128]{1,0:T(8,128)(2,1)S(1)} %collective-permute-done.7), kind=kLoop, calls=%fused_computation.2 | loop fusion | flops 229376 | bytes 393216 | tf_op jit(solution)/shard_map/convert_element_type | solution.py:297
  36.6 3.0 %collective-permute-done.8.far_ref = bf16[272,128]{1,0:T(8,128)(2,1)S(1)} collective-permute-done((bf16[272,128]{1,0:T(8,128)(2,1)S(1)}, bf16[272,128]{1,0:T(8,128)(2,1)S(1)}, u32[]{:S(2)}, u32[]{:S(2)}) %collective-permute-start.8) | collective-permute-done | bytes 69664 | tf_op jit(solution)/shard_map/ppermute | solution.py:242
  39.6 0.7 %finish.1 = (f32[128,256]{1,0:T(8,128)}, f32[1,256]{1,0:T(1,128)}) custom-call(bf16[272,128]{1,0:T(8,128)(2,1)S(1)} %add_convert_fusion.1.near_ref, bf16[272,128]{1,0:T(8,128)(2,1)S(1)} %collective-permute-done.8.far_ref), custom_call_target="tpu_custom_call" | custom-call | tf_op jit(solution)/shard_map/finish/pallas_call | solution.py:299
  (12 shorter events, 0.1 us)
Async XLA Ops:
  0.6 14.6 %collective-permute-start.3 = (bf16[256,256]{1,0:T(8,128)(2,1)}, bf16[256,256]{1,0:T(8,128)(2,1)S(1)}, u32[]{:S(2)}, u32[]{:S(2)}) collective-permute-start(bf16[256,256]{1,0:T(8,128)(2,1)} %cot_ref.1), channel_id=1, source_target_pairs={{0,2},{1,3},{2,0},{3,1},{4,6},{5,7},{6,4},{7,5},{8,10},{9,11},{10,... | collective-permute-start | bytes 393224 | tf_op jit(solution)/shard_map/ppermute | solution.py:242
  3.6 11.6 %collective-permute-start.1 = (bf16[256,128]{1,0:T(8,128)(2,1)}, bf16[256,128]{1,0:T(8,128)(2,1)S(1)}, u32[]{:S(2)}, u32[]{:S(2)}) collective-permute-start(bf16[256,128]{1,0:T(8,128)(2,1)} %x0), channel_id=1, source_target_pairs={{0,8},{4,12},{8,0},{12,4},{1,9},{5,13},{9,1},{13,5},{2,10},{6,14},... | collective-permute-start | bytes 196616 | tf_op jit(solution)/shard_map/ppermute | solution.py:242
  6.2 9.0 %collective-permute-start = (bf16[256,128]{1,0:T(8,128)(2,1)}, bf16[256,128]{1,0:T(8,128)(2,1)S(1)}, u32[]{:S(2)}, u32[]{:S(2)}) collective-permute-start(bf16[256,128]{1,0:T(8,128)(2,1)} %x0), channel_id=1, source_target_pairs={{0,4},{4,0},{8,12},{12,8},{1,5},{5,1},{9,13},{13,9},{2,6},{6,2},{1... | collective-permute-start | bytes 196616 | tf_op jit(solution)/shard_map/ppermute | solution.py:242
  7.8 7.5 %collective-permute-start.2 = (bf16[256,128]{1,0:T(8,128)(2,1)}, bf16[256,128]{1,0:T(8,128)(2,1)S(1)}, u32[]{:S(2)}, u32[]{:S(2)}) collective-permute-start(bf16[256,128]{1,0:T(8,128)(2,1)} %x0), channel_id=1, source_target_pairs={{0,12},{4,8},{8,4},{12,0},{1,13},{5,9},{9,5},{13,1},{2,14},{6,10},... | collective-permute-start | bytes 196616 | tf_op jit(solution)/shard_map/ppermute | solution.py:242
  8.7 2.2 %copy-start = (bf16[128,128,128]{2,1,0:T(8,128)(2,1)S(1)}, bf16[128,128,128]{2,1,0:T(8,128)(2,1)}, u32[]{:S(2)}) copy-start(bf16[128,128,128]{2,1,0:T(8,128)(2,1)} %values_ref.1) | copy-start | bytes 12582916
  10.9 0.7 %copy-start.5 = (s32[128]{0:T(128)S(1)}, s32[128]{0:T(128)}, u32[]{:S(2)}) copy-start(s32[128]{0:T(128)} %rows_ref.1) | copy-start | bytes 1540
  11.5 0.7 %copy-start.6 = (s32[128]{0:T(128)S(1)}, s32[128]{0:T(128)}, u32[]{:S(2)}) copy-start(s32[128]{0:T(128)} %cols_ref.1) | copy-start | bytes 1540
  12.2 3.1 %copy-start.2 = (bf16[256,128]{1,0:T(8,128)(2,1)S(1)}, bf16[256,128]{1,0:T(8,128)(2,1)}, u32[]{:S(2)}) copy-start(bf16[256,128]{1,0:T(8,128)(2,1)} %x0) | copy-start | bytes 196612
  12.2 10.9 %copy-start.1 = (bf16[256,256]{1,0:T(8,128)(2,1)S(1)}, bf16[256,256]{1,0:T(8,128)(2,1)}, u32[]{:S(2)}) copy-start(bf16[256,256]{1,0:T(8,128)(2,1)} %cot_ref.1) | copy-start | bytes 393220
  12.2 10.9 %copy-start.3 = (bf16[128,256]{1,0:T(8,128)(2,1)S(1)}, bf16[128,256]{1,0:T(8,128)(2,1)}, u32[]{:S(2)}) copy-start(bf16[128,256]{1,0:T(8,128)(2,1)} %weight_ref.1) | copy-start | bytes 196612
  12.2 10.9 %copy-start.4 = (f32[256]{0:T(256)S(1)}, f32[256]{0:T(256)}, u32[]{:S(2)}) copy-start(f32[256]{0:T(256)} %param.14) | copy-start | bytes 3076
  16.0 1.4 %collective-permute-start.4 = (bf16[512,128]{1,0:T(8,128)(2,1)S(1)}, bf16[512,128]{1,0:T(8,128)(2,1)S(1)}, u32[]{:S(2)}, u32[]{:S(2)}) collective-permute-start(bf16[512,128]{1,0:T(8,128)(2,1)S(1)} %get-tuple-element.24), channel_id=1, source_target_pairs={{0,1},{1,0},{2,3},{3,2},{4,5},{5,4},{6,7},{7,6},{8,9},{9,8},{10,11... | collective-permute-start | bytes 393224 | tf_op jit(solution)/shard_map/ppermute | solution.py:242
  17.5 5.6 %collective-permute-start.5 = (bf16[512,128]{1,0:T(8,128)(2,1)S(1)}, bf16[512,128]{1,0:T(8,128)(2,1)S(1)}, u32[]{:S(2)}, u32[]{:S(2)}) collective-permute-start(bf16[512,128]{1,0:T(8,128)(2,1)S(1)} %add_convert_fusion.near_ref), channel_id=1, source_target_pairs={{0,2},{1,3},{2,0},{3,1},{4,6},{5,7},{6,4},{7,5},{8,10},{9,11},{10,... | collective-permute-start | bytes 393224 | tf_op jit(solution)/shard_map/ppermute | solution.py:242
  24.2 1.4 %collective-permute-start.6 = (bf16[784,128]{1,0:T(8,128)(2,1)S(1)}, bf16[784,128]{1,0:T(8,128)(2,1)S(1)}, u32[]{:S(2)}, u32[]{:S(2)}) collective-permute-start(bf16[784,128]{1,0:T(8,128)(2,1)S(1)} %get-tuple-element.27.own_ref), channel_id=1, source_target_pairs={{0,1},{1,0},{2,3},{3,2},{4,5},{5,4},{6,7},{7,6},{8,9},{9,8},{10,11... | collective-permute-start | bytes 602120 | tf_op jit(solution)/shard_map/ppermute | solution.py:242
  26.5 7.1 %collective-permute-start.7 = (bf16[528,128]{1,0:T(8,128)(2,1)S(1)}, bf16[528,128]{1,0:T(8,128)(2,1)S(1)}, u32[]{:S(2)}, u32[]{:S(2)}) collective-permute-start(bf16[528,128]{1,0:T(8,128)(2,1)S(1)} %get-tuple-element.28), channel_id=1, source_target_pairs={{0,4},{4,0},{8,12},{12,8},{1,5},{5,1},{9,13},{13,9},{2,6},{6,2},{1... | collective-permute-start | bytes 405512 | tf_op jit(solution)/shard_map/ppermute | solution.py:242
  27.0 7.6 %collective-permute-start.9 = (bf16[256,128]{1,0:T(8,128)(2,1)S(1)}, bf16[256,128]{1,0:T(8,128)(2,1)S(1)}, u32[]{:S(2)}, u32[]{:S(2)}) collective-permute-start(bf16[256,128]{1,0:T(8,128)(2,1)S(1)} %get-tuple-element.32), channel_id=1, source_target_pairs={{0,8},{4,12},{8,0},{12,4},{1,9},{5,13},{9,1},{13,5},{2,10},{6,14},... | collective-permute-start | bytes 196616 | tf_op jit(solution)/shard_map/ppermute | solution.py:242
  29.7 6.2 %collective-permute-start.10 = (bf16[256,128]{1,0:T(8,128)(2,1)S(1)}, bf16[256,128]{1,0:T(8,128)(2,1)S(1)}, u32[]{:S(2)}, u32[]{:S(2)}) collective-permute-start(bf16[256,128]{1,0:T(8,128)(2,1)S(1)} %get-tuple-element.33), channel_id=1, source_target_pairs={{0,12},{4,8},{8,4},{12,0},{1,13},{5,9},{9,5},{13,1},{2,14},{6,10},... | collective-permute-start | bytes 196616 | tf_op jit(solution)/shard_map/ppermute | solution.py:242
  33.6 6.0 %collective-permute-start.8 = (bf16[272,128]{1,0:T(8,128)(2,1)S(1)}, bf16[272,128]{1,0:T(8,128)(2,1)S(1)}, u32[]{:S(2)}, u32[]{:S(2)}) collective-permute-start(bf16[272,128]{1,0:T(8,128)(2,1)S(1)} %add_convert_fusion.1.near_ref), channel_id=1, source_target_pairs={{0,8},{4,12},{8,0},{12,4},{1,9},{5,13},{9,1},{13,5},{2,10},{6,14},... | collective-permute-start | bytes 208904 | tf_op jit(solution)/shard_map/ppermute | solution.py:242

commit v3 on v2

--- a/solution.py
+++ b/solution.py
@@ -15,6 +15,7 @@
 SCALARS = pl.BlockSpec(memory_space=pltpu.SMEM)
 LIMIT = pltpu.CompilerParams(vmem_limit_bytes=16 * 2**20)
 BIAS_ROWS = 16
+GROUP = 4
 
 
 def pick_rows(pick_index, live_mask, source_rows):
@@ -94,28 +95,45 @@
     return (hidden, grad_weight * norm_scale, grad_bias * norm_scale, grad_features)
 
 
-def densify_kernel(chunks, row_blocks, col_blocks, rows_ref, cols_ref, count_ref, values_ref, tile_ref, held, acc, sems):
+def densify_kernel(chunks, row_blocks, col_blocks, count_in, rows_in, cols_in, values_ref, tile_ref,
+                   held, acc, count_ref, rows_ref, cols_ref, sems, scalar_sems):
     slots, block, _ = values_ref.shape
     size = slots // chunks
+    scalars = [
+        pltpu.make_async_copy(source, held_in, scalar_sems.at[i])
+        for i, (source, held_in) in enumerate(
+            ((count_in, count_ref), (rows_in, rows_ref), (cols_in, cols_ref))
+        )
+    ]
     copies = [
         pltpu.make_async_copy(
             values_ref.at[pl.ds(i * size, size)], held.at[pl.ds(i * size, size)], sems.at[i]
         )
         for i in range(chunks)
     ]
-    for copy in copies:
+    for copy in scalars + copies:
         copy.start()
     acc[...] = jnp.zeros_like(acc)
-    live = count_ref[0]
+    for copy in scalars:
+        copy.wait()
+    live = count_ref[0, 0]
 
     def add_slot(i, carry):
         place = rows_ref[i] * col_blocks + cols_ref[i]
         acc[place] = acc[place] + held[i].astype(F32)
         return carry
 
+    def add_group(first, i, carry):
+        for j in range(GROUP):
+            add_slot(first + i * GROUP + j, carry)
+        return carry
+
     for i, copy in enumerate(copies):
         copy.wait()
-        lax.fori_loop(i * size, jnp.clip(live, i * size, (i + 1) * size), add_slot, 0)
+        here = jnp.clip(live - i * size, 0, size)
+        groups = here // GROUP
+        lax.fori_loop(0, groups, functools.partial(add_group, i * size), 0)
+        lax.fori_loop(i * size + groups * GROUP, i * size + here, add_slot, 0)
     for r in range(row_blocks):
         for c in range(col_blocks):
             tile_ref[pl.ds(r * block, block), pl.ds(c * block, block)] = acc[
@@ -126,20 +144,28 @@
 def densify(values, rows, cols, count, row_blocks, col_blocks):
     slots, block, _ = values.shape
     chunks = 8
+    in_hbm = [
+        pltpu.with_memory_space_constraint(array, pltpu.HBM)
+        for array in (rows, cols, values)
+    ]
     return pl.pallas_call(
         functools.partial(densify_kernel, chunks, row_blocks, col_blocks),
-        in_specs=[SCALARS] * 3 + [pl.BlockSpec(memory_space=pltpu.HBM)],
+        in_specs=[WHOLE] + [pl.BlockSpec(memory_space=pltpu.HBM)] * 3,
         out_specs=WHOLE,
         out_shape=jax.ShapeDtypeStruct((row_blocks * block, col_blocks * block), BF16),
         scratch_shapes=[
             pltpu.VMEM(values.shape, BF16),
             pltpu.VMEM((row_blocks * col_blocks, block, block), F32),
+            pltpu.SMEM((1, 1), jnp.int32),
+            pltpu.SMEM(rows.shape, jnp.int32),
+            pltpu.SMEM(cols.shape, jnp.int32),
             pltpu.SemaphoreType.DMA((chunks,)),
+            pltpu.SemaphoreType.DMA((3,)),
         ],
         compiler_params=LIMIT,
         cost_estimate=pl.CostEstimate(flops=slots * block * block, bytes_accessed=values.size * 2, transcendentals=0),
         name="densify",
-    )(rows, cols, count, values)
+    )(count.reshape(1, 1), *in_hbm)
 
 
 def forward_kernel(tile_ref, x0, x1, x2, x3, send_ref, keep_ref):
@@ -202,22 +228,32 @@
     ).astype(BF16)
 
 
-def backward_kernel(tile_ref, own_ref, sib_ref, keep_ref, send1, send2, send3):
-    row = lax.axis_index("row")
+def backward_terms(tile_ref, half, k, grad_ref, rows):
+    col_at = pl.multiple_of(jnp.bitwise_xor(lax.axis_index("row"), k) * rows, rows)
+    total = None
+    for x in range(2):
+        row_at = pl.multiple_of((2 * x + half) * rows, rows)
+        term = lax.dot_general(
+            tile_ref[pl.ds(row_at, rows), pl.ds(col_at, rows)],
+            grad_ref[pl.ds(x * rows, rows), :],
+            (((0,), (0,)), ((), ())),
+            preferred_element_type=F32,
+        )
+        total = term if total is None else total + term
+    return total
+
+
+def backward_mine_kernel(tile_ref, own_ref, part_ref):
+    core = lax.rem(lax.axis_index("col"), 2)
+    for k in range(ROWS):
+        part_ref[k] = backward_terms(tile_ref, core, k, own_ref, part_ref.shape[1])
+
+
+def backward_kernel(tile_ref, own_ref, sib_ref, part_ref, keep_ref, send1, send2, send3):
     core = lax.rem(lax.axis_index("col"), 2)
     rows = keep_ref.shape[0]
     for k, out in ((1, send1), (2, send2), (3, send3), (0, keep_ref)):
-        col_at = pl.multiple_of(jnp.bitwise_xor(row, k) * rows, rows)
-        total = None
-        for half, ref in ((core, own_ref), (1 - core, sib_ref)):
-            for x in range(2):
-                row_at = pl.multiple_of((2 * x + half) * rows, rows)
-                tile = tile_ref[pl.ds(row_at, rows), pl.ds(col_at, rows)]
-                term = lax.dot_general(
-                    tile, ref[pl.ds(x * rows, rows), :], (((0,), (0,)), ((), ())),
-                    preferred_element_type=F32,
-                )
-                total = term if total is None else total + term
+        total = part_ref[k] + backward_terms(tile_ref, 1 - core, k, sib_ref, rows)
         out[pl.ds(0, rows), :] = total.astype(out.dtype)
     extra = pl.ds(2 * rows, own_ref.shape[0] - 2 * rows)
     send1[pl.ds(rows, send1.shape[0] - rows), :] = (
@@ -251,8 +287,9 @@
     col_blocks = ROWS * node_rows // block_size
     extra = hid + BIAS_ROWS
     shards = [features] + [swap(features, "row", k) for k in (1, 2, 3)]
-    shards, cot_far = lax.optimization_barrier((shards, swap(cotangent, "col", 2)))
     tile = densify(block_values, block_rows, block_cols, block_count, row_blocks, col_blocks)
+    tile, shards[1], cotangent = lax.optimization_barrier((tile, shards[1], cotangent))
+    cot_far = swap(cotangent, "col", 2)
     half = (2 * node_rows, width_in)
     send, keep = pl.pallas_call(
         forward_kernel,
@@ -262,7 +299,8 @@
         compiler_params=LIMIT,
         name="forward",
     )(tile, *shards)
-    near = (keep + swap(send, "col", 1).astype(F32)).astype(BF16)
+    sib, cot_far = lax.optimization_barrier((swap(send, "col", 1), cot_far))
+    near = (keep + sib.astype(F32)).astype(BF16)
     far = swap(near, "col", 2)
     hidden, grads = pl.pallas_call(
         layer_kernel,
@@ -276,9 +314,18 @@
         name="layer",
     )(near, far, cotangent, cot_far, weight, bias.reshape(1, hid))
     block = jax.ShapeDtypeStruct((node_rows, width_in), BF16)
+    part = pl.pallas_call(
+        backward_mine_kernel,
+        in_specs=[WHOLE] * 2,
+        out_specs=WHOLE,
+        out_shape=jax.ShapeDtypeStruct((ROWS, node_rows, width_in), F32),
+        compiler_params=LIMIT,
+        cost_estimate=pl.CostEstimate(flops=tile.size * width_in, bytes_accessed=tile.size, transcendentals=0),
+        name="backward_mine",
+    )(tile, grads)
     own, *sends = pl.pallas_call(
         backward_kernel,
-        in_specs=[WHOLE] * 3,
+        in_specs=[WHOLE] * 4,
         out_specs=[WHOLE] * 4,
         out_shape=[
             jax.ShapeDtypeStruct(block.shape, F32),
@@ -288,7 +335,7 @@
         ],
         compiler_params=LIMIT,
         name="backward",
-    )(tile, grads, swap(grads, "col", 1))
+    )(tile, grads, swap(grads, "col", 1), part)
     got = [swap(part, "row", k) for k, part in zip((1, 2, 3), sends)]
     pair = (sends[0][node_rows:].astype(F32) + got[0][node_rows:].astype(F32)).astype(BF16)
     pair_far = swap(pair, "row", 2)

time: 40.5 us -> 36.9 us (0.911)
  local copies, waits for them, and re-layouts: 3.51 us -> 0.02 us
  starting transfers between devices: 13.2 us -> 15.7 us
  waiting for transfers between devices: 15.1 us -> 12.7 us
    unnamed x14 -> x8, local copies, waits for them, and re-layouts: 3.51 us -> 0.02 us
    ppermute x11, starting transfers between devices: 13.2 us -> 15.7 us  [swap(): return lax.ppermute(array, axis, [(i, i ^ bit) for i in range(size)])]
    ppermute x11, waiting for transfers between devices: 15.1 us -> 12.7 us  [swap(): return lax.ppermute(array, axis, [(i, i ^ bit) for i in range(size)])]
    pallas_call x1 -> x2, Pallas kernels: 0.85 us -> 1.05 us  [the longest x1 0.54 us: dense_tile(): pl.pallas_call(backward_kernel, in_specs=[WHOLE] * 4, out_specs=[WHOLE] *...]
  transfers between devices with their start and end apart: 11 -> 11, of which waited for: 6 -> 7; matrix products, arithmetic and copies ran while one was open for 2% -> 2% of each run, Pallas kernels for 8% -> 11%
where the time goes in v3:
time: 36.9 us; the launch traced here: 36.8 us
  starting transfers between devices  15.7 us (43%)
  waiting for transfers between devices  12.7 us (34%)
  Pallas kernels  6.25 us (17%)
  between operations  1.39 us (4%)
  other arithmetic  0.72 us (2%)
    ppermute x11, starting transfers between devices, swap(): return lax.ppermute(array, axis, [(i, i ^ bit) for i in range(size)])  15.7 us
    ppermute x11, waiting for transfers between devices, swap(): return lax.ppermute(array, axis, [(i, i ^ bit) for i in range(size)])  12.7 us
    pallas_call x1, Pallas kernels, densify(): pl.pallas_call(functools.partial(densify_kernel, chunks, row_blocks, col_...  2.71 us
    pallas_call x1, Pallas kernels, dense_tile(): pl.pallas_call(layer_kernel, in_specs=[WHOLE] * 6, out_specs=[WHOLE] * 2,...  1.11 us
  transfers between devices with their start and end apart: 11, of which 7 were waited for; matrix products, arithmetic and copies ran while one was open for 2% of the time, Pallas kernels for 11%

profile of v3, /device:TPU:0, one launch (start us, length us, event | category | flops | bytes accessed | tf_op | source)
XLA Modules:
  0.0 36.8 jit_solution(15928053506611607281)
XLA Ops:
  0.6 0.0 copy-start.1
  0.6 0.0 copy-start
  0.7 3.1 %collective-permute-start = (bf16[256,128]{1,0:T(8,128)(2,1)}, bf16[256,128]{1,0:T(8,128)(2,1)S(1)}, u32[]{:S(2)}, u32[]{:S(2)}) collective-permute-start(bf16[256,128]{1,0:T(8,128)(2,1)} %x0.1), channel_id=1, source_target_pairs={{0,4},{4,0},{8,12},{12,8},{1,5},{5,1},{9,13},{13,9},{2,6},{6,2},{1... | collective-permute-start | bytes 196616 | tf_op jit(solution)/shard_map/ppermute | solution.py:278
  3.7 2.6 %collective-permute-start.1 = (bf16[256,128]{1,0:T(8,128)(2,1)}, bf16[256,128]{1,0:T(8,128)(2,1)S(1)}, u32[]{:S(2)}, u32[]{:S(2)}) collective-permute-start(bf16[256,128]{1,0:T(8,128)(2,1)} %x0.1), channel_id=1, source_target_pairs={{0,8},{4,12},{8,0},{12,4},{1,9},{5,13},{9,1},{13,5},{2,10},{6,14},... | collective-permute-start | bytes 196616 | tf_op jit(solution)/shard_map/ppermute | solution.py:278
  6.3 0.0 collective-permute-start.2
  7.0 2.7 %densify.1.tile_ref = bf16[1024,1024]{1,0:T(8,128)(2,1)S(1)} custom-call(s32[1,1]{1,0:T(1,128)} %bitcast.3.count_in, s32[128]{0:T(128)} %rows_in.1, s32[128]{0:T(128)} %cols_in.1, bf16[128,128,128]{2,1,0:T(8,128)(2,1)} %values_ref.1), custom_call_target="tpu_custom_call" | custom-call | flops 2097152 | bytes 4194304 | tf_op jit(solution)/shard_map/densify/pallas_call | solution.py:151
  9.7 0.0 collective-permute-done.x1
  9.7 1.8 %collective-permute-start.4 = (bf16[256,256]{1,0:T(8,128)(2,1)S(1)}, bf16[256,256]{1,0:T(8,128)(2,1)S(1)}, u32[]{:S(2)}, u32[]{:S(2)}) collective-permute-start(bf16[256,256]{1,0:T(8,128)(2,1)S(1)} %copy-done), channel_id=1, source_target_pairs={{0,2},{1,3},{2,0},{3,1},{4,6},{5,7},{6,4},{7,5},{8,10},{9,11},{10,... | collective-permute-start | bytes 393224 | tf_op jit(solution)/shard_map/ppermute | solution.py:278
  11.5 0.0 collective-permute-done.1.x2
  11.5 1.1 %collective-permute-done.2.x3 = bf16[256,128]{1,0:T(8,128)(2,1)S(1)} collective-permute-done((bf16[256,128]{1,0:T(8,128)(2,1)}, bf16[256,128]{1,0:T(8,128)(2,1)S(1)}, u32[]{:S(2)}, u32[]{:S(2)}) %collective-permute-start.2) | collective-permute-done | bytes 65568 | tf_op jit(solution)/shard_map/ppermute | solution.py:278
  12.6 0.0 copy-done.1
  12.6 0.7 %forward.1 = (bf16[512,128]{1,0:T(8,128)(2,1)S(1)}, f32[512,128]{1,0:T(8,128)S(1)}) custom-call(bf16[1024,1024]{1,0:T(8,128)(2,1)S(1)} %densify.1.tile_ref, bf16[256,128]{1,0:T(8,128)(2,1)S(1)} %copy-done.1, bf16[256,128]{1,0:T(8,128)(2,1)S(1)} %collective-permute-done.x1, bf16[256,128]{1,0:T(8,128)(2,1)S(1)} %collective-permute-done.1.x2, ...), custom_call_target="tpu_custom_call" | custom-call | tf_op jit(solution)/shard_map/forward/pallas_call | solution.py:294
  13.3 0.1 collective-permute-start.3
  13.4 1.4 %collective-permute-done.4.cot_far_ref = bf16[256,256]{1,0:T(8,128)(2,1)S(1)} collective-permute-done((bf16[256,256]{1,0:T(8,128)(2,1)S(1)}, bf16[256,256]{1,0:T(8,128)(2,1)S(1)}, u32[]{:S(2)}, u32[]{:S(2)}) %collective-permute-start.4) | collective-permute-done | bytes 131104 | tf_op jit(solution)/shard_map/ppermute | solution.py:278
  14.8 0.0 collective-permute-done.3
  14.8 1.8 %collective-permute-start.5 = (bf16[512,128]{1,0:T(8,128)(2,1)S(1)}, bf16[512,128]{1,0:T(8,128)(2,1)S(1)}, u32[]{:S(2)}, u32[]{:S(2)}) collective-permute-start(bf16[512,128]{1,0:T(8,128)(2,1)S(1)} %add_convert_fusion.near_ref), channel_id=1, source_target_pairs={{0,2},{1,3},{2,0},{3,1},{4,6},{5,7},{6,4},{7,5},{8,10},{9,11},{10,... | collective-permute-start | bytes 393224 | tf_op jit(solution)/shard_map/ppermute | solution.py:278
  16.6 3.8 %collective-permute-done.5.far_ref = bf16[512,128]{1,0:T(8,128)(2,1)S(1)} collective-permute-done((bf16[512,128]{1,0:T(8,128)(2,1)S(1)}, bf16[512,128]{1,0:T(8,128)(2,1)S(1)}, u32[]{:S(2)}, u32[]{:S(2)}) %collective-permute-start.5) | collective-permute-done | bytes 131104 | tf_op jit(solution)/shard_map/ppermute | solution.py:278
  20.4 1.1 %layer.1 = (bf16[256,256]{1,0:T(8,128)(2,1)}, bf16[784,128]{1,0:T(8,128)(2,1)S(1)}) custom-call(bf16[512,128]{1,0:T(8,128)(2,1)S(1)} %add_convert_fusion.near_ref, bf16[512,128]{1,0:T(8,128)(2,1)S(1)} %collective-permute-done.5.far_ref, bf16[256,256]{1,0:T(8,128)(2,1)S(1)} %copy-done, bf16[256,256]{1,0:T(8,128)(2,1)S(1)} %collective-permute-done.4.cot_far_ref, ...), custom_call_target="tpu_custom_call" | custom-call | tf_op jit(solution)/shard_map/layer/pallas_call | solution.py:305
  21.5 0.0 collective-permute-start.6
  21.5 0.5 %backward_mine.1.part_ref = f32[4,256,128]{2,1,0:T(8,128)S(1)} custom-call(bf16[1024,1024]{1,0:T(8,128)(2,1)S(1)} %densify.1.tile_ref, bf16[784,128]{1,0:T(8,128)(2,1)S(1)} %get-tuple-element.27.own_ref), custom_call_target="tpu_custom_call" | custom-call | flops 134217728 | bytes 1048576 | tf_op jit(solution)/shard_map/backward_mine/pallas_call | solution.py:317
  22.0 0.9 %collective-permute-done.6.sib_ref = bf16[784,128]{1,0:T(8,128)(2,1)S(1)} collective-permute-done((bf16[784,128]{1,0:T(8,128)(2,1)S(1)}, bf16[784,128]{1,0:T(8,128)(2,1)S(1)}, u32[]{:S(2)}, u32[]{:S(2)}) %collective-permute-start.6) | collective-permute-done | bytes 200736 | tf_op jit(solution)/shard_map/ppermute | solution.py:278
  23.0 0.5 %backward.1 = (f32[256,128]{1,0:T(8,128)S(1)}, bf16[528,128]{1,0:T(8,128)(2,1)S(1)}, bf16[256,128]{1,0:T(8,128)(2,1)S(1)}, bf16[256,128]{1,0:T(8,128)(2,1)S(1)}) custom-call(bf16[1024,1024]{1,0:T(8,128)(2,1)S(1)} %densify.1.tile_ref, bf16[784,128]{1,0:T(8,128)(2,1)S(1)} %get-tuple-element.27.own_ref, bf16[784,128]{1,0:T(8,128)(2,1)S(1)} %collective-permute-done.6.sib_ref, ...), custom_call_target="tpu_custom_call" | custom-call | tf_op jit(solution)/shard_map/backward/pallas_call | solution.py:326
  23.5 0.4 %collective-permute-start.7 = (bf16[528,128]{1,0:T(8,128)(2,1)S(1)}, bf16[528,128]{1,0:T(8,128)(2,1)S(1)}, u32[]{:S(2)}, u32[]{:S(2)}) collective-permute-start(bf16[528,128]{1,0:T(8,128)(2,1)S(1)} %get-tuple-element.28), channel_id=1, source_target_pairs={{0,4},{4,0},{8,12},{12,8},{1,5},{5,1},{9,13},{13,9},{2,6},{6,2},{1... | collective-permute-start | bytes 405512 | tf_op jit(solution)/shard_map/ppermute | solution.py:278
  23.9 3.5 %collective-permute-start.9 = (bf16[256,128]{1,0:T(8,128)(2,1)S(1)}, bf16[256,128]{1,0:T(8,128)(2,1)S(1)}, u32[]{:S(2)}, u32[]{:S(2)}) collective-permute-start(bf16[256,128]{1,0:T(8,128)(2,1)S(1)} %get-tuple-element.32), channel_id=1, source_target_pairs={{0,8},{4,12},{8,0},{12,4},{1,9},{5,13},{9,1},{13,5},{2,10},{6,14},... | collective-permute-start | bytes 196616 | tf_op jit(solution)/shard_map/ppermute | solution.py:278
  27.4 0.6 %collective-permute-start.10 = (bf16[256,128]{1,0:T(8,128)(2,1)S(1)}, bf16[256,128]{1,0:T(8,128)(2,1)S(1)}, u32[]{:S(2)}, u32[]{:S(2)}) collective-permute-start(bf16[256,128]{1,0:T(8,128)(2,1)S(1)} %get-tuple-element.33), channel_id=1, source_target_pairs={{0,12},{4,8},{8,4},{12,0},{1,13},{5,9},{9,5},{13,1},{2,14},{6,10},... | collective-permute-start | bytes 196616 | tf_op jit(solution)/shard_map/ppermute | solution.py:278
  28.0 2.6 %collective-permute-done.7 = bf16[528,128]{1,0:T(8,128)(2,1)S(1)} collective-permute-done((bf16[528,128]{1,0:T(8,128)(2,1)S(1)}, bf16[528,128]{1,0:T(8,128)(2,1)S(1)}, u32[]{:S(2)}, u32[]{:S(2)}) %collective-permute-start.7) | collective-permute-done | bytes 135200 | tf_op jit(solution)/shard_map/ppermute | solution.py:278
  30.6 1.9 %collective-permute-start.8 = (bf16[272,128]{1,0:T(8,128)(2,1)S(1)}, bf16[272,128]{1,0:T(8,128)(2,1)S(1)}, u32[]{:S(2)}, u32[]{:S(2)}) collective-permute-start(bf16[272,128]{1,0:T(8,128)(2,1)S(1)} %add_convert_fusion.1.near_ref), channel_id=1, source_target_pairs={{0,8},{4,12},{8,0},{12,4},{1,9},{5,13},{9,1},{13,5},{2,10},{6,14},... | collective-permute-start | bytes 208904 | tf_op jit(solution)/shard_map/ppermute | solution.py:278
  32.6 0.0 collective-permute-done.9
  32.6 1.1 %collective-permute-done.10 = bf16[256,128]{1,0:T(8,128)(2,1)S(1)} collective-permute-done((bf16[256,128]{1,0:T(8,128)(2,1)S(1)}, bf16[256,128]{1,0:T(8,128)(2,1)S(1)}, u32[]{:S(2)}, u32[]{:S(2)}) %collective-permute-start.10) | collective-permute-done | bytes 65568 | tf_op jit(solution)/shard_map/ppermute | solution.py:278
  33.6 0.7 %add_convert_fusion.2 = bf16[256,128]{1,0:T(8,128)(2,1)} fusion(bf16[256,128]{1,0:T(8,128)(2,1)S(1)} %collective-permute-done.10, bf16[256,128]{1,0:T(8,128)(2,1)S(1)} %collective-permute-done.9, f32[256,128]{1,0:T(8,128)S(1)} %get-tuple-element.31, bf16[528,128]{1,0:T(8,128)(2,1)S(1)} %collective-permute-done.7), kind=kLoop, calls=%fused_computation.2 | loop fusion | flops 229376 | bytes 393216 | tf_op jit(solution)/shard_map/convert_element_type | solution.py:344
  34.3 1.8 %collective-permute-done.8.far_ref = bf16[272,128]{1,0:T(8,128)(2,1)S(1)} collective-permute-done((bf16[272,128]{1,0:T(8,128)(2,1)S(1)}, bf16[272,128]{1,0:T(8,128)(2,1)S(1)}, u32[]{:S(2)}, u32[]{:S(2)}) %collective-permute-start.8) | collective-permute-done | bytes 69664 | tf_op jit(solution)/shard_map/ppermute | solution.py:278
  36.1 0.7 %finish.1 = (f32[128,256]{1,0:T(8,128)}, f32[1,256]{1,0:T(1,128)}) custom-call(bf16[272,128]{1,0:T(8,128)(2,1)S(1)} %add_convert_fusion.1.near_ref, bf16[272,128]{1,0:T(8,128)(2,1)S(1)} %collective-permute-done.8.far_ref), custom_call_target="tpu_custom_call" | custom-call | tf_op jit(solution)/shard_map/finish/pallas_call | solution.py:346
  (7 shorter events, 0.1 us)
Async XLA Ops:
  0.6 12.0 %copy-start.1 = (bf16[256,128]{1,0:T(8,128)(2,1)S(1)}, bf16[256,128]{1,0:T(8,128)(2,1)}, u32[]{:S(2)}) copy-start(bf16[256,128]{1,0:T(8,128)(2,1)} %x0.1) | copy-start | bytes 196612
  0.6 9.1 %copy-start = (bf16[256,256]{1,0:T(8,128)(2,1)S(1)}, bf16[256,256]{1,0:T(8,128)(2,1)}, u32[]{:S(2)}) copy-start(bf16[256,256]{1,0:T(8,128)(2,1)} %cot_ref) | copy-start | bytes 393220
  0.7 9.1 %collective-permute-start = (bf16[256,128]{1,0:T(8,128)(2,1)}, bf16[256,128]{1,0:T(8,128)(2,1)S(1)}, u32[]{:S(2)}, u32[]{:S(2)}) collective-permute-start(bf16[256,128]{1,0:T(8,128)(2,1)} %x0.1), channel_id=1, source_target_pairs={{0,4},{4,0},{8,12},{12,8},{1,5},{5,1},{9,13},{13,9},{2,6},{6,2},{1... | collective-permute-start | bytes 196616 | tf_op jit(solution)/shard_map/ppermute | solution.py:278
  3.7 7.8 %collective-permute-start.1 = (bf16[256,128]{1,0:T(8,128)(2,1)}, bf16[256,128]{1,0:T(8,128)(2,1)S(1)}, u32[]{:S(2)}, u32[]{:S(2)}) collective-permute-start(bf16[256,128]{1,0:T(8,128)(2,1)} %x0.1), channel_id=1, source_target_pairs={{0,8},{4,12},{8,0},{12,4},{1,9},{5,13},{9,1},{13,5},{2,10},{6,14},... | collective-permute-start | bytes 196616 | tf_op jit(solution)/shard_map/ppermute | solution.py:278
  6.3 6.3 %collective-permute-start.2 = (bf16[256,128]{1,0:T(8,128)(2,1)}, bf16[256,128]{1,0:T(8,128)(2,1)S(1)}, u32[]{:S(2)}, u32[]{:S(2)}) collective-permute-start(bf16[256,128]{1,0:T(8,128)(2,1)} %x0.1), channel_id=1, source_target_pairs={{0,12},{4,8},{8,4},{12,0},{1,13},{5,9},{9,5},{13,1},{2,14},{6,10},... | collective-permute-start | bytes 196616 | tf_op jit(solution)/shard_map/ppermute | solution.py:278
  7.0 13.4 %copy-start.2 = (bf16[128,256]{1,0:T(8,128)(2,1)S(1)}, bf16[128,256]{1,0:T(8,128)(2,1)}, u32[]{:S(2)}) copy-start(bf16[128,256]{1,0:T(8,128)(2,1)} %weight_ref.1) | copy-start | bytes 196612
  7.0 13.4 %copy-start.3 = (f32[256]{0:T(256)S(1)}, f32[256]{0:T(256)}, u32[]{:S(2)}) copy-start(f32[256]{0:T(256)} %param.14) | copy-start | bytes 3076
  9.7 5.0 %collective-permute-start.4 = (bf16[256,256]{1,0:T(8,128)(2,1)S(1)}, bf16[256,256]{1,0:T(8,128)(2,1)S(1)}, u32[]{:S(2)}, u32[]{:S(2)}) collective-permute-start(bf16[256,256]{1,0:T(8,128)(2,1)S(1)} %copy-done), channel_id=1, source_target_pairs={{0,2},{1,3},{2,0},{3,1},{4,6},{5,7},{6,4},{7,5},{8,10},{9,11},{10,... | collective-permute-start | bytes 393224 | tf_op jit(solution)/shard_map/ppermute | solution.py:278
  13.3 1.4 %collective-permute-start.3 = (bf16[512,128]{1,0:T(8,128)(2,1)S(1)}, bf16[512,128]{1,0:T(8,128)(2,1)S(1)}, u32[]{:S(2)}, u32[]{:S(2)}) collective-permute-start(bf16[512,128]{1,0:T(8,128)(2,1)S(1)} %get-tuple-element.22), channel_id=1, source_target_pairs={{0,1},{1,0},{2,3},{3,2},{4,5},{5,4},{6,7},{7,6},{8,9},{9,8},{10,11... | collective-permute-start | bytes 393224 | tf_op jit(solution)/shard_map/ppermute | solution.py:278
  14.8 5.6 %collective-permute-start.5 = (bf16[512,128]{1,0:T(8,128)(2,1)S(1)}, bf16[512,128]{1,0:T(8,128)(2,1)S(1)}, u32[]{:S(2)}, u32[]{:S(2)}) collective-permute-start(bf16[512,128]{1,0:T(8,128)(2,1)S(1)} %add_convert_fusion.near_ref), channel_id=1, source_target_pairs={{0,2},{1,3},{2,0},{3,1},{4,6},{5,7},{6,4},{7,5},{8,10},{9,11},{10,... | collective-permute-start | bytes 393224 | tf_op jit(solution)/shard_map/ppermute | solution.py:278
  21.5 1.4 %collective-permute-start.6 = (bf16[784,128]{1,0:T(8,128)(2,1)S(1)}, bf16[784,128]{1,0:T(8,128)(2,1)S(1)}, u32[]{:S(2)}, u32[]{:S(2)}) collective-permute-start(bf16[784,128]{1,0:T(8,128)(2,1)S(1)} %get-tuple-element.27.own_ref), channel_id=1, source_target_pairs={{0,1},{1,0},{2,3},{3,2},{4,5},{5,4},{6,7},{7,6},{8,9},{9,8},{10,11... | collective-permute-start | bytes 602120 | tf_op jit(solution)/shard_map/ppermute | solution.py:278
  23.5 7.1 %collective-permute-start.7 = (bf16[528,128]{1,0:T(8,128)(2,1)S(1)}, bf16[528,128]{1,0:T(8,128)(2,1)S(1)}, u32[]{:S(2)}, u32[]{:S(2)}) collective-permute-start(bf16[528,128]{1,0:T(8,128)(2,1)S(1)} %get-tuple-element.28), channel_id=1, source_target_pairs={{0,4},{4,0},{8,12},{12,8},{1,5},{5,1},{9,13},{13,9},{2,6},{6,2},{1... | collective-permute-start | bytes 405512 | tf_op jit(solution)/shard_map/ppermute | solution.py:278
  23.9 8.7 %collective-permute-start.9 = (bf16[256,128]{1,0:T(8,128)(2,1)S(1)}, bf16[256,128]{1,0:T(8,128)(2,1)S(1)}, u32[]{:S(2)}, u32[]{:S(2)}) collective-permute-start(bf16[256,128]{1,0:T(8,128)(2,1)S(1)} %get-tuple-element.32), channel_id=1, source_target_pairs={{0,8},{4,12},{8,0},{12,4},{1,9},{5,13},{9,1},{13,5},{2,10},{6,14},... | collective-permute-start | bytes 196616 | tf_op jit(solution)/shard_map/ppermute | solution.py:278
  27.4 6.2 %collective-permute-start.10 = (bf16[256,128]{1,0:T(8,128)(2,1)S(1)}, bf16[256,128]{1,0:T(8,128)(2,1)S(1)}, u32[]{:S(2)}, u32[]{:S(2)}) collective-permute-start(bf16[256,128]{1,0:T(8,128)(2,1)S(1)} %get-tuple-element.33), channel_id=1, source_target_pairs={{0,12},{4,8},{8,4},{12,0},{1,13},{5,9},{9,5},{13,1},{2,14},{6,10},... | collective-permute-start | bytes 196616 | tf_op jit(solution)/shard_map/ppermute | solution.py:278
  30.6 5.5 %collective-permute-start.8 = (bf16[272,128]{1,0:T(8,128)(2,1)S(1)}, bf16[272,128]{1,0:T(8,128)(2,1)S(1)}, u32[]{:S(2)}, u32[]{:S(2)}) collective-permute-start(bf16[272,128]{1,0:T(8,128)(2,1)S(1)} %add_convert_fusion.1.near_ref), channel_id=1, source_target_pairs={{0,8},{4,12},{8,0},{12,4},{1,9},{5,13},{9,1},{13,5},{2,10},{6,14},... | collective-permute-start | bytes 208904 | tf_op jit(solution)/shard_map/ppermute | solution.py:278

commit v4 on v3

--- a/solution.py
+++ b/solution.py
@@ -168,17 +168,17 @@
     )(count.reshape(1, 1), *in_hbm)
 
 
-def forward_kernel(tile_ref, x0, x1, x2, x3, send_ref, keep_ref):
+def forward_kernel(tile_ref, outer_ref, x1, x2, send_ref, keep_ref):
     row = lax.axis_index("row")
     core = lax.rem(lax.axis_index("col"), 2)
-    rows = x0.shape[0]
+    rows = x1.shape[0]
 
     def part(block):
         total = None
-        for k, x in enumerate((x0, x1, x2, x3)):
+        for k, shard in ((0, outer_ref[:rows, :]), (3, outer_ref[rows:, :]), (1, x1[...]), (2, x2[...])):
             col_at = pl.multiple_of(jnp.bitwise_xor(row, k) * rows, rows)
             tile = tile_ref[pl.ds(pl.multiple_of(block * rows, rows), rows), pl.ds(col_at, rows)]
-            term = jnp.dot(tile, x[...], preferred_element_type=F32)
+            term = jnp.dot(tile, shard, preferred_element_type=F32)
             total = term if total is None else total + term
         return total
 
@@ -261,6 +261,10 @@
     ).astype(BF16)
 
 
+def write_kernel(source_ref, out_ref):
+    out_ref[...] = source_ref[...]
+
+
 def finish_kernel(scale, near_ref, far_ref, gw_ref, gb_ref):
     width_in, hid = gw_ref.shape
     for j in range(hid // width_in):
@@ -286,19 +290,19 @@
     row_blocks = COLS * node_rows // block_size
     col_blocks = ROWS * node_rows // block_size
     extra = hid + BIAS_ROWS
-    shards = [features] + [swap(features, "row", k) for k in (1, 2, 3)]
+    shards = [swap(features, "row", k) for k in (1, 2)]
+    outer = jnp.concatenate([features, swap(features, "row", 3)])
     tile = densify(block_values, block_rows, block_cols, block_count, row_blocks, col_blocks)
-    tile, shards[1], cotangent = lax.optimization_barrier((tile, shards[1], cotangent))
     cot_far = swap(cotangent, "col", 2)
     half = (2 * node_rows, width_in)
     send, keep = pl.pallas_call(
         forward_kernel,
-        in_specs=[WHOLE] * 5,
+        in_specs=[WHOLE] * 4,
         out_specs=[WHOLE] * 2,
         out_shape=[jax.ShapeDtypeStruct(half, BF16), jax.ShapeDtypeStruct(half, F32)],
         compiler_params=LIMIT,
         name="forward",
-    )(tile, *shards)
+    )(tile, outer, *shards)
     sib, cot_far = lax.optimization_barrier((swap(send, "col", 1), cot_far))
     near = (keep + sib.astype(F32)).astype(BF16)
     far = swap(near, "col", 2)
@@ -307,7 +311,7 @@
         in_specs=[WHOLE] * 6,
         out_specs=[WHOLE] * 2,
         out_shape=[
-            jax.ShapeDtypeStruct((node_rows, hid), BF16),
+            pltpu.VMEM((node_rows, hid), BF16),
             jax.ShapeDtypeStruct((2 * node_rows + extra, width_in), BF16),
         ],
         compiler_params=LIMIT,
@@ -342,6 +346,15 @@
     grad_features = (
         own + got[0][:node_rows].astype(F32) + got[1].astype(F32) + got[2].astype(F32)
     ).astype(BF16)
+    grad_features, hidden = lax.optimization_barrier((grad_features, hidden))
+    hidden = pl.pallas_call(
+        write_kernel,
+        in_specs=[WHOLE],
+        out_specs=WHOLE,
+        out_shape=jax.ShapeDtypeStruct(hidden.shape, BF16),
+        compiler_params=LIMIT,
+        name="write_hidden",
+    )(hidden)
     norm_scale = float(node_rows * ROWS * COLS) ** (-0.5)
     grad_weight, grad_bias = pl.pallas_call(
         functools.partial(finish_kernel, norm_scale),

time: 36.9 us -> 35.9 us (0.973)
  waiting for transfers between devices: 12.7 us -> 11.4 us
    ppermute x11, waiting for transfers between devices: 12.7 us -> 11.4 us  [swap(): return lax.ppermute(array, axis, [(i, i ^ bit) for i in range(size)])]
    pallas_call x1 -> x2, Pallas kernels: 0.7 us -> 1.36 us  [the longest x1 0.7 us: dense_tile(): pl.pallas_call(forward_kernel, in_specs=[WHOLE] * 4, out_specs=[WHOLE] *...]
    pallas_call x1, Pallas kernels: 1.11 us -> 0.72 us  [dense_tile(): pl.pallas_call(layer_kernel, in_specs=[WHOLE] * 6, out_specs=[WHOLE] * 2,...]
  transfers between devices with their start and end apart: 11 -> 11, of which waited for: 7 -> 7; matrix products, arithmetic and copies ran while one was open for 2% -> 2% of each run, Pallas kernels for 11% -> 13%
where the time goes in v4:
time: 35.9 us; the launch traced here: 35.7 us
  starting transfers between devices  15.6 us (43%)
  waiting for transfers between devices  11.4 us (32%)
  Pallas kernels  6.54 us (18%)
  between operations  1.42 us (4%)
  other arithmetic  0.73 us (2%)
    ppermute x11, starting transfers between devices, swap(): return lax.ppermute(array, axis, [(i, i ^ bit) for i in range(size)])  15.6 us
    ppermute x11, waiting for transfers between devices, swap(): return lax.ppermute(array, axis, [(i, i ^ bit) for i in range(size)])  11.4 us
    pallas_call x1, Pallas kernels, densify(): pl.pallas_call(functools.partial(densify_kernel, chunks, row_blocks, col_...  2.72 us
    pallas_call x1, Pallas kernels, dense_tile(): pl.pallas_call(layer_kernel, in_specs=[WHOLE] * 6, out_specs=[WHOLE] * 2,...  0.72 us
  transfers between devices with their start and end apart: 11, of which 7 were waited for; matrix products, arithmetic and copies ran while one was open for 2% of the time, Pallas kernels for 13%

profile of v4, /device:TPU:0, one launch (start us, length us, event | category | flops | bytes accessed | tf_op | source)
XLA Modules:
  0.0 35.7 jit_solution(8020517042961098070)
XLA Ops:
  0.6 0.0 copy-start.3
  0.6 5.1 %collective-permute-start = (bf16[256,128]{1,0:T(8,128)(2,1)}, bf16[256,128]{1,0:T(8,128)(2,1)S(1)}, u32[]{:S(2)}, u32[]{:S(2)}) collective-permute-start(bf16[256,128]{1,0:T(8,128)(2,1)} %param.8), channel_id=1, source_target_pairs={{0,12},{4,8},{8,4},{12,0},{1,13},{5,9},{9,5},{13,1},{2,14},{6,10},... | collective-permute-start | bytes 196616 | tf_op jit(solution)/shard_map/ppermute | solution.py:282
  5.8 0.0 collective-permute-start.2
  5.8 0.6 %collective-permute-start.1 = (bf16[256,128]{1,0:T(8,128)(2,1)}, bf16[256,128]{1,0:T(8,128)(2,1)S(1)}, u32[]{:S(2)}, u32[]{:S(2)}) collective-permute-start(bf16[256,128]{1,0:T(8,128)(2,1)} %param.8), channel_id=1, source_target_pairs={{0,4},{4,0},{8,12},{12,8},{1,5},{5,1},{9,13},{13,9},{2,6},{6,2},{1... | collective-permute-start | bytes 196616 | tf_op jit(solution)/shard_map/ppermute | solution.py:282
  6.4 1.6 %collective-permute-start.4 = (bf16[256,256]{1,0:T(8,128)(2,1)}, bf16[256,256]{1,0:T(8,128)(2,1)S(1)}, u32[]{:S(2)}, u32[]{:S(2)}) collective-permute-start(bf16[256,256]{1,0:T(8,128)(2,1)} %cot_ref.1), channel_id=1, source_target_pairs={{0,2},{1,3},{2,0},{3,1},{4,6},{5,7},{6,4},{7,5},{8,10},{9,11},{10,... | collective-permute-start | bytes 393224 | tf_op jit(solution)/shard_map/ppermute | solution.py:282
  8.7 2.7 %densify.1.tile_ref = bf16[1024,1024]{1,0:T(8,128)(2,1)S(1)} custom-call(s32[1,1]{1,0:T(1,128)} %bitcast.3.count_in, s32[128]{0:T(128)} %rows_in.1, s32[128]{0:T(128)} %cols_in.1, bf16[128,128,128]{2,1,0:T(8,128)(2,1)} %values_ref.1), custom_call_target="tpu_custom_call" | custom-call | flops 2097152 | bytes 4194304 | tf_op jit(solution)/shard_map/densify/pallas_call | solution.py:151
  11.4 0.0 collective-permute-done
  11.5 0.1 collective-permute-done.2.x2
  11.6 0.0 collective-permute-done.1.x1
  11.6 0.7 %forward.1 = (bf16[512,128]{1,0:T(8,128)(2,1)S(1)}, f32[512,128]{1,0:T(8,128)S(1)}) custom-call(bf16[1024,1024]{1,0:T(8,128)(2,1)S(1)} %densify.1.tile_ref, bf16[512,128]{1,0:T(8,128)(2,1)S(1)} %pad_maximum_fusion.outer_ref, bf16[256,128]{1,0:T(8,128)(2,1)S(1)} %collective-permute-done.1.x1, bf16[256,128]{1,0:T(8,128)(2,1)S(1)} %collective-permute-done.2.x2), custom_call_target="tpu_custom_call" | custom-call | tf_op jit(solution)/shard_map/forward/pallas_call | solution.py:298
  12.3 0.1 collective-permute-start.3
  12.4 0.0 collective-permute-done.4.cot_far_ref
  12.4 1.3 %collective-permute-done.3 = bf16[512,128]{1,0:T(8,128)(2,1)S(1)} collective-permute-done((bf16[512,128]{1,0:T(8,128)(2,1)S(1)}, bf16[512,128]{1,0:T(8,128)(2,1)S(1)}, u32[]{:S(2)}, u32[]{:S(2)}) %collective-permute-start.3) | collective-permute-done | bytes 131104 | tf_op jit(solution)/shard_map/ppermute | solution.py:282
  13.7 1.6 %collective-permute-start.5 = (bf16[512,128]{1,0:T(8,128)(2,1)S(1)}, bf16[512,128]{1,0:T(8,128)(2,1)S(1)}, u32[]{:S(2)}, u32[]{:S(2)}) collective-permute-start(bf16[512,128]{1,0:T(8,128)(2,1)S(1)} %add_convert_fusion.near_ref), channel_id=1, source_target_pairs={{0,2},{1,3},{2,0},{3,1},{4,6},{5,7},{6,4},{7,5},{8,10},{9,11},{10,... | collective-permute-start | bytes 393224 | tf_op jit(solution)/shard_map/ppermute | solution.py:282
  15.3 4.1 %collective-permute-done.5.far_ref = bf16[512,128]{1,0:T(8,128)(2,1)S(1)} collective-permute-done((bf16[512,128]{1,0:T(8,128)(2,1)S(1)}, bf16[512,128]{1,0:T(8,128)(2,1)S(1)}, u32[]{:S(2)}, u32[]{:S(2)}) %collective-permute-start.5) | collective-permute-done | bytes 131104 | tf_op jit(solution)/shard_map/ppermute | solution.py:282
  19.3 0.0 copy-done
  19.4 0.7 %layer.1 = (bf16[256,256]{1,0:T(8,128)(2,1)S(1)}, bf16[784,128]{1,0:T(8,128)(2,1)S(1)}) custom-call(bf16[512,128]{1,0:T(8,128)(2,1)S(1)} %add_convert_fusion.near_ref, bf16[512,128]{1,0:T(8,128)(2,1)S(1)} %collective-permute-done.5.far_ref, bf16[256,256]{1,0:T(8,128)(2,1)S(1)} %copy-done, bf16[256,256]{1,0:T(8,128)(2,1)S(1)} %collective-permute-done.4.cot_far_ref, ...), custom_call_target="tpu_custom_call" | custom-call | tf_op jit(solution)/shard_map/layer/pallas_call | solution.py:309
  20.1 0.1 collective-permute-start.6
  20.2 0.5 %backward_mine.1.part_ref = f32[4,256,128]{2,1,0:T(8,128)S(1)} custom-call(bf16[1024,1024]{1,0:T(8,128)(2,1)S(1)} %densify.1.tile_ref, bf16[784,128]{1,0:T(8,128)(2,1)S(1)} %get-tuple-element.22.own_ref), custom_call_target="tpu_custom_call" | custom-call | flops 134217728 | bytes 1048576 | tf_op jit(solution)/shard_map/backward_mine/pallas_call | solution.py:321
  20.7 0.9 %collective-permute-done.6.sib_ref = bf16[784,128]{1,0:T(8,128)(2,1)S(1)} collective-permute-done((bf16[784,128]{1,0:T(8,128)(2,1)S(1)}, bf16[784,128]{1,0:T(8,128)(2,1)S(1)}, u32[]{:S(2)}, u32[]{:S(2)}) %collective-permute-start.6) | collective-permute-done | bytes 200736 | tf_op jit(solution)/shard_map/ppermute | solution.py:282
  21.6 0.5 %backward.1 = (f32[256,128]{1,0:T(8,128)S(1)}, bf16[528,128]{1,0:T(8,128)(2,1)S(1)}, bf16[256,128]{1,0:T(8,128)(2,1)S(1)}, bf16[256,128]{1,0:T(8,128)(2,1)S(1)}) custom-call(bf16[1024,1024]{1,0:T(8,128)(2,1)S(1)} %densify.1.tile_ref, bf16[784,128]{1,0:T(8,128)(2,1)S(1)} %get-tuple-element.22.own_ref, bf16[784,128]{1,0:T(8,128)(2,1)S(1)} %collective-permute-done.6.sib_ref, ...), custom_call_target="tpu_custom_call" | custom-call | tf_op jit(solution)/shard_map/backward/pallas_call | solution.py:330
  22.1 1.3 %collective-permute-start.7 = (bf16[528,128]{1,0:T(8,128)(2,1)S(1)}, bf16[528,128]{1,0:T(8,128)(2,1)S(1)}, u32[]{:S(2)}, u32[]{:S(2)}) collective-permute-start(bf16[528,128]{1,0:T(8,128)(2,1)S(1)} %get-tuple-element.24), channel_id=1, source_target_pairs={{0,4},{4,0},{8,12},{12,8},{1,5},{5,1},{9,13},{13,9},{2,6},{6,2},{1... | collective-permute-start | bytes 405512 | tf_op jit(solution)/shard_map/ppermute | solution.py:282
  23.4 2.9 %collective-permute-start.8 = (bf16[256,128]{1,0:T(8,128)(2,1)S(1)}, bf16[256,128]{1,0:T(8,128)(2,1)S(1)}, u32[]{:S(2)}, u32[]{:S(2)}) collective-permute-start(bf16[256,128]{1,0:T(8,128)(2,1)S(1)} %get-tuple-element.25), channel_id=1, source_target_pairs={{0,8},{4,12},{8,0},{12,4},{1,9},{5,13},{9,1},{13,5},{2,10},{6,14},... | collective-permute-start | bytes 196616 | tf_op jit(solution)/shard_map/ppermute | solution.py:282
  26.3 0.3 collective-permute-start.9
  26.6 2.6 %collective-permute-done.7 = bf16[528,128]{1,0:T(8,128)(2,1)S(1)} collective-permute-done((bf16[528,128]{1,0:T(8,128)(2,1)S(1)}, bf16[528,128]{1,0:T(8,128)(2,1)S(1)}, u32[]{:S(2)}, u32[]{:S(2)}) %collective-permute-start.7) | collective-permute-done | bytes 135200 | tf_op jit(solution)/shard_map/ppermute | solution.py:282
  29.3 2.1 %collective-permute-start.10 = (bf16[272,128]{1,0:T(8,128)(2,1)S(1)}, bf16[272,128]{1,0:T(8,128)(2,1)S(1)}, u32[]{:S(2)}, u32[]{:S(2)}) collective-permute-start(bf16[272,128]{1,0:T(8,128)(2,1)S(1)} %add_convert_fusion.1.near_ref), channel_id=1, source_target_pairs={{0,8},{4,12},{8,0},{12,4},{1,9},{5,13},{9,1},{13,5},{2,10},{6,14},... | collective-permute-start | bytes 208904 | tf_op jit(solution)/shard_map/ppermute | solution.py:282
  31.3 0.0 collective-permute-done.8
  31.3 1.2 %collective-permute-done.9 = bf16[256,128]{1,0:T(8,128)(2,1)S(1)} collective-permute-done((bf16[256,128]{1,0:T(8,128)(2,1)S(1)}, bf16[256,128]{1,0:T(8,128)(2,1)S(1)}, u32[]{:S(2)}, u32[]{:S(2)}) %collective-permute-start.9) | collective-permute-done | bytes 65568 | tf_op jit(solution)/shard_map/ppermute | solution.py:282
  32.5 0.7 %add_convert_fusion.2 = bf16[256,128]{1,0:T(8,128)(2,1)} fusion(bf16[256,128]{1,0:T(8,128)(2,1)S(1)} %collective-permute-done.9, bf16[256,128]{1,0:T(8,128)(2,1)S(1)} %collective-permute-done.8, f32[256,128]{1,0:T(8,128)S(1)} %get-tuple-element.23, bf16[528,128]{1,0:T(8,128)(2,1)S(1)} %collective-permute-done.7), kind=kLoop, calls=%fused_computation.3 | loop fusion | flops 229376 | bytes 393216 | tf_op jit(solution)/shard_map/convert_element_type | solution.py:348
  33.2 0.7 %write_hidden.1 = bf16[256,256]{1,0:T(8,128)(2,1)} custom-call(bf16[256,256]{1,0:T(8,128)(2,1)S(1)} %get-tuple-element.28.source_ref), custom_call_target="tpu_custom_call" | custom-call | tf_op jit(solution)/shard_map/write_hidden/pallas_call | solution.py:350
  33.9 1.1 %collective-permute-done.10.far_ref = bf16[272,128]{1,0:T(8,128)(2,1)S(1)} collective-permute-done((bf16[272,128]{1,0:T(8,128)(2,1)S(1)}, bf16[272,128]{1,0:T(8,128)(2,1)S(1)}, u32[]{:S(2)}, u32[]{:S(2)}) %collective-permute-start.10) | collective-permute-done | bytes 69664 | tf_op jit(solution)/shard_map/ppermute | solution.py:282
  35.0 0.7 %finish.1 = (f32[128,256]{1,0:T(8,128)}, f32[1,256]{1,0:T(1,128)}) custom-call(bf16[272,128]{1,0:T(8,128)(2,1)S(1)} %add_convert_fusion.1.near_ref, bf16[272,128]{1,0:T(8,128)(2,1)S(1)} %collective-permute-done.10.far_ref), custom_call_target="tpu_custom_call" | custom-call | tf_op jit(solution)/shard_map/finish/pallas_call | solution.py:359
  (9 shorter events, 0.1 us)
Async XLA Ops:
  0.6 10.8 %copy-start.3 = (bf16[256,128]{1,0:T(8,128)(2,1)S(1)}, bf16[256,128]{1,0:T(8,128)(2,1)}, u32[]{:S(2)}) copy-start(bf16[256,128]{1,0:T(8,128)(2,1)} %param.8) | copy-start | bytes 196612
  0.6 10.8 %collective-permute-start = (bf16[256,128]{1,0:T(8,128)(2,1)}, bf16[256,128]{1,0:T(8,128)(2,1)S(1)}, u32[]{:S(2)}, u32[]{:S(2)}) collective-permute-start(bf16[256,128]{1,0:T(8,128)(2,1)} %param.8), channel_id=1, source_target_pairs={{0,12},{4,8},{8,4},{12,0},{1,13},{5,9},{9,5},{13,1},{2,14},{6,10},... | collective-permute-start | bytes 196616 | tf_op jit(solution)/shard_map/ppermute | solution.py:282
  5.8 5.8 %collective-permute-start.2 = (bf16[256,128]{1,0:T(8,128)(2,1)}, bf16[256,128]{1,0:T(8,128)(2,1)S(1)}, u32[]{:S(2)}, u32[]{:S(2)}) collective-permute-start(bf16[256,128]{1,0:T(8,128)(2,1)} %param.8), channel_id=1, source_target_pairs={{0,8},{4,12},{8,0},{12,4},{1,9},{5,13},{9,1},{13,5},{2,10},{6,14},... | collective-permute-start | bytes 196616 | tf_op jit(solution)/shard_map/ppermute | solution.py:282
  5.8 5.8 %collective-permute-start.1 = (bf16[256,128]{1,0:T(8,128)(2,1)}, bf16[256,128]{1,0:T(8,128)(2,1)S(1)}, u32[]{:S(2)}, u32[]{:S(2)}) collective-permute-start(bf16[256,128]{1,0:T(8,128)(2,1)} %param.8), channel_id=1, source_target_pairs={{0,4},{4,0},{8,12},{12,8},{1,5},{5,1},{9,13},{13,9},{2,6},{6,2},{1... | collective-permute-start | bytes 196616 | tf_op jit(solution)/shard_map/ppermute | solution.py:282
  6.4 6.0 %collective-permute-start.4 = (bf16[256,256]{1,0:T(8,128)(2,1)}, bf16[256,256]{1,0:T(8,128)(2,1)S(1)}, u32[]{:S(2)}, u32[]{:S(2)}) collective-permute-start(bf16[256,256]{1,0:T(8,128)(2,1)} %cot_ref.1), channel_id=1, source_target_pairs={{0,2},{1,3},{2,0},{3,1},{4,6},{5,7},{6,4},{7,5},{8,10},{9,11},{10,... | collective-permute-start | bytes 393224 | tf_op jit(solution)/shard_map/ppermute | solution.py:282
  8.7 10.7 %copy-start = (bf16[256,256]{1,0:T(8,128)(2,1)S(1)}, bf16[256,256]{1,0:T(8,128)(2,1)}, u32[]{:S(2)}) copy-start(bf16[256,256]{1,0:T(8,128)(2,1)} %cot_ref.1) | copy-start | bytes 393220
  8.7 10.7 %copy-start.1 = (bf16[128,256]{1,0:T(8,128)(2,1)S(1)}, bf16[128,256]{1,0:T(8,128)(2,1)}, u32[]{:S(2)}) copy-start(bf16[128,256]{1,0:T(8,128)(2,1)} %weight_ref.1) | copy-start | bytes 196612
  8.7 10.6 %copy-start.2 = (f32[256]{0:T(256)S(1)}, f32[256]{0:T(256)}, u32[]{:S(2)}) copy-start(f32[256]{0:T(256)} %param.14) | copy-start | bytes 3076
  12.3 1.4 %collective-permute-start.3 = (bf16[512,128]{1,0:T(8,128)(2,1)S(1)}, bf16[512,128]{1,0:T(8,128)(2,1)S(1)}, u32[]{:S(2)}, u32[]{:S(2)}) collective-permute-start(bf16[512,128]{1,0:T(8,128)(2,1)S(1)} %get-tuple-element.19), channel_id=1, source_target_pairs={{0,1},{1,0},{2,3},{3,2},{4,5},{5,4},{6,7},{7,6},{8,9},{9,8},{10,11... | collective-permute-start | bytes 393224 | tf_op jit(solution)/shard_map/ppermute | solution.py:282
  13.7 5.6 %collective-permute-start.5 = (bf16[512,128]{1,0:T(8,128)(2,1)S(1)}, bf16[512,128]{1,0:T(8,128)(2,1)S(1)}, u32[]{:S(2)}, u32[]{:S(2)}) collective-permute-start(bf16[512,128]{1,0:T(8,128)(2,1)S(1)} %add_convert_fusion.near_ref), channel_id=1, source_target_pairs={{0,2},{1,3},{2,0},{3,1},{4,6},{5,7},{6,4},{7,5},{8,10},{9,11},{10,... | collective-permute-start | bytes 393224 | tf_op jit(solution)/shard_map/ppermute | solution.py:282
  20.1 1.5 %collective-permute-start.6 = (bf16[784,128]{1,0:T(8,128)(2,1)S(1)}, bf16[784,128]{1,0:T(8,128)(2,1)S(1)}, u32[]{:S(2)}, u32[]{:S(2)}) collective-permute-start(bf16[784,128]{1,0:T(8,128)(2,1)S(1)} %get-tuple-element.22.own_ref), channel_id=1, source_target_pairs={{0,1},{1,0},{2,3},{3,2},{4,5},{5,4},{6,7},{7,6},{8,9},{9,8},{10,11... | collective-permute-start | bytes 602120 | tf_op jit(solution)/shard_map/ppermute | solution.py:282
  22.1 7.1 %collective-permute-start.7 = (bf16[528,128]{1,0:T(8,128)(2,1)S(1)}, bf16[528,128]{1,0:T(8,128)(2,1)S(1)}, u32[]{:S(2)}, u32[]{:S(2)}) collective-permute-start(bf16[528,128]{1,0:T(8,128)(2,1)S(1)} %get-tuple-element.24), channel_id=1, source_target_pairs={{0,4},{4,0},{8,12},{12,8},{1,5},{5,1},{9,13},{13,9},{2,6},{6,2},{1... | collective-permute-start | bytes 405512 | tf_op jit(solution)/shard_map/ppermute | solution.py:282
  23.4 7.9 %collective-permute-start.8 = (bf16[256,128]{1,0:T(8,128)(2,1)S(1)}, bf16[256,128]{1,0:T(8,128)(2,1)S(1)}, u32[]{:S(2)}, u32[]{:S(2)}) collective-permute-start(bf16[256,128]{1,0:T(8,128)(2,1)S(1)} %get-tuple-element.25), channel_id=1, source_target_pairs={{0,8},{4,12},{8,0},{12,4},{1,9},{5,13},{9,1},{13,5},{2,10},{6,14},... | collective-permute-start | bytes 196616 | tf_op jit(solution)/shard_map/ppermute | solution.py:282
  26.3 6.2 %collective-permute-start.9 = (bf16[256,128]{1,0:T(8,128)(2,1)S(1)}, bf16[256,128]{1,0:T(8,128)(2,1)S(1)}, u32[]{:S(2)}, u32[]{:S(2)}) collective-permute-start(bf16[256,128]{1,0:T(8,128)(2,1)S(1)} %get-tuple-element.26), channel_id=1, source_target_pairs={{0,12},{4,8},{8,4},{12,0},{1,13},{5,9},{9,5},{13,1},{2,14},{6,10},... | collective-permute-start | bytes 196616 | tf_op jit(solution)/shard_map/ppermute | solution.py:282
  29.3 5.8 %collective-permute-start.10 = (bf16[272,128]{1,0:T(8,128)(2,1)S(1)}, bf16[272,128]{1,0:T(8,128)(2,1)S(1)}, u32[]{:S(2)}, u32[]{:S(2)}) collective-permute-start(bf16[272,128]{1,0:T(8,128)(2,1)S(1)} %add_convert_fusion.1.near_ref), channel_id=1, source_target_pairs={{0,8},{4,12},{8,0},{12,4},{1,9},{5,13},{9,1},{13,5},{2,10},{6,14},... | collective-permute-start | bytes 208904 | tf_op jit(solution)/shard_map/ppermute | solution.py:282

commit v5 on v3

--- a/solution.py
+++ b/solution.py
@@ -15,7 +15,7 @@
 SCALARS = pl.BlockSpec(memory_space=pltpu.SMEM)
 LIMIT = pltpu.CompilerParams(vmem_limit_bytes=16 * 2**20)
 BIAS_ROWS = 16
-GROUP = 4
+GROUP = 8
 
 
 def pick_rows(pick_index, live_mask, source_rows):
@@ -168,27 +168,36 @@
     )(count.reshape(1, 1), *in_hbm)
 
 
-def forward_kernel(tile_ref, x0, x1, x2, x3, send_ref, keep_ref):
+def forward_kernel(mine, tile_ref, outer_ref, x1, x2, out_ref):
     row = lax.axis_index("row")
     core = lax.rem(lax.axis_index("col"), 2)
-    rows = x0.shape[0]
-
-    def part(block):
+    half = core if mine else 1 - core
+    rows = x1.shape[0]
+    for x in range(2):
+        row_at = pl.multiple_of((2 * x + half) * rows, rows)
         total = None
-        for k, x in enumerate((x0, x1, x2, x3)):
+        for k, shard in ((0, outer_ref[:rows, :]), (3, outer_ref[rows:, :]), (1, x1[...]), (2, x2[...])):
             col_at = pl.multiple_of(jnp.bitwise_xor(row, k) * rows, rows)
-            tile = tile_ref[pl.ds(pl.multiple_of(block * rows, rows), rows), pl.ds(col_at, rows)]
-            term = jnp.dot(tile, x[...], preferred_element_type=F32)
+            tile = tile_ref[pl.ds(row_at, rows), pl.ds(col_at, rows)]
+            term = jnp.dot(tile, shard, preferred_element_type=F32)
             total = term if total is None else total + term
-        return total
-
-    for x in range(2):
-        send_ref[pl.ds(x * rows, rows), :] = part(2 * x + 1 - core).astype(BF16)
-    for x in range(2):
-        keep_ref[pl.ds(x * rows, rows), :] = part(2 * x + core)
-
-
-def layer_kernel(near_ref, far_ref, cot_ref, cot_far_ref, weight_ref, bias_ref, hidden_ref, swap_ref):
+        out_ref[pl.ds(x * rows, rows), :] = total.astype(out_ref.dtype)
+
+
+def forward(mine, tile, outer, shards):
+    rows, width_in = shards[0].shape
+    return pl.pallas_call(
+        functools.partial(forward_kernel, mine),
+        in_specs=[WHOLE] * 4,
+        out_specs=WHOLE,
+        out_shape=jax.ShapeDtypeStruct((2 * rows, width_in), F32 if mine else BF16),
+        compiler_params=LIMIT,
+        cost_estimate=pl.CostEstimate(flops=tile.size * width_in, bytes_accessed=tile.size, transcendentals=0),
+        name="forward_mine" if mine else "forward_sibling",
+    )(tile, outer, *shards)
+
+
+def layer_kernel(near_ref, far_ref, cot_ref, cot_far_ref, weight_ref, bias_ref, act_ref, swap_ref):
     mine = lax.rem(lax.axis_index("col") // 2, 2)
     rows, hid = cot_ref.shape
     width_in = near_ref.shape[1]
@@ -203,7 +212,7 @@
 
         @pl.when(mine == x)
         def _():
-            hidden_ref[...] = (pre_act * sigmoid_pre).astype(BF16)
+            act_ref[...] = pre_act
 
         cot = jnp.where(mine == x, cot_ref[...], cot_far_ref[...]).astype(F32)
         pre_grad = (cot * sigmoid_pre * (1.0 + pre_act * (1.0 - sigmoid_pre))).astype(BF16)
@@ -254,23 +263,37 @@
     rows = keep_ref.shape[0]
     for k, out in ((1, send1), (2, send2), (3, send3), (0, keep_ref)):
         total = part_ref[k] + backward_terms(tile_ref, 1 - core, k, sib_ref, rows)
-        out[pl.ds(0, rows), :] = total.astype(out.dtype)
-    extra = pl.ds(2 * rows, own_ref.shape[0] - 2 * rows)
-    send1[pl.ds(rows, send1.shape[0] - rows), :] = (
-        own_ref[extra, :].astype(F32) + sib_ref[extra, :].astype(F32)
-    ).astype(BF16)
-
-
-def finish_kernel(scale, near_ref, far_ref, gw_ref, gb_ref):
+        out[...] = total.astype(out.dtype)
+
+
+def stripe_kernel(own_ref, sib_ref, stripe_ref):
+    core = lax.rem(lax.axis_index("col"), 2)
+    width_in = own_ref.shape[1]
+    first = own_ref.shape[0] - BIAS_ROWS - 2 * width_in
+    for source, target, size in (
+        (pl.multiple_of(first + core * width_in, BIAS_ROWS), 0, width_in),
+        (own_ref.shape[0] - BIAS_ROWS, width_in, BIAS_ROWS),
+    ):
+        stripe_ref[pl.ds(target, size), :] = (
+            own_ref[pl.ds(source, size), :].astype(F32) + sib_ref[pl.ds(source, size), :].astype(F32)
+        ).astype(BF16)
+
+
+def last_kernel(scale, keep_ref, got1, got2, got3, pair_ref, pair_far_ref, half_ref, sib_ref,
+                features_ref, gw_ref, gb_ref):
+    core = lax.rem(lax.axis_index("col"), 2)
     width_in, hid = gw_ref.shape
-    for j in range(hid // width_in):
-        lanes = slice(j * width_in, (j + 1) * width_in)
-        block = pl.ds(j * width_in, width_in)
-        gw_ref[:, lanes] = (near_ref[block, :].astype(F32) + far_ref[block, :].astype(F32)) * scale
-    block = pl.ds(hid, BIAS_ROWS)
-    both = (near_ref[block, :].astype(F32) + far_ref[block, :].astype(F32)) * scale
+    half = half_ref[...] * scale
+    sib = sib_ref[...] * scale
+    for j in range(2):
+        gw_ref[:, j * width_in : (j + 1) * width_in] = jnp.where(core == j, half, sib)
+    block = pl.ds(width_in, BIAS_ROWS)
+    both = (pair_ref[block, :].astype(F32) + pair_far_ref[block, :].astype(F32)) * scale
     for j in range(hid // width_in):
         gb_ref[:, j * width_in : (j + 1) * width_in] = both[j : j + 1, :]
+    total = keep_ref[...] + got1[...].astype(F32)
+    total = total + got2[...].astype(F32) + got3[...].astype(F32)
+    features_ref[...] = total.astype(BF16)
 
 
 def swap(array, axis, bit):
@@ -286,28 +309,21 @@
     row_blocks = COLS * node_rows // block_size
     col_blocks = ROWS * node_rows // block_size
     extra = hid + BIAS_ROWS
-    shards = [features] + [swap(features, "row", k) for k in (1, 2, 3)]
+    shards = [swap(features, "row", k) for k in (1, 2)]
+    outer = jnp.concatenate([features, swap(features, "row", 3)])
     tile = densify(block_values, block_rows, block_cols, block_count, row_blocks, col_blocks)
-    tile, shards[1], cotangent = lax.optimization_barrier((tile, shards[1], cotangent))
     cot_far = swap(cotangent, "col", 2)
-    half = (2 * node_rows, width_in)
-    send, keep = pl.pallas_call(
-        forward_kernel,
-        in_specs=[WHOLE] * 5,
-        out_specs=[WHOLE] * 2,
-        out_shape=[jax.ShapeDtypeStruct(half, BF16), jax.ShapeDtypeStruct(half, F32)],
-        compiler_params=LIMIT,
-        name="forward",
-    )(tile, *shards)
+    send = forward(False, tile, outer, shards)
+    keep = forward(True, tile, outer, shards)
     sib, cot_far = lax.optimization_barrier((swap(send, "col", 1), cot_far))
     near = (keep + sib.astype(F32)).astype(BF16)
     far = swap(near, "col", 2)
-    hidden, grads = pl.pallas_call(
+    pre_act, grads = pl.pallas_call(
         layer_kernel,
         in_specs=[WHOLE] * 6,
         out_specs=[WHOLE] * 2,
         out_shape=[
-            jax.ShapeDtypeStruct((node_rows, hid), BF16),
+            pltpu.VMEM((node_rows, hid), F32),
             jax.ShapeDtypeStruct((2 * node_rows + extra, width_in), BF16),
         ],
         compiler_params=LIMIT,
@@ -323,37 +339,46 @@
         cost_estimate=pl.CostEstimate(flops=tile.size * width_in, bytes_accessed=tile.size, transcendentals=0),
         name="backward_mine",
     )(tile, grads)
+    part, grads_sib = lax.optimization_barrier((part, swap(grads, "col", 1)))
+    stripe = pl.pallas_call(
+        stripe_kernel,
+        in_specs=[WHOLE] * 2,
+        out_specs=WHOLE,
+        out_shape=jax.ShapeDtypeStruct((width_in + BIAS_ROWS, width_in), BF16),
+        compiler_params=LIMIT,
+        name="stripe",
+    )(grads, grads_sib)
+    stripe_far = swap(stripe, "row", 1)
     own, *sends = pl.pallas_call(
         backward_kernel,
         in_specs=[WHOLE] * 4,
         out_specs=[WHOLE] * 4,
+        out_shape=[jax.ShapeDtypeStruct(block.shape, F32)] + [block] * 3,
+        compiler_params=LIMIT,
+        name="backward",
+    )(tile, grads, grads_sib, part)
+    pair = (stripe.astype(F32) + stripe_far.astype(F32)).astype(BF16)
+    pair, sends[2] = lax.optimization_barrier((pair, sends[2]))
+    got = [swap(send, "row", k) for k, send in zip((1, 2, 3), sends)]
+    pair, pre_act = lax.optimization_barrier((pair, pre_act))
+    hidden = (pre_act * jax.nn.sigmoid(pre_act)).astype(BF16)
+    pair_far = swap(pair, "row", 2)
+    gw_half = pair[:width_in].astype(F32) + pair_far[:width_in].astype(F32)
+    gw_half, hidden = lax.optimization_barrier((gw_half, hidden))
+    gw_sib = swap(gw_half, "col", 1)
+    norm_scale = float(node_rows * ROWS * COLS) ** (-0.5)
+    grad_features, grad_weight, grad_bias = pl.pallas_call(
+        functools.partial(last_kernel, norm_scale),
+        in_specs=[WHOLE] * 8,
+        out_specs=[WHOLE] * 3,
         out_shape=[
-            jax.ShapeDtypeStruct(block.shape, F32),
-            jax.ShapeDtypeStruct((node_rows + extra, width_in), BF16),
             block,
-            block,
-        ],
-        compiler_params=LIMIT,
-        name="backward",
-    )(tile, grads, swap(grads, "col", 1), part)
-    got = [swap(part, "row", k) for k, part in zip((1, 2, 3), sends)]
-    pair = (sends[0][node_rows:].astype(F32) + got[0][node_rows:].astype(F32)).astype(BF16)
-    pair_far = swap(pair, "row", 2)
-    grad_features = (
-        own + got[0][:node_rows].astype(F32) + got[1].astype(F32) + got[2].astype(F32)
-    ).astype(BF16)
-    norm_scale = float(node_rows * ROWS * COLS) ** (-0.5)
-    grad_weight, grad_bias = pl.pallas_call(
-        functools.partial(finish_kernel, norm_scale),
-        in_specs=[WHOLE] * 2,
-        out_specs=[WHOLE] * 2,
-        out_shape=[
             jax.ShapeDtypeStruct((width_in, hid), F32),
             jax.ShapeDtypeStruct((1, hid), F32),
         ],
         compiler_params=LIMIT,
-        name="finish",
-    )(pair, pair_far)
+        name="last",
+    )(own, *got, pair, pair_far, gw_half, gw_sib)
     return hidden, grad_weight, grad_bias.reshape(hid), grad_features
 
 

time: 36.9 us -> 35.5 us (0.962)
  waiting for transfers between devices: 12.7 us -> 9.17 us
  starting transfers between devices: 15.7 us -> 17.8 us
    ppermute x11 -> x13, waiting for transfers between devices: 12.7 us -> 9.17 us  [swap(): return lax.ppermute(array, axis, [(i, i ^ bit) for i in range(size)])]
    ppermute x11 -> x13, starting transfers between devices: 15.7 us -> 17.8 us  [swap(): return lax.ppermute(array, axis, [(i, i ^ bit) for i in range(size)])]
    pallas_call x1, Pallas kernels: 1.11 us -> 0.7 us  [dense_tile(): pl.pallas_call(layer_kernel, in_specs=[WHOLE] * 6, out_specs=[WHOLE] * 2,...]
    pallas_call x2 -> x4, Pallas kernels: 1.38 us -> 1.58 us  [the longest x2 0.86 us: forward(): pl.pallas_call(functools.partial(forward_kernel, mine), in_specs=[WHOLE]...]
  transfers between devices with their start and end apart: 11 -> 13, of which waited for: 7 -> 6; matrix products, arithmetic and copies ran while one was open for 2% -> 2% of each run, Pallas kernels for 11% -> 13%
where the time goes in v5:
time: 35.5 us; the launch traced here: 35.3 us
  starting transfers between devices  17.8 us (50%)
  waiting for transfers between devices  9.17 us (26%)
  Pallas kernels  6.05 us (17%)
  between operations  1.46 us (4%)
  other arithmetic  0.78 us (2%)
    ppermute x13, starting transfers between devices, swap(): return lax.ppermute(array, axis, [(i, i ^ bit) for i in range(size)])  17.8 us
    ppermute x13, waiting for transfers between devices, swap(): return lax.ppermute(array, axis, [(i, i ^ bit) for i in range(size)])  9.17 us
    pallas_call x1, Pallas kernels, densify(): pl.pallas_call(functools.partial(densify_kernel, chunks, row_blocks, col_...  2.74 us
    pallas_call x2, Pallas kernels, forward(): pl.pallas_call(functools.partial(forward_kernel, mine), in_specs=[WHOLE]...  0.86 us
    convert_element_type x1, other arithmetic, dense_tile(): hidden = (pre_act * jax.nn.sigmoid(pre_act)).astype(BF16)  0.73 us
  transfers between devices with their start and end apart: 13, of which 6 were waited for; matrix products, arithmetic and copies ran while one was open for 2% of the time, Pallas kernels for 13%

profile of v5, /device:TPU:0, one launch (start us, length us, event | category | flops | bytes accessed | tf_op | source)
XLA Modules:
  0.0 35.3 jit_solution(6062921013599676314)
XLA Ops:
  0.6 5.1 %collective-permute-start = (bf16[256,128]{1,0:T(8,128)(2,1)}, bf16[256,128]{1,0:T(8,128)(2,1)S(1)}, u32[]{:S(2)}, u32[]{:S(2)}) collective-permute-start(bf16[256,128]{1,0:T(8,128)(2,1)} %param.8), channel_id=1, source_target_pairs={{0,12},{4,8},{8,4},{12,0},{1,13},{5,9},{9,5},{13,1},{2,14},{6,10},... | collective-permute-start | bytes 196616 | tf_op jit(solution)/shard_map/ppermute | solution.py:301
  5.8 0.6 %collective-permute-start.1 = (bf16[256,128]{1,0:T(8,128)(2,1)}, bf16[256,128]{1,0:T(8,128)(2,1)S(1)}, u32[]{:S(2)}, u32[]{:S(2)}) collective-permute-start(bf16[256,128]{1,0:T(8,128)(2,1)} %param.8), channel_id=1, source_target_pairs={{0,4},{4,0},{8,12},{12,8},{1,5},{5,1},{9,13},{13,9},{2,6},{6,2},{1... | collective-permute-start | bytes 196616 | tf_op jit(solution)/shard_map/ppermute | solution.py:301
  6.4 1.6 %collective-permute-start.4 = (bf16[256,256]{1,0:T(8,128)(2,1)}, bf16[256,256]{1,0:T(8,128)(2,1)S(1)}, u32[]{:S(2)}, u32[]{:S(2)}) collective-permute-start(bf16[256,256]{1,0:T(8,128)(2,1)} %cot_ref.1), channel_id=1, source_target_pairs={{0,2},{1,3},{2,0},{3,1},{4,6},{5,7},{6,4},{7,5},{8,10},{9,11},{10,... | collective-permute-start | bytes 393224 | tf_op jit(solution)/shard_map/ppermute | solution.py:301
  8.7 2.7 %densify.1.tile_ref = bf16[1024,1024]{1,0:T(8,128)(2,1)S(1)} custom-call(s32[1,1]{1,0:T(1,128)} %bitcast.3.count_in, s32[128]{0:T(128)} %rows_in.1, s32[128]{0:T(128)} %cols_in.1, bf16[128,128,128]{2,1,0:T(8,128)(2,1)} %values_ref.1), custom_call_target="tpu_custom_call" | custom-call | flops 2097152 | bytes 4194304 | tf_op jit(solution)/shard_map/densify/pallas_call | solution.py:151
  11.4 0.0 copy-start
  11.5 0.0 copy-start.1
  11.5 0.0 copy-start.2
  11.5 0.0 collective-permute-done
  11.5 0.1 collective-permute-done.2.x2
  11.6 0.0 collective-permute-done.1.x1
  11.6 0.4 %forward_sibling.1 = bf16[512,128]{1,0:T(8,128)(2,1)S(1)} custom-call(bf16[1024,1024]{1,0:T(8,128)(2,1)S(1)} %densify.1.tile_ref, bf16[512,128]{1,0:T(8,128)(2,1)S(1)} %constant_dynamic-update-slice_fusion.outer_ref, bf16[256,128]{1,0:T(8,128)(2,1)S(1)} %collective-permute-done.1.x1, bf16[256,128]{1,0:T(8,128)(2,1)S(1)} %collective-permute-done.2.x2), custom_call_target="tpu_custom_call" | custom-call | flops 134217728 | bytes 1048576 | tf_op jit(solution)/shard_map/forward_sibling/pallas_call | solution.py:189
  12.0 0.1 collective-permute-start.3
  12.1 0.4 %forward_mine.1 = f32[512,128]{1,0:T(8,128)S(1)} custom-call(bf16[1024,1024]{1,0:T(8,128)(2,1)S(1)} %densify.1.tile_ref, bf16[512,128]{1,0:T(8,128)(2,1)S(1)} %constant_dynamic-update-slice_fusion.outer_ref, bf16[256,128]{1,0:T(8,128)(2,1)S(1)} %collective-permute-done.1.x1, bf16[256,128]{1,0:T(8,128)(2,1)S(1)} %collective-permute-done.2.x2), custom_call_target="tpu_custom_call" | custom-call | flops 134217728 | bytes 1048576 | tf_op jit(solution)/shard_map/forward_mine/pallas_call | solution.py:189
  12.5 0.9 %collective-permute-done.3 = bf16[512,128]{1,0:T(8,128)(2,1)S(1)} collective-permute-done((bf16[512,128]{1,0:T(8,128)(2,1)S(1)}, bf16[512,128]{1,0:T(8,128)(2,1)S(1)}, u32[]{:S(2)}, u32[]{:S(2)}) %collective-permute-start.3) | collective-permute-done | bytes 131104 | tf_op jit(solution)/shard_map/ppermute | solution.py:301
  13.5 1.6 %collective-permute-start.5 = (bf16[512,128]{1,0:T(8,128)(2,1)S(1)}, bf16[512,128]{1,0:T(8,128)(2,1)S(1)}, u32[]{:S(2)}, u32[]{:S(2)}) collective-permute-start(bf16[512,128]{1,0:T(8,128)(2,1)S(1)} %add_convert_fusion.near_ref), channel_id=1, source_target_pairs={{0,2},{1,3},{2,0},{3,1},{4,6},{5,7},{6,4},{7,5},{8,10},{9,11},{10,... | collective-permute-start | bytes 393224 | tf_op jit(solution)/shard_map/ppermute | solution.py:301
  15.0 4.1 %collective-permute-done.5.far_ref = bf16[512,128]{1,0:T(8,128)(2,1)S(1)} collective-permute-done((bf16[512,128]{1,0:T(8,128)(2,1)S(1)}, bf16[512,128]{1,0:T(8,128)(2,1)S(1)}, u32[]{:S(2)}, u32[]{:S(2)}) %collective-permute-start.5) | collective-permute-done | bytes 131104 | tf_op jit(solution)/shard_map/ppermute | solution.py:301
  19.1 0.7 %layer.1 = (f32[256,256]{1,0:T(8,128)S(1)}, bf16[784,128]{1,0:T(8,128)(2,1)S(1)}) custom-call(bf16[512,128]{1,0:T(8,128)(2,1)S(1)} %add_convert_fusion.near_ref, bf16[512,128]{1,0:T(8,128)(2,1)S(1)} %collective-permute-done.5.far_ref, bf16[256,256]{1,0:T(8,128)(2,1)S(1)} %copy-done, bf16[256,256]{1,0:T(8,128)(2,1)S(1)} %collective-permute-done.4.cot_far_ref, ...), custom_call_target="tpu_custom_call" | custom-call | tf_op jit(solution)/shard_map/layer/pallas_call | solution.py:321
  19.8 0.1 collective-permute-start.6
  19.9 0.5 %backward_mine.1.part_ref = f32[4,256,128]{2,1,0:T(8,128)S(1)} custom-call(bf16[1024,1024]{1,0:T(8,128)(2,1)S(1)} %densify.1.tile_ref, bf16[784,128]{1,0:T(8,128)(2,1)S(1)} %get-tuple-element.25.own_ref), custom_call_target="tpu_custom_call" | custom-call | flops 134217728 | bytes 1048576 | tf_op jit(solution)/shard_map/backward_mine/pallas_call | solution.py:333
  20.4 0.9 %collective-permute-done.6.sib_ref = bf16[784,128]{1,0:T(8,128)(2,1)S(1)} collective-permute-done((bf16[784,128]{1,0:T(8,128)(2,1)S(1)}, bf16[784,128]{1,0:T(8,128)(2,1)S(1)}, u32[]{:S(2)}, u32[]{:S(2)}) %collective-permute-start.6) | collective-permute-done | bytes 200736 | tf_op jit(solution)/shard_map/ppermute | solution.py:301
  21.3 1.2 %collective-permute-start.7 = (bf16[144,128]{1,0:T(8,128)(2,1)S(1)}, bf16[144,128]{1,0:T(8,128)(2,1)S(1)}, u32[]{:S(2)}, u32[]{:S(2)}) collective-permute-start(bf16[144,128]{1,0:T(8,128)(2,1)S(1)} %stripe.1), channel_id=1, source_target_pairs={{0,4},{4,0},{8,12},{12,8},{1,5},{5,1},{9,13},{13,9},{2,6},{6,2},{1... | collective-permute-start | bytes 110600 | tf_op jit(solution)/shard_map/ppermute | solution.py:301
  22.5 0.5 %backward.1 = (f32[256,128]{1,0:T(8,128)S(1)}, bf16[256,128]{1,0:T(8,128)(2,1)S(1)}, bf16[256,128]{1,0:T(8,128)(2,1)S(1)}, bf16[256,128]{1,0:T(8,128)(2,1)S(1)}) custom-call(bf16[1024,1024]{1,0:T(8,128)(2,1)S(1)} %densify.1.tile_ref, bf16[784,128]{1,0:T(8,128)(2,1)S(1)} %get-tuple-element.25.own_ref, bf16[784,128]{1,0:T(8,128)(2,1)S(1)} %collective-permute-done.6.sib_ref, ...), custom_call_target="tpu_custom_call" | custom-call | tf_op jit(solution)/shard_map/backward/pallas_call | solution.py:352
  23.1 1.0 %collective-permute-start.9 = (bf16[256,128]{1,0:T(8,128)(2,1)S(1)}, bf16[256,128]{1,0:T(8,128)(2,1)S(1)}, u32[]{:S(2)}, u32[]{:S(2)}) collective-permute-start(bf16[256,128]{1,0:T(8,128)(2,1)S(1)} %get-tuple-element.35), channel_id=1, source_target_pairs={{0,4},{4,0},{8,12},{12,8},{1,5},{5,1},{9,13},{13,9},{2,6},{6,2},{1... | collective-permute-start | bytes 196616 | tf_op jit(solution)/shard_map/ppermute | solution.py:301
  24.0 2.1 %collective-permute-start.10 = (bf16[256,128]{1,0:T(8,128)(2,1)S(1)}, bf16[256,128]{1,0:T(8,128)(2,1)S(1)}, u32[]{:S(2)}, u32[]{:S(2)}) collective-permute-start(bf16[256,128]{1,0:T(8,128)(2,1)S(1)} %get-tuple-element.36), channel_id=1, source_target_pairs={{0,8},{4,12},{8,0},{12,4},{1,9},{5,13},{9,1},{13,5},{2,10},{6,14},... | collective-permute-start | bytes 196616 | tf_op jit(solution)/shard_map/ppermute | solution.py:301
  26.1 1.3 %collective-permute-start.8 = (bf16[144,128]{1,0:T(8,128)(2,1)S(1)}, bf16[144,128]{1,0:T(8,128)(2,1)S(1)}, u32[]{:S(2)}, u32[]{:S(2)}) collective-permute-start(bf16[144,128]{1,0:T(8,128)(2,1)S(1)} %add_convert_fusion.1.pair_ref), channel_id=1, source_target_pairs={{0,8},{4,12},{8,0},{12,4},{1,9},{5,13},{9,1},{13,5},{2,10},{6,14},... | collective-permute-start | bytes 110600 | tf_op jit(solution)/shard_map/ppermute | solution.py:301
  27.5 0.7 %multiply_convert_fusion = bf16[256,256]{1,0:T(8,128)(2,1)} fusion(f32[256,256]{1,0:T(8,128)S(1)} %get-tuple-element.32), kind=kLoop, calls=%fused_computation | loop fusion | flops 327680 | bytes 393216 | tf_op jit(solution)/shard_map/convert_element_type | solution.py:364
  28.2 3.0 %collective-permute-start.11 = (bf16[256,128]{1,0:T(8,128)(2,1)S(1)}, bf16[256,128]{1,0:T(8,128)(2,1)S(1)}, u32[]{:S(2)}, u32[]{:S(2)}) collective-permute-start(bf16[256,128]{1,0:T(8,128)(2,1)S(1)} %get-tuple-element.37), channel_id=1, source_target_pairs={{0,12},{4,8},{8,4},{12,0},{1,13},{5,9},{9,5},{13,1},{2,14},{6,10},... | collective-permute-start | bytes 196616 | tf_op jit(solution)/shard_map/ppermute | solution.py:301
  31.3 2.0 %collective-permute-done.8.pair_far_ref = bf16[144,128]{1,0:T(8,128)(2,1)S(1)} collective-permute-done((bf16[144,128]{1,0:T(8,128)(2,1)S(1)}, bf16[144,128]{1,0:T(8,128)(2,1)S(1)}, u32[]{:S(2)}, u32[]{:S(2)}) %collective-permute-start.8) | collective-permute-done | bytes 36896 | tf_op jit(solution)/shard_map/ppermute | solution.py:301
  33.3 0.1 collective-permute-start.12
  33.4 1.0 %collective-permute-done.11.got3 = bf16[256,128]{1,0:T(8,128)(2,1)S(1)} collective-permute-done((bf16[256,128]{1,0:T(8,128)(2,1)S(1)}, bf16[256,128]{1,0:T(8,128)(2,1)S(1)}, u32[]{:S(2)}, u32[]{:S(2)}) %collective-permute-start.11) | collective-permute-done | bytes 65568 | tf_op jit(solution)/shard_map/ppermute | solution.py:301
  34.3 0.3 collective-permute-done.12.sib_ref
  34.6 0.7 %last.1 = (bf16[256,128]{1,0:T(8,128)(2,1)}, f32[128,256]{1,0:T(8,128)}, f32[1,256]{1,0:T(1,128)}) custom-call(f32[256,128]{1,0:T(8,128)S(1)} %get-tuple-element.34.keep_ref, bf16[256,128]{1,0:T(8,128)(2,1)S(1)} %collective-permute-done.9.got1, bf16[256,128]{1,0:T(8,128)(2,1)S(1)} %collective-permute-done.10.got2, ...), custom_call_target="tpu_custom_call" | custom-call | tf_op jit(solution)/shard_map/last/pallas_call | solution.py:370
  (16 shorter events, 0.1 us)
Async XLA Ops:
  0.6 10.8 %copy-start.3 = (bf16[256,128]{1,0:T(8,128)(2,1)S(1)}, bf16[256,128]{1,0:T(8,128)(2,1)}, u32[]{:S(2)}) copy-start(bf16[256,128]{1,0:T(8,128)(2,1)} %param.8) | copy-start | bytes 196612
  0.6 10.9 %collective-permute-start = (bf16[256,128]{1,0:T(8,128)(2,1)}, bf16[256,128]{1,0:T(8,128)(2,1)S(1)}, u32[]{:S(2)}, u32[]{:S(2)}) collective-permute-start(bf16[256,128]{1,0:T(8,128)(2,1)} %param.8), channel_id=1, source_target_pairs={{0,12},{4,8},{8,4},{12,0},{1,13},{5,9},{9,5},{13,1},{2,14},{6,10},... | collective-permute-start | bytes 196616 | tf_op jit(solution)/shard_map/ppermute | solution.py:301
  5.8 5.8 %collective-permute-start.2 = (bf16[256,128]{1,0:T(8,128)(2,1)}, bf16[256,128]{1,0:T(8,128)(2,1)S(1)}, u32[]{:S(2)}, u32[]{:S(2)}) collective-permute-start(bf16[256,128]{1,0:T(8,128)(2,1)} %param.8), channel_id=1, source_target_pairs={{0,8},{4,12},{8,0},{12,4},{1,9},{5,13},{9,1},{13,5},{2,10},{6,14},... | collective-permute-start | bytes 196616 | tf_op jit(solution)/shard_map/ppermute | solution.py:301
  5.8 5.8 %collective-permute-start.1 = (bf16[256,128]{1,0:T(8,128)(2,1)}, bf16[256,128]{1,0:T(8,128)(2,1)S(1)}, u32[]{:S(2)}, u32[]{:S(2)}) collective-permute-start(bf16[256,128]{1,0:T(8,128)(2,1)} %param.8), channel_id=1, source_target_pairs={{0,4},{4,0},{8,12},{12,8},{1,5},{5,1},{9,13},{13,9},{2,6},{6,2},{1... | collective-permute-start | bytes 196616 | tf_op jit(solution)/shard_map/ppermute | solution.py:301
  6.4 6.1 %collective-permute-start.4 = (bf16[256,256]{1,0:T(8,128)(2,1)}, bf16[256,256]{1,0:T(8,128)(2,1)S(1)}, u32[]{:S(2)}, u32[]{:S(2)}) collective-permute-start(bf16[256,256]{1,0:T(8,128)(2,1)} %cot_ref.1), channel_id=1, source_target_pairs={{0,2},{1,3},{2,0},{3,1},{4,6},{5,7},{6,4},{7,5},{8,10},{9,11},{10,... | collective-permute-start | bytes 393224 | tf_op jit(solution)/shard_map/ppermute | solution.py:301
  11.4 7.6 %copy-start = (bf16[256,256]{1,0:T(8,128)(2,1)S(1)}, bf16[256,256]{1,0:T(8,128)(2,1)}, u32[]{:S(2)}) copy-start(bf16[256,256]{1,0:T(8,128)(2,1)} %cot_ref.1) | copy-start | bytes 393220
  11.5 7.6 %copy-start.1 = (bf16[128,256]{1,0:T(8,128)(2,1)S(1)}, bf16[128,256]{1,0:T(8,128)(2,1)}, u32[]{:S(2)}) copy-start(bf16[128,256]{1,0:T(8,128)(2,1)} %weight_ref.1) | copy-start | bytes 196612
  11.5 7.6 %copy-start.2 = (f32[256]{0:T(256)S(1)}, f32[256]{0:T(256)}, u32[]{:S(2)}) copy-start(f32[256]{0:T(256)} %param.14) | copy-start | bytes 3076
  12.0 1.4 %collective-permute-start.3 = (bf16[512,128]{1,0:T(8,128)(2,1)S(1)}, bf16[512,128]{1,0:T(8,128)(2,1)S(1)}, u32[]{:S(2)}, u32[]{:S(2)}) collective-permute-start(bf16[512,128]{1,0:T(8,128)(2,1)S(1)} %forward_sibling.1), channel_id=1, source_target_pairs={{0,1},{1,0},{2,3},{3,2},{4,5},{5,4},{6,7},{7,6},{8,9},{9,8},{10,11... | collective-permute-start | bytes 393224 | tf_op jit(solution)/shard_map/ppermute | solution.py:301
  13.5 5.6 %collective-permute-start.5 = (bf16[512,128]{1,0:T(8,128)(2,1)S(1)}, bf16[512,128]{1,0:T(8,128)(2,1)S(1)}, u32[]{:S(2)}, u32[]{:S(2)}) collective-permute-start(bf16[512,128]{1,0:T(8,128)(2,1)S(1)} %add_convert_fusion.near_ref), channel_id=1, source_target_pairs={{0,2},{1,3},{2,0},{3,1},{4,6},{5,7},{6,4},{7,5},{8,10},{9,11},{10,... | collective-permute-start | bytes 393224 | tf_op jit(solution)/shard_map/ppermute | solution.py:301
  19.8 1.5 %collective-permute-start.6 = (bf16[784,128]{1,0:T(8,128)(2,1)S(1)}, bf16[784,128]{1,0:T(8,128)(2,1)S(1)}, u32[]{:S(2)}, u32[]{:S(2)}) collective-permute-start(bf16[784,128]{1,0:T(8,128)(2,1)S(1)} %get-tuple-element.25.own_ref), channel_id=1, source_target_pairs={{0,1},{1,0},{2,3},{3,2},{4,5},{5,4},{6,7},{7,6},{8,9},{9,8},{10,11... | collective-permute-start | bytes 602120 | tf_op jit(solution)/shard_map/ppermute | solution.py:301
  21.3 4.8 %collective-permute-start.7 = (bf16[144,128]{1,0:T(8,128)(2,1)S(1)}, bf16[144,128]{1,0:T(8,128)(2,1)S(1)}, u32[]{:S(2)}, u32[]{:S(2)}) collective-permute-start(bf16[144,128]{1,0:T(8,128)(2,1)S(1)} %stripe.1), channel_id=1, source_target_pairs={{0,4},{4,0},{8,12},{12,8},{1,5},{5,1},{9,13},{13,9},{2,6},{6,2},{1... | collective-permute-start | bytes 110600 | tf_op jit(solution)/shard_map/ppermute | solution.py:301
  23.1 10.3 %collective-permute-start.9 = (bf16[256,128]{1,0:T(8,128)(2,1)S(1)}, bf16[256,128]{1,0:T(8,128)(2,1)S(1)}, u32[]{:S(2)}, u32[]{:S(2)}) collective-permute-start(bf16[256,128]{1,0:T(8,128)(2,1)S(1)} %get-tuple-element.35), channel_id=1, source_target_pairs={{0,4},{4,0},{8,12},{12,8},{1,5},{5,1},{9,13},{13,9},{2,6},{6,2},{1... | collective-permute-start | bytes 196616 | tf_op jit(solution)/shard_map/ppermute | solution.py:301
  24.0 9.4 %collective-permute-start.10 = (bf16[256,128]{1,0:T(8,128)(2,1)S(1)}, bf16[256,128]{1,0:T(8,128)(2,1)S(1)}, u32[]{:S(2)}, u32[]{:S(2)}) collective-permute-start(bf16[256,128]{1,0:T(8,128)(2,1)S(1)} %get-tuple-element.36), channel_id=1, source_target_pairs={{0,8},{4,12},{8,0},{12,4},{1,9},{5,13},{9,1},{13,5},{2,10},{6,14},... | collective-permute-start | bytes 196616 | tf_op jit(solution)/shard_map/ppermute | solution.py:301
  26.1 7.1 %collective-permute-start.8 = (bf16[144,128]{1,0:T(8,128)(2,1)S(1)}, bf16[144,128]{1,0:T(8,128)(2,1)S(1)}, u32[]{:S(2)}, u32[]{:S(2)}) collective-permute-start(bf16[144,128]{1,0:T(8,128)(2,1)S(1)} %add_convert_fusion.1.pair_ref), channel_id=1, source_target_pairs={{0,8},{4,12},{8,0},{12,4},{1,9},{5,13},{9,1},{13,5},{2,10},{6,14},... | collective-permute-start | bytes 110600 | tf_op jit(solution)/shard_map/ppermute | solution.py:301
  28.2 6.1 %collective-permute-start.11 = (bf16[256,128]{1,0:T(8,128)(2,1)S(1)}, bf16[256,128]{1,0:T(8,128)(2,1)S(1)}, u32[]{:S(2)}, u32[]{:S(2)}) collective-permute-start(bf16[256,128]{1,0:T(8,128)(2,1)S(1)} %get-tuple-element.37), channel_id=1, source_target_pairs={{0,12},{4,8},{8,4},{12,0},{1,13},{5,9},{9,5},{13,1},{2,14},{6,10},... | collective-permute-start | bytes 196616 | tf_op jit(solution)/shard_map/ppermute | solution.py:301
  33.3 1.3 %collective-permute-start.12 = (f32[128,128]{1,0:T(8,128)S(1)}, f32[128,128]{1,0:T(8,128)S(1)}, u32[]{:S(2)}, u32[]{:S(2)}) collective-permute-start(f32[128,128]{1,0:T(8,128)S(1)} %convert_add_fusion.half_ref), channel_id=1, source_target_pairs={{0,1},{1,0},{2,3},{3,2},{4,5},{5,4},{6,7},{7,6},{8,9},{9,8},{10,11... | collective-permute-start | bytes 196616 | tf_op jit(solution)/shard_map/ppermute | solution.py:301

commit v6 on v5

--- a/solution.py
+++ b/solution.py
@@ -279,8 +279,8 @@
         ).astype(BF16)
 
 
-def last_kernel(scale, keep_ref, got1, got2, got3, pair_ref, pair_far_ref, half_ref, sib_ref,
-                features_ref, gw_ref, gb_ref):
+def last_kernel(scale, keep_ref, got1, got2, got3, act_ref, pair_ref, pair_far_ref, half_ref, sib_ref,
+                features_ref, hidden_ref, gw_ref, gb_ref):
     core = lax.rem(lax.axis_index("col"), 2)
     width_in, hid = gw_ref.shape
     half = half_ref[...] * scale
@@ -294,6 +294,7 @@
     total = keep_ref[...] + got1[...].astype(F32)
     total = total + got2[...].astype(F32) + got3[...].astype(F32)
     features_ref[...] = total.astype(BF16)
+    hidden_ref[...] = act_ref[...]
 
 
 def swap(array, axis, bit):
@@ -348,7 +349,7 @@
         compiler_params=LIMIT,
         name="stripe",
     )(grads, grads_sib)
-    stripe_far = swap(stripe, "row", 1)
+    stripe_far = swap(stripe, "row", 2)
     own, *sends = pl.pallas_call(
         backward_kernel,
         in_specs=[WHOLE] * 4,
@@ -362,23 +363,24 @@
     got = [swap(send, "row", k) for k, send in zip((1, 2, 3), sends)]
     pair, pre_act = lax.optimization_barrier((pair, pre_act))
     hidden = (pre_act * jax.nn.sigmoid(pre_act)).astype(BF16)
-    pair_far = swap(pair, "row", 2)
+    pair_far = swap(pair, "row", 1)
     gw_half = pair[:width_in].astype(F32) + pair_far[:width_in].astype(F32)
     gw_half, hidden = lax.optimization_barrier((gw_half, hidden))
     gw_sib = swap(gw_half, "col", 1)
     norm_scale = float(node_rows * ROWS * COLS) ** (-0.5)
-    grad_features, grad_weight, grad_bias = pl.pallas_call(
+    grad_features, hidden, grad_weight, grad_bias = pl.pallas_call(
         functools.partial(last_kernel, norm_scale),
-        in_specs=[WHOLE] * 8,
-        out_specs=[WHOLE] * 3,
+        in_specs=[WHOLE] * 9,
+        out_specs=[WHOLE] * 4,
         out_shape=[
             block,
+            jax.ShapeDtypeStruct(hidden.shape, BF16),
             jax.ShapeDtypeStruct((width_in, hid), F32),
             jax.ShapeDtypeStruct((1, hid), F32),
         ],
         compiler_params=LIMIT,
         name="last",
-    )(own, *got, pair, pair_far, gw_half, gw_sib)
+    )(own, *got, hidden, pair, pair_far, gw_half, gw_sib)
     return hidden, grad_weight, grad_bias.reshape(hid), grad_features
 
 

time: 35.5 us -> 34.9 us (0.983)
  waiting for transfers between devices: 9.17 us -> 10.2 us
  starting transfers between devices: 17.8 us -> 16.8 us
  other arithmetic: 0.78 us -> 0.13 us
    ppermute x13, waiting for transfers between devices: 9.17 us -> 10.2 us  [swap(): return lax.ppermute(array, axis, [(i, i ^ bit) for i in range(size)])]
    ppermute x13, starting transfers between devices: 17.8 us -> 16.8 us  [swap(): return lax.ppermute(array, axis, [(i, i ^ bit) for i in range(size)])]
    convert_element_type x1, other arithmetic: 0.73 us -> 0.08 us  [dense_tile(): hidden = (pre_act * jax.nn.sigmoid(pre_act)).astype(BF16)]
  transfers between devices with their start and end apart: 13 -> 13, of which waited for: 6 -> 8; matrix products, arithmetic and copies ran while one was open for 2% -> 0% of each run, Pallas kernels for 13% -> 13%
where the time goes in v6:
time: 34.9 us; the launch traced here: 34.7 us
  starting transfers between devices  16.8 us (48%)
  waiting for transfers between devices  10.2 us (29%)
  Pallas kernels  6.04 us (17%)
  between operations  1.45 us (4%)
    ppermute x13, starting transfers between devices, swap(): return lax.ppermute(array, axis, [(i, i ^ bit) for i in range(size)])  16.8 us
    ppermute x13, waiting for transfers between devices, swap(): return lax.ppermute(array, axis, [(i, i ^ bit) for i in range(size)])  10.2 us
    pallas_call x1, Pallas kernels, densify(): pl.pallas_call(functools.partial(densify_kernel, chunks, row_blocks, col_...  2.68 us
    pallas_call x2, Pallas kernels, forward(): pl.pallas_call(functools.partial(forward_kernel, mine), in_specs=[WHOLE]...  0.86 us
    pallas_call x1, Pallas kernels, dense_tile(): pl.pallas_call(functools.partial(last_kernel, norm_scale), in_specs=[WHOL...  0.76 us
    pallas_call x1, Pallas kernels, dense_tile(): pl.pallas_call(layer_kernel, in_specs=[WHOLE] * 6, out_specs=[WHOLE] * 2,...  0.7 us
  transfers between devices with their start and end apart: 13, of which 8 were waited for; matrix products, arithmetic and copies ran while one was open for 0% of the time, Pallas kernels for 13%

profile of v6, /device:TPU:0, one launch (start us, length us, event | category | flops | bytes accessed | tf_op | source)
XLA Modules:
  0.0 34.7 jit_solution(2487570122274671589)
XLA Ops:
  0.6 5.1 %collective-permute-start = (bf16[256,128]{1,0:T(8,128)(2,1)}, bf16[256,128]{1,0:T(8,128)(2,1)S(1)}, u32[]{:S(2)}, u32[]{:S(2)}) collective-permute-start(bf16[256,128]{1,0:T(8,128)(2,1)} %param.8), channel_id=1, source_target_pairs={{0,12},{4,8},{8,4},{12,0},{1,13},{5,9},{9,5},{13,1},{2,14},{6,10},... | collective-permute-start | bytes 196616 | tf_op jit(solution)/shard_map/ppermute | solution.py:302
  5.8 0.6 %collective-permute-start.1 = (bf16[256,128]{1,0:T(8,128)(2,1)}, bf16[256,128]{1,0:T(8,128)(2,1)S(1)}, u32[]{:S(2)}, u32[]{:S(2)}) collective-permute-start(bf16[256,128]{1,0:T(8,128)(2,1)} %param.8), channel_id=1, source_target_pairs={{0,4},{4,0},{8,12},{12,8},{1,5},{5,1},{9,13},{13,9},{2,6},{6,2},{1... | collective-permute-start | bytes 196616 | tf_op jit(solution)/shard_map/ppermute | solution.py:302
  6.4 1.6 %collective-permute-start.4 = (bf16[256,256]{1,0:T(8,128)(2,1)}, bf16[256,256]{1,0:T(8,128)(2,1)S(1)}, u32[]{:S(2)}, u32[]{:S(2)}) collective-permute-start(bf16[256,256]{1,0:T(8,128)(2,1)} %cot_ref.1), channel_id=1, source_target_pairs={{0,2},{1,3},{2,0},{3,1},{4,6},{5,7},{6,4},{7,5},{8,10},{9,11},{10,... | collective-permute-start | bytes 393224 | tf_op jit(solution)/shard_map/ppermute | solution.py:302
  8.7 2.7 %densify.1.tile_ref = bf16[1024,1024]{1,0:T(8,128)(2,1)S(1)} custom-call(s32[1,1]{1,0:T(1,128)} %bitcast.3.count_in, s32[128]{0:T(128)} %rows_in.1, s32[128]{0:T(128)} %cols_in.1, bf16[128,128,128]{2,1,0:T(8,128)(2,1)} %values_ref.1), custom_call_target="tpu_custom_call" | custom-call | flops 2097152 | bytes 4194304 | tf_op jit(solution)/shard_map/densify/pallas_call | solution.py:151
  11.4 0.0 copy-start
  11.4 0.0 copy-start.1
  11.4 0.0 copy-start.2
  11.4 0.0 collective-permute-done
  11.5 0.1 collective-permute-done.2.x2
  11.6 0.4 %forward_sibling.1 = bf16[512,128]{1,0:T(8,128)(2,1)S(1)} custom-call(bf16[1024,1024]{1,0:T(8,128)(2,1)S(1)} %densify.1.tile_ref, bf16[512,128]{1,0:T(8,128)(2,1)S(1)} %constant_dynamic-update-slice_fusion.outer_ref, bf16[256,128]{1,0:T(8,128)(2,1)S(1)} %collective-permute-done.1.x1, bf16[256,128]{1,0:T(8,128)(2,1)S(1)} %collective-permute-done.2.x2), custom_call_target="tpu_custom_call" | custom-call | flops 134217728 | bytes 1048576 | tf_op jit(solution)/shard_map/forward_sibling/pallas_call | solution.py:189
  12.0 0.1 collective-permute-start.3
  12.1 0.4 %forward_mine.1 = f32[512,128]{1,0:T(8,128)S(1)} custom-call(bf16[1024,1024]{1,0:T(8,128)(2,1)S(1)} %densify.1.tile_ref, bf16[512,128]{1,0:T(8,128)(2,1)S(1)} %constant_dynamic-update-slice_fusion.outer_ref, bf16[256,128]{1,0:T(8,128)(2,1)S(1)} %collective-permute-done.1.x1, bf16[256,128]{1,0:T(8,128)(2,1)S(1)} %collective-permute-done.2.x2), custom_call_target="tpu_custom_call" | custom-call | flops 134217728 | bytes 1048576 | tf_op jit(solution)/shard_map/forward_mine/pallas_call | solution.py:189
  12.5 0.9 %collective-permute-done.3 = bf16[512,128]{1,0:T(8,128)(2,1)S(1)} collective-permute-done((bf16[512,128]{1,0:T(8,128)(2,1)S(1)}, bf16[512,128]{1,0:T(8,128)(2,1)S(1)}, u32[]{:S(2)}, u32[]{:S(2)}) %collective-permute-start.3) | collective-permute-done | bytes 131104 | tf_op jit(solution)/shard_map/ppermute | solution.py:302
  13.5 1.6 %collective-permute-start.5 = (bf16[512,128]{1,0:T(8,128)(2,1)S(1)}, bf16[512,128]{1,0:T(8,128)(2,1)S(1)}, u32[]{:S(2)}, u32[]{:S(2)}) collective-permute-start(bf16[512,128]{1,0:T(8,128)(2,1)S(1)} %add_convert_fusion.near_ref), channel_id=1, source_target_pairs={{0,2},{1,3},{2,0},{3,1},{4,6},{5,7},{6,4},{7,5},{8,10},{9,11},{10,... | collective-permute-start | bytes 393224 | tf_op jit(solution)/shard_map/ppermute | solution.py:302
  15.0 4.1 %collective-permute-done.5.far_ref = bf16[512,128]{1,0:T(8,128)(2,1)S(1)} collective-permute-done((bf16[512,128]{1,0:T(8,128)(2,1)S(1)}, bf16[512,128]{1,0:T(8,128)(2,1)S(1)}, u32[]{:S(2)}, u32[]{:S(2)}) %collective-permute-start.5) | collective-permute-done | bytes 131104 | tf_op jit(solution)/shard_map/ppermute | solution.py:302
  19.1 0.7 %layer.1 = (f32[256,256]{1,0:T(8,128)S(1)}, bf16[784,128]{1,0:T(8,128)(2,1)S(1)}) custom-call(bf16[512,128]{1,0:T(8,128)(2,1)S(1)} %add_convert_fusion.near_ref, bf16[512,128]{1,0:T(8,128)(2,1)S(1)} %collective-permute-done.5.far_ref, bf16[256,256]{1,0:T(8,128)(2,1)S(1)} %copy-done, bf16[256,256]{1,0:T(8,128)(2,1)S(1)} %collective-permute-done.4.cot_far_ref, ...), custom_call_target="tpu_custom_call" | custom-call | tf_op jit(solution)/shard_map/layer/pallas_call | solution.py:322
  19.8 0.1 collective-permute-start.6
  19.9 0.5 %backward_mine.1.part_ref = f32[4,256,128]{2,1,0:T(8,128)S(1)} custom-call(bf16[1024,1024]{1,0:T(8,128)(2,1)S(1)} %densify.1.tile_ref, bf16[784,128]{1,0:T(8,128)(2,1)S(1)} %get-tuple-element.26.own_ref), custom_call_target="tpu_custom_call" | custom-call | flops 134217728 | bytes 1048576 | tf_op jit(solution)/shard_map/backward_mine/pallas_call | solution.py:334
  20.4 0.9 %collective-permute-done.6.sib_ref = bf16[784,128]{1,0:T(8,128)(2,1)S(1)} collective-permute-done((bf16[784,128]{1,0:T(8,128)(2,1)S(1)}, bf16[784,128]{1,0:T(8,128)(2,1)S(1)}, u32[]{:S(2)}, u32[]{:S(2)}) %collective-permute-start.6) | collective-permute-done | bytes 200736 | tf_op jit(solution)/shard_map/ppermute | solution.py:302
  21.3 2.1 %collective-permute-start.9 = (bf16[144,128]{1,0:T(8,128)(2,1)S(1)}, bf16[144,128]{1,0:T(8,128)(2,1)S(1)}, u32[]{:S(2)}, u32[]{:S(2)}) collective-permute-start(bf16[144,128]{1,0:T(8,128)(2,1)S(1)} %stripe.1), channel_id=1, source_target_pairs={{0,8},{4,12},{8,0},{12,4},{1,9},{5,13},{9,1},{13,5},{2,10},{6,14},... | collective-permute-start | bytes 110600 | tf_op jit(solution)/shard_map/ppermute | solution.py:302
  23.4 0.5 %backward.1 = (f32[256,128]{1,0:T(8,128)S(1)}, bf16[256,128]{1,0:T(8,128)(2,1)S(1)}, bf16[256,128]{1,0:T(8,128)(2,1)S(1)}, bf16[256,128]{1,0:T(8,128)(2,1)S(1)}) custom-call(bf16[1024,1024]{1,0:T(8,128)(2,1)S(1)} %densify.1.tile_ref, bf16[784,128]{1,0:T(8,128)(2,1)S(1)} %get-tuple-element.26.own_ref, bf16[784,128]{1,0:T(8,128)(2,1)S(1)} %collective-permute-done.6.sib_ref, ...), custom_call_target="tpu_custom_call" | custom-call | tf_op jit(solution)/shard_map/backward/pallas_call | solution.py:353
  24.0 2.1 %collective-permute-start.7 = (bf16[256,128]{1,0:T(8,128)(2,1)S(1)}, bf16[256,128]{1,0:T(8,128)(2,1)S(1)}, u32[]{:S(2)}, u32[]{:S(2)}) collective-permute-start(bf16[256,128]{1,0:T(8,128)(2,1)S(1)} %get-tuple-element.30), channel_id=1, source_target_pairs={{0,4},{4,0},{8,12},{12,8},{1,5},{5,1},{9,13},{13,9},{2,6},{6,2},{1... | collective-permute-start | bytes 196616 | tf_op jit(solution)/shard_map/ppermute | solution.py:302
  26.0 0.0 collective-permute-start.8
  26.1 1.0 %collective-permute-done.9 = bf16[144,128]{1,0:T(8,128)(2,1)S(1)} collective-permute-done((bf16[144,128]{1,0:T(8,128)(2,1)S(1)}, bf16[144,128]{1,0:T(8,128)(2,1)S(1)}, u32[]{:S(2)}, u32[]{:S(2)}) %collective-permute-start.9) | collective-permute-done | bytes 36896 | tf_op jit(solution)/shard_map/ppermute | solution.py:302
  27.1 0.5 %collective-permute-start.11 = (bf16[144,128]{1,0:T(8,128)(2,1)S(1)}, bf16[144,128]{1,0:T(8,128)(2,1)S(1)}, u32[]{:S(2)}, u32[]{:S(2)}) collective-permute-start(bf16[144,128]{1,0:T(8,128)(2,1)S(1)} %add_convert_fusion.1.pair_ref), channel_id=1, source_target_pairs={{0,4},{4,0},{8,12},{12,8},{1,5},{5,1},{9,13},{13,9},{2,6},{6,2},{1... | collective-permute-start | bytes 110600 | tf_op jit(solution)/shard_map/ppermute | solution.py:302
  27.6 0.1 multiply_convert_fusion.act_ref
  27.7 3.0 %collective-permute-start.10 = (bf16[256,128]{1,0:T(8,128)(2,1)S(1)}, bf16[256,128]{1,0:T(8,128)(2,1)S(1)}, u32[]{:S(2)}, u32[]{:S(2)}) collective-permute-start(bf16[256,128]{1,0:T(8,128)(2,1)S(1)} %get-tuple-element.33), channel_id=1, source_target_pairs={{0,12},{4,8},{8,4},{12,0},{1,13},{5,9},{9,5},{13,1},{2,14},{6,10},... | collective-permute-start | bytes 196616 | tf_op jit(solution)/shard_map/ppermute | solution.py:302
  30.7 1.6 %collective-permute-done.11.pair_far_ref = bf16[144,128]{1,0:T(8,128)(2,1)S(1)} collective-permute-done((bf16[144,128]{1,0:T(8,128)(2,1)S(1)}, bf16[144,128]{1,0:T(8,128)(2,1)S(1)}, u32[]{:S(2)}, u32[]{:S(2)}) %collective-permute-start.11) | collective-permute-done | bytes 36896 | tf_op jit(solution)/shard_map/ppermute | solution.py:302
  32.2 0.1 collective-permute-start.12
  32.3 0.7 %collective-permute-done.8.got2 = bf16[256,128]{1,0:T(8,128)(2,1)S(1)} collective-permute-done((bf16[256,128]{1,0:T(8,128)(2,1)S(1)}, bf16[256,128]{1,0:T(8,128)(2,1)S(1)}, u32[]{:S(2)}, u32[]{:S(2)}) %collective-permute-start.8) | collective-permute-done | bytes 65568 | tf_op jit(solution)/shard_map/ppermute | solution.py:302
  33.0 0.9 %collective-permute-done.10.got3 = bf16[256,128]{1,0:T(8,128)(2,1)S(1)} collective-permute-done((bf16[256,128]{1,0:T(8,128)(2,1)S(1)}, bf16[256,128]{1,0:T(8,128)(2,1)S(1)}, u32[]{:S(2)}, u32[]{:S(2)}) %collective-permute-start.10) | collective-permute-done | bytes 65568 | tf_op jit(solution)/shard_map/ppermute | solution.py:302
  33.9 0.8 %last.1 = (bf16[256,128]{1,0:T(8,128)(2,1)}, bf16[256,256]{1,0:T(8,128)(2,1)}, f32[128,256]{1,0:T(8,128)}, f32[1,256]{1,0:T(1,128)}) custom-call(f32[256,128]{1,0:T(8,128)S(1)} %get-tuple-element.29.keep_ref, bf16[256,128]{1,0:T(8,128)(2,1)S(1)} %collective-permute-done.7.got1, bf16[256,128]{1,0:T(8,128)(2,1)S(1)} %collective-permute-done.8.got2, ...), custom_call_target="tpu_custom_call" | custom-call | tf_op jit(solution)/shard_map/last/pallas_call | solution.py:371
  (16 shorter events, 0.1 us)
Async XLA Ops:
  0.6 10.7 %copy-start.3 = (bf16[256,128]{1,0:T(8,128)(2,1)S(1)}, bf16[256,128]{1,0:T(8,128)(2,1)}, u32[]{:S(2)}) copy-start(bf16[256,128]{1,0:T(8,128)(2,1)} %param.8) | copy-start | bytes 196612
  0.6 10.8 %collective-permute-start = (bf16[256,128]{1,0:T(8,128)(2,1)}, bf16[256,128]{1,0:T(8,128)(2,1)S(1)}, u32[]{:S(2)}, u32[]{:S(2)}) collective-permute-start(bf16[256,128]{1,0:T(8,128)(2,1)} %param.8), channel_id=1, source_target_pairs={{0,12},{4,8},{8,4},{12,0},{1,13},{5,9},{9,5},{13,1},{2,14},{6,10},... | collective-permute-start | bytes 196616 | tf_op jit(solution)/shard_map/ppermute | solution.py:302
  5.8 5.8 %collective-permute-start.2 = (bf16[256,128]{1,0:T(8,128)(2,1)}, bf16[256,128]{1,0:T(8,128)(2,1)S(1)}, u32[]{:S(2)}, u32[]{:S(2)}) collective-permute-start(bf16[256,128]{1,0:T(8,128)(2,1)} %param.8), channel_id=1, source_target_pairs={{0,8},{4,12},{8,0},{12,4},{1,9},{5,13},{9,1},{13,5},{2,10},{6,14},... | collective-permute-start | bytes 196616 | tf_op jit(solution)/shard_map/ppermute | solution.py:302
  5.8 5.8 %collective-permute-start.1 = (bf16[256,128]{1,0:T(8,128)(2,1)}, bf16[256,128]{1,0:T(8,128)(2,1)S(1)}, u32[]{:S(2)}, u32[]{:S(2)}) collective-permute-start(bf16[256,128]{1,0:T(8,128)(2,1)} %param.8), channel_id=1, source_target_pairs={{0,4},{4,0},{8,12},{12,8},{1,5},{5,1},{9,13},{13,9},{2,6},{6,2},{1... | collective-permute-start | bytes 196616 | tf_op jit(solution)/shard_map/ppermute | solution.py:302
  6.4 6.1 %collective-permute-start.4 = (bf16[256,256]{1,0:T(8,128)(2,1)}, bf16[256,256]{1,0:T(8,128)(2,1)S(1)}, u32[]{:S(2)}, u32[]{:S(2)}) collective-permute-start(bf16[256,256]{1,0:T(8,128)(2,1)} %cot_ref.1), channel_id=1, source_target_pairs={{0,2},{1,3},{2,0},{3,1},{4,6},{5,7},{6,4},{7,5},{8,10},{9,11},{10,... | collective-permute-start | bytes 393224 | tf_op jit(solution)/shard_map/ppermute | solution.py:302
  11.4 7.7 %copy-start = (bf16[256,256]{1,0:T(8,128)(2,1)S(1)}, bf16[256,256]{1,0:T(8,128)(2,1)}, u32[]{:S(2)}) copy-start(bf16[256,256]{1,0:T(8,128)(2,1)} %cot_ref.1) | copy-start | bytes 393220
  11.4 7.7 %copy-start.1 = (bf16[128,256]{1,0:T(8,128)(2,1)S(1)}, bf16[128,256]{1,0:T(8,128)(2,1)}, u32[]{:S(2)}) copy-start(bf16[128,256]{1,0:T(8,128)(2,1)} %weight_ref.1) | copy-start | bytes 196612
  11.4 7.7 %copy-start.2 = (f32[256]{0:T(256)S(1)}, f32[256]{0:T(256)}, u32[]{:S(2)}) copy-start(f32[256]{0:T(256)} %param.14) | copy-start | bytes 3076
  12.0 1.4 %collective-permute-start.3 = (bf16[512,128]{1,0:T(8,128)(2,1)S(1)}, bf16[512,128]{1,0:T(8,128)(2,1)S(1)}, u32[]{:S(2)}, u32[]{:S(2)}) collective-permute-start(bf16[512,128]{1,0:T(8,128)(2,1)S(1)} %forward_sibling.1), channel_id=1, source_target_pairs={{0,1},{1,0},{2,3},{3,2},{4,5},{5,4},{6,7},{7,6},{8,9},{9,8},{10,11... | collective-permute-start | bytes 393224 | tf_op jit(solution)/shard_map/ppermute | solution.py:302
  13.5 5.6 %collective-permute-start.5 = (bf16[512,128]{1,0:T(8,128)(2,1)S(1)}, bf16[512,128]{1,0:T(8,128)(2,1)S(1)}, u32[]{:S(2)}, u32[]{:S(2)}) collective-permute-start(bf16[512,128]{1,0:T(8,128)(2,1)S(1)} %add_convert_fusion.near_ref), channel_id=1, source_target_pairs={{0,2},{1,3},{2,0},{3,1},{4,6},{5,7},{6,4},{7,5},{8,10},{9,11},{10,... | collective-permute-start | bytes 393224 | tf_op jit(solution)/shard_map/ppermute | solution.py:302
  19.8 1.5 %collective-permute-start.6 = (bf16[784,128]{1,0:T(8,128)(2,1)S(1)}, bf16[784,128]{1,0:T(8,128)(2,1)S(1)}, u32[]{:S(2)}, u32[]{:S(2)}) collective-permute-start(bf16[784,128]{1,0:T(8,128)(2,1)S(1)} %get-tuple-element.26.own_ref), channel_id=1, source_target_pairs={{0,1},{1,0},{2,3},{3,2},{4,5},{5,4},{6,7},{7,6},{8,9},{9,8},{10,11... | collective-permute-start | bytes 602120 | tf_op jit(solution)/shard_map/ppermute | solution.py:302
  21.3 5.8 %collective-permute-start.9 = (bf16[144,128]{1,0:T(8,128)(2,1)S(1)}, bf16[144,128]{1,0:T(8,128)(2,1)S(1)}, u32[]{:S(2)}, u32[]{:S(2)}) collective-permute-start(bf16[144,128]{1,0:T(8,128)(2,1)S(1)} %stripe.1), channel_id=1, source_target_pairs={{0,8},{4,12},{8,0},{12,4},{1,9},{5,13},{9,1},{13,5},{2,10},{6,14},... | collective-permute-start | bytes 110600 | tf_op jit(solution)/shard_map/ppermute | solution.py:302
  24.0 8.4 %collective-permute-start.7 = (bf16[256,128]{1,0:T(8,128)(2,1)S(1)}, bf16[256,128]{1,0:T(8,128)(2,1)S(1)}, u32[]{:S(2)}, u32[]{:S(2)}) collective-permute-start(bf16[256,128]{1,0:T(8,128)(2,1)S(1)} %get-tuple-element.30), channel_id=1, source_target_pairs={{0,4},{4,0},{8,12},{12,8},{1,5},{5,1},{9,13},{13,9},{2,6},{6,2},{1... | collective-permute-start | bytes 196616 | tf_op jit(solution)/shard_map/ppermute | solution.py:302
  26.0 6.9 %collective-permute-start.8 = (bf16[256,128]{1,0:T(8,128)(2,1)S(1)}, bf16[256,128]{1,0:T(8,128)(2,1)S(1)}, u32[]{:S(2)}, u32[]{:S(2)}) collective-permute-start(bf16[256,128]{1,0:T(8,128)(2,1)S(1)} %get-tuple-element.31), channel_id=1, source_target_pairs={{0,8},{4,12},{8,0},{12,4},{1,9},{5,13},{9,1},{13,5},{2,10},{6,14},... | collective-permute-start | bytes 196616 | tf_op jit(solution)/shard_map/ppermute | solution.py:302
  27.1 5.1 %collective-permute-start.11 = (bf16[144,128]{1,0:T(8,128)(2,1)S(1)}, bf16[144,128]{1,0:T(8,128)(2,1)S(1)}, u32[]{:S(2)}, u32[]{:S(2)}) collective-permute-start(bf16[144,128]{1,0:T(8,128)(2,1)S(1)} %add_convert_fusion.1.pair_ref), channel_id=1, source_target_pairs={{0,4},{4,0},{8,12},{12,8},{1,5},{5,1},{9,13},{13,9},{2,6},{6,2},{1... | collective-permute-start | bytes 110600 | tf_op jit(solution)/shard_map/ppermute | solution.py:302
  27.7 6.2 %collective-permute-start.10 = (bf16[256,128]{1,0:T(8,128)(2,1)S(1)}, bf16[256,128]{1,0:T(8,128)(2,1)S(1)}, u32[]{:S(2)}, u32[]{:S(2)}) collective-permute-start(bf16[256,128]{1,0:T(8,128)(2,1)S(1)} %get-tuple-element.33), channel_id=1, source_target_pairs={{0,12},{4,8},{8,4},{12,0},{1,13},{5,9},{9,5},{13,1},{2,14},{6,10},... | collective-permute-start | bytes 196616 | tf_op jit(solution)/shard_map/ppermute | solution.py:302
  32.2 1.7 %collective-permute-start.12 = (f32[128,128]{1,0:T(8,128)S(1)}, f32[128,128]{1,0:T(8,128)S(1)}, u32[]{:S(2)}, u32[]{:S(2)}) collective-permute-start(f32[128,128]{1,0:T(8,128)S(1)} %convert_add_fusion.half_ref), channel_id=1, source_target_pairs={{0,1},{1,0},{2,3},{3,2},{4,5},{5,4},{6,7},{7,6},{8,9},{9,8},{10,11... | collective-permute-start | bytes 196616 | tf_op jit(solution)/shard_map/ppermute | solution.py:302

commit v7 on v6

--- a/solution.py
+++ b/solution.py
@@ -204,17 +204,14 @@
     weight = weight_ref[...]
     gw = None
     gb = None
-    for x in range(2):
-        block = pl.ds(x * rows, rows)
+    for other, source_ref in enumerate((cot_ref, cot_far_ref)):
+        block = pl.ds(pl.multiple_of(jnp.bitwise_xor(mine, other) * rows, rows), rows)
         aggregate = (near_ref[block, :].astype(F32) + far_ref[block, :].astype(F32)).astype(BF16)
         pre_act = jnp.dot(aggregate, weight, preferred_element_type=F32) + bias_ref[...]
         sigmoid_pre = jax.nn.sigmoid(pre_act)
-
-        @pl.when(mine == x)
-        def _():
+        if other == 0:
             act_ref[...] = pre_act
-
-        cot = jnp.where(mine == x, cot_ref[...], cot_far_ref[...]).astype(F32)
+        cot = source_ref[...].astype(F32)
         pre_grad = (cot * sigmoid_pre * (1.0 + pre_act * (1.0 - sigmoid_pre))).astype(BF16)
         swap_ref[block, :] = lax.dot_general(
             pre_grad, weight, (((1,), (1,)), ((), ())), preferred_element_type=F32

time: 34.9 us -> 34.8 us (level)
  starting transfers between devices: 16.8 us -> 17.2 us
where the time goes in v7:
time: 34.8 us; the launch traced here: 34.7 us
  starting transfers between devices  17.2 us (49%)
  waiting for transfers between devices  10 us (29%)
  Pallas kernels  5.88 us (17%)
  between operations  1.45 us (4%)
    ppermute x13, starting transfers between devices, swap(): return lax.ppermute(array, axis, [(i, i ^ bit) for i in range(size)])  17.2 us
    ppermute x13, waiting for transfers between devices, swap(): return lax.ppermute(array, axis, [(i, i ^ bit) for i in range(size)])  10 us
    pallas_call x1, Pallas kernels, densify(): pl.pallas_call(functools.partial(densify_kernel, chunks, row_blocks, col_...  2.68 us
    pallas_call x2, Pallas kernels, forward(): pl.pallas_call(functools.partial(forward_kernel, mine), in_specs=[WHOLE]...  0.86 us
    pallas_call x1, Pallas kernels, dense_tile(): pl.pallas_call(functools.partial(last_kernel, norm_scale), in_specs=[WHOL...  0.76 us
  transfers between devices with their start and end apart: 13, of which 8 were waited for; matrix products, arithmetic and copies ran while one was open for 0% of the time, Pallas kernels for 13%

profile of v7, /device:TPU:0, one launch (start us, length us, event | category | flops | bytes accessed | tf_op | source)
XLA Modules:
  0.0 34.7 jit_solution(7074496490081720326)
XLA Ops:
  0.6 5.1 %collective-permute-start = (bf16[256,128]{1,0:T(8,128)(2,1)}, bf16[256,128]{1,0:T(8,128)(2,1)S(1)}, u32[]{:S(2)}, u32[]{:S(2)}) collective-permute-start(bf16[256,128]{1,0:T(8,128)(2,1)} %param.8), channel_id=1, source_target_pairs={{0,12},{4,8},{8,4},{12,0},{1,13},{5,9},{9,5},{13,1},{2,14},{6,10},... | collective-permute-start | bytes 196616 | tf_op jit(solution)/shard_map/ppermute | solution.py:299
  5.8 0.0 collective-permute-start.2
  5.8 0.6 %collective-permute-start.1 = (bf16[256,128]{1,0:T(8,128)(2,1)}, bf16[256,128]{1,0:T(8,128)(2,1)S(1)}, u32[]{:S(2)}, u32[]{:S(2)}) collective-permute-start(bf16[256,128]{1,0:T(8,128)(2,1)} %param.8), channel_id=1, source_target_pairs={{0,4},{4,0},{8,12},{12,8},{1,5},{5,1},{9,13},{13,9},{2,6},{6,2},{1... | collective-permute-start | bytes 196616 | tf_op jit(solution)/shard_map/ppermute | solution.py:299
  6.4 1.6 %collective-permute-start.4 = (bf16[256,256]{1,0:T(8,128)(2,1)}, bf16[256,256]{1,0:T(8,128)(2,1)S(1)}, u32[]{:S(2)}, u32[]{:S(2)}) collective-permute-start(bf16[256,256]{1,0:T(8,128)(2,1)} %cot_ref.1), channel_id=1, source_target_pairs={{0,2},{1,3},{2,0},{3,1},{4,6},{5,7},{6,4},{7,5},{8,10},{9,11},{10,... | collective-permute-start | bytes 393224 | tf_op jit(solution)/shard_map/ppermute | solution.py:299
  8.7 2.7 %densify.1.tile_ref = bf16[1024,1024]{1,0:T(8,128)(2,1)S(1)} custom-call(s32[1,1]{1,0:T(1,128)} %bitcast.3.count_in, s32[128]{0:T(128)} %rows_in.1, s32[128]{0:T(128)} %cols_in.1, bf16[128,128,128]{2,1,0:T(8,128)(2,1)} %values_ref.1), custom_call_target="tpu_custom_call" | custom-call | flops 2097152 | bytes 4194304 | tf_op jit(solution)/shard_map/densify/pallas_call | solution.py:151
  11.4 0.0 copy-start
  11.4 0.0 copy-start.1
  11.4 0.0 copy-start.2
  11.5 0.1 collective-permute-done.2.x2
  11.6 0.4 %forward_sibling.1 = bf16[512,128]{1,0:T(8,128)(2,1)S(1)} custom-call(bf16[1024,1024]{1,0:T(8,128)(2,1)S(1)} %densify.1.tile_ref, bf16[512,128]{1,0:T(8,128)(2,1)S(1)} %constant_dynamic-update-slice_fusion.outer_ref, bf16[256,128]{1,0:T(8,128)(2,1)S(1)} %collective-permute-done.1.x1, bf16[256,128]{1,0:T(8,128)(2,1)S(1)} %collective-permute-done.2.x2), custom_call_target="tpu_custom_call" | custom-call | flops 134217728 | bytes 1048576 | tf_op jit(solution)/shard_map/forward_sibling/pallas_call | solution.py:189
  12.0 0.1 collective-permute-start.3
  12.1 0.4 %forward_mine.1 = f32[512,128]{1,0:T(8,128)S(1)} custom-call(bf16[1024,1024]{1,0:T(8,128)(2,1)S(1)} %densify.1.tile_ref, bf16[512,128]{1,0:T(8,128)(2,1)S(1)} %constant_dynamic-update-slice_fusion.outer_ref, bf16[256,128]{1,0:T(8,128)(2,1)S(1)} %collective-permute-done.1.x1, bf16[256,128]{1,0:T(8,128)(2,1)S(1)} %collective-permute-done.2.x2), custom_call_target="tpu_custom_call" | custom-call | flops 134217728 | bytes 1048576 | tf_op jit(solution)/shard_map/forward_mine/pallas_call | solution.py:189
  12.5 0.9 %collective-permute-done.3 = bf16[512,128]{1,0:T(8,128)(2,1)S(1)} collective-permute-done((bf16[512,128]{1,0:T(8,128)(2,1)S(1)}, bf16[512,128]{1,0:T(8,128)(2,1)S(1)}, u32[]{:S(2)}, u32[]{:S(2)}) %collective-permute-start.3) | collective-permute-done | bytes 131104 | tf_op jit(solution)/shard_map/ppermute | solution.py:299
  13.5 1.6 %collective-permute-start.5 = (bf16[512,128]{1,0:T(8,128)(2,1)S(1)}, bf16[512,128]{1,0:T(8,128)(2,1)S(1)}, u32[]{:S(2)}, u32[]{:S(2)}) collective-permute-start(bf16[512,128]{1,0:T(8,128)(2,1)S(1)} %add_convert_fusion.near_ref), channel_id=1, source_target_pairs={{0,2},{1,3},{2,0},{3,1},{4,6},{5,7},{6,4},{7,5},{8,10},{9,11},{10,... | collective-permute-start | bytes 393224 | tf_op jit(solution)/shard_map/ppermute | solution.py:299
  15.0 4.1 %collective-permute-done.5.far_ref = bf16[512,128]{1,0:T(8,128)(2,1)S(1)} collective-permute-done((bf16[512,128]{1,0:T(8,128)(2,1)S(1)}, bf16[512,128]{1,0:T(8,128)(2,1)S(1)}, u32[]{:S(2)}, u32[]{:S(2)}) %collective-permute-start.5) | collective-permute-done | bytes 131104 | tf_op jit(solution)/shard_map/ppermute | solution.py:299
  19.1 0.5 %layer.1 = (f32[256,256]{1,0:T(8,128)S(1)}, bf16[784,128]{1,0:T(8,128)(2,1)S(1)}) custom-call(bf16[512,128]{1,0:T(8,128)(2,1)S(1)} %add_convert_fusion.near_ref, bf16[512,128]{1,0:T(8,128)(2,1)S(1)} %collective-permute-done.5.far_ref, bf16[256,256]{1,0:T(8,128)(2,1)S(1)} %copy-done, bf16[256,256]{1,0:T(8,128)(2,1)S(1)} %collective-permute-done.4.cot_far_ref, ...), custom_call_target="tpu_custom_call" | custom-call | tf_op jit(solution)/shard_map/layer/pallas_call | solution.py:319
  19.6 0.1 collective-permute-start.6
  19.7 0.5 %backward_mine.1.part_ref = f32[4,256,128]{2,1,0:T(8,128)S(1)} custom-call(bf16[1024,1024]{1,0:T(8,128)(2,1)S(1)} %densify.1.tile_ref, bf16[784,128]{1,0:T(8,128)(2,1)S(1)} %get-tuple-element.26.own_ref), custom_call_target="tpu_custom_call" | custom-call | flops 134217728 | bytes 1048576 | tf_op jit(solution)/shard_map/backward_mine/pallas_call | solution.py:331
  20.2 0.9 %collective-permute-done.6.sib_ref = bf16[784,128]{1,0:T(8,128)(2,1)S(1)} collective-permute-done((bf16[784,128]{1,0:T(8,128)(2,1)S(1)}, bf16[784,128]{1,0:T(8,128)(2,1)S(1)}, u32[]{:S(2)}, u32[]{:S(2)}) %collective-permute-start.6) | collective-permute-done | bytes 200736 | tf_op jit(solution)/shard_map/ppermute | solution.py:299
  21.2 2.1 %collective-permute-start.9 = (bf16[144,128]{1,0:T(8,128)(2,1)S(1)}, bf16[144,128]{1,0:T(8,128)(2,1)S(1)}, u32[]{:S(2)}, u32[]{:S(2)}) collective-permute-start(bf16[144,128]{1,0:T(8,128)(2,1)S(1)} %stripe.1), channel_id=1, source_target_pairs={{0,8},{4,12},{8,0},{12,4},{1,9},{5,13},{9,1},{13,5},{2,10},{6,14},... | collective-permute-start | bytes 110600 | tf_op jit(solution)/shard_map/ppermute | solution.py:299
  23.3 0.5 %backward.1 = (f32[256,128]{1,0:T(8,128)S(1)}, bf16[256,128]{1,0:T(8,128)(2,1)S(1)}, bf16[256,128]{1,0:T(8,128)(2,1)S(1)}, bf16[256,128]{1,0:T(8,128)(2,1)S(1)}) custom-call(bf16[1024,1024]{1,0:T(8,128)(2,1)S(1)} %densify.1.tile_ref, bf16[784,128]{1,0:T(8,128)(2,1)S(1)} %get-tuple-element.26.own_ref, bf16[784,128]{1,0:T(8,128)(2,1)S(1)} %collective-permute-done.6.sib_ref, ...), custom_call_target="tpu_custom_call" | custom-call | tf_op jit(solution)/shard_map/backward/pallas_call | solution.py:350
  23.8 2.2 %collective-permute-start.7 = (bf16[256,128]{1,0:T(8,128)(2,1)S(1)}, bf16[256,128]{1,0:T(8,128)(2,1)S(1)}, u32[]{:S(2)}, u32[]{:S(2)}) collective-permute-start(bf16[256,128]{1,0:T(8,128)(2,1)S(1)} %get-tuple-element.30), channel_id=1, source_target_pairs={{0,4},{4,0},{8,12},{12,8},{1,5},{5,1},{9,13},{13,9},{2,6},{6,2},{1... | collective-permute-start | bytes 196616 | tf_op jit(solution)/shard_map/ppermute | solution.py:299
  26.0 0.1 collective-permute-start.8
  26.0 0.8 %collective-permute-done.9 = bf16[144,128]{1,0:T(8,128)(2,1)S(1)} collective-permute-done((bf16[144,128]{1,0:T(8,128)(2,1)S(1)}, bf16[144,128]{1,0:T(8,128)(2,1)S(1)}, u32[]{:S(2)}, u32[]{:S(2)}) %collective-permute-start.9) | collective-permute-done | bytes 36896 | tf_op jit(solution)/shard_map/ppermute | solution.py:299
  26.8 0.8 %collective-permute-start.11 = (bf16[144,128]{1,0:T(8,128)(2,1)S(1)}, bf16[144,128]{1,0:T(8,128)(2,1)S(1)}, u32[]{:S(2)}, u32[]{:S(2)}) collective-permute-start(bf16[144,128]{1,0:T(8,128)(2,1)S(1)} %add_convert_fusion.1.pair_ref), channel_id=1, source_target_pairs={{0,4},{4,0},{8,12},{12,8},{1,5},{5,1},{9,13},{13,9},{2,6},{6,2},{1... | collective-permute-start | bytes 110600 | tf_op jit(solution)/shard_map/ppermute | solution.py:299
  27.6 0.1 multiply_convert_fusion.act_ref
  27.7 2.9 %collective-permute-start.10 = (bf16[256,128]{1,0:T(8,128)(2,1)S(1)}, bf16[256,128]{1,0:T(8,128)(2,1)S(1)}, u32[]{:S(2)}, u32[]{:S(2)}) collective-permute-start(bf16[256,128]{1,0:T(8,128)(2,1)S(1)} %get-tuple-element.33), channel_id=1, source_target_pairs={{0,12},{4,8},{8,4},{12,0},{1,13},{5,9},{9,5},{13,1},{2,14},{6,10},... | collective-permute-start | bytes 196616 | tf_op jit(solution)/shard_map/ppermute | solution.py:299
  30.6 0.5 %collective-permute-done.11.pair_far_ref = bf16[144,128]{1,0:T(8,128)(2,1)S(1)} collective-permute-done((bf16[144,128]{1,0:T(8,128)(2,1)S(1)}, bf16[144,128]{1,0:T(8,128)(2,1)S(1)}, u32[]{:S(2)}, u32[]{:S(2)}) %collective-permute-start.11) | collective-permute-done | bytes 36896 | tf_op jit(solution)/shard_map/ppermute | solution.py:299
  31.1 0.1 collective-permute-start.12
  31.2 1.7 %collective-permute-done.8.got2 = bf16[256,128]{1,0:T(8,128)(2,1)S(1)} collective-permute-done((bf16[256,128]{1,0:T(8,128)(2,1)S(1)}, bf16[256,128]{1,0:T(8,128)(2,1)S(1)}, u32[]{:S(2)}, u32[]{:S(2)}) %collective-permute-start.8) | collective-permute-done | bytes 65568 | tf_op jit(solution)/shard_map/ppermute | solution.py:299
  32.9 1.0 %collective-permute-done.10.got3 = bf16[256,128]{1,0:T(8,128)(2,1)S(1)} collective-permute-done((bf16[256,128]{1,0:T(8,128)(2,1)S(1)}, bf16[256,128]{1,0:T(8,128)(2,1)S(1)}, u32[]{:S(2)}, u32[]{:S(2)}) %collective-permute-start.10) | collective-permute-done | bytes 65568 | tf_op jit(solution)/shard_map/ppermute | solution.py:299
  33.9 0.8 %last.1 = (bf16[256,128]{1,0:T(8,128)(2,1)}, bf16[256,256]{1,0:T(8,128)(2,1)}, f32[128,256]{1,0:T(8,128)}, f32[1,256]{1,0:T(1,128)}) custom-call(f32[256,128]{1,0:T(8,128)S(1)} %get-tuple-element.29.keep_ref, bf16[256,128]{1,0:T(8,128)(2,1)S(1)} %collective-permute-done.7.got1, bf16[256,128]{1,0:T(8,128)(2,1)S(1)} %collective-permute-done.8.got2, ...), custom_call_target="tpu_custom_call" | custom-call | tf_op jit(solution)/shard_map/last/pallas_call | solution.py:368
  (16 shorter events, 0.1 us)
Async XLA Ops:
  0.6 10.7 %copy-start.3 = (bf16[256,128]{1,0:T(8,128)(2,1)S(1)}, bf16[256,128]{1,0:T(8,128)(2,1)}, u32[]{:S(2)}) copy-start(bf16[256,128]{1,0:T(8,128)(2,1)} %param.8) | copy-start | bytes 196612
  0.6 10.8 %collective-permute-start = (bf16[256,128]{1,0:T(8,128)(2,1)}, bf16[256,128]{1,0:T(8,128)(2,1)S(1)}, u32[]{:S(2)}, u32[]{:S(2)}) collective-permute-start(bf16[256,128]{1,0:T(8,128)(2,1)} %param.8), channel_id=1, source_target_pairs={{0,12},{4,8},{8,4},{12,0},{1,13},{5,9},{9,5},{13,1},{2,14},{6,10},... | collective-permute-start | bytes 196616 | tf_op jit(solution)/shard_map/ppermute | solution.py:299
  5.8 5.8 %collective-permute-start.2 = (bf16[256,128]{1,0:T(8,128)(2,1)}, bf16[256,128]{1,0:T(8,128)(2,1)S(1)}, u32[]{:S(2)}, u32[]{:S(2)}) collective-permute-start(bf16[256,128]{1,0:T(8,128)(2,1)} %param.8), channel_id=1, source_target_pairs={{0,8},{4,12},{8,0},{12,4},{1,9},{5,13},{9,1},{13,5},{2,10},{6,14},... | collective-permute-start | bytes 196616 | tf_op jit(solution)/shard_map/ppermute | solution.py:299
  5.8 5.8 %collective-permute-start.1 = (bf16[256,128]{1,0:T(8,128)(2,1)}, bf16[256,128]{1,0:T(8,128)(2,1)S(1)}, u32[]{:S(2)}, u32[]{:S(2)}) collective-permute-start(bf16[256,128]{1,0:T(8,128)(2,1)} %param.8), channel_id=1, source_target_pairs={{0,4},{4,0},{8,12},{12,8},{1,5},{5,1},{9,13},{13,9},{2,6},{6,2},{1... | collective-permute-start | bytes 196616 | tf_op jit(solution)/shard_map/ppermute | solution.py:299
  6.4 6.1 %collective-permute-start.4 = (bf16[256,256]{1,0:T(8,128)(2,1)}, bf16[256,256]{1,0:T(8,128)(2,1)S(1)}, u32[]{:S(2)}, u32[]{:S(2)}) collective-permute-start(bf16[256,256]{1,0:T(8,128)(2,1)} %cot_ref.1), channel_id=1, source_target_pairs={{0,2},{1,3},{2,0},{3,1},{4,6},{5,7},{6,4},{7,5},{8,10},{9,11},{10,... | collective-permute-start | bytes 393224 | tf_op jit(solution)/shard_map/ppermute | solution.py:299
  11.4 7.7 %copy-start = (bf16[256,256]{1,0:T(8,128)(2,1)S(1)}, bf16[256,256]{1,0:T(8,128)(2,1)}, u32[]{:S(2)}) copy-start(bf16[256,256]{1,0:T(8,128)(2,1)} %cot_ref.1) | copy-start | bytes 393220
  11.4 7.7 %copy-start.1 = (bf16[128,256]{1,0:T(8,128)(2,1)S(1)}, bf16[128,256]{1,0:T(8,128)(2,1)}, u32[]{:S(2)}) copy-start(bf16[128,256]{1,0:T(8,128)(2,1)} %weight_ref.1) | copy-start | bytes 196612
  11.4 7.7 %copy-start.2 = (f32[256]{0:T(256)S(1)}, f32[256]{0:T(256)}, u32[]{:S(2)}) copy-start(f32[256]{0:T(256)} %param.14) | copy-start | bytes 3076
  12.0 1.4 %collective-permute-start.3 = (bf16[512,128]{1,0:T(8,128)(2,1)S(1)}, bf16[512,128]{1,0:T(8,128)(2,1)S(1)}, u32[]{:S(2)}, u32[]{:S(2)}) collective-permute-start(bf16[512,128]{1,0:T(8,128)(2,1)S(1)} %forward_sibling.1), channel_id=1, source_target_pairs={{0,1},{1,0},{2,3},{3,2},{4,5},{5,4},{6,7},{7,6},{8,9},{9,8},{10,11... | collective-permute-start | bytes 393224 | tf_op jit(solution)/shard_map/ppermute | solution.py:299
  13.5 5.6 %collective-permute-start.5 = (bf16[512,128]{1,0:T(8,128)(2,1)S(1)}, bf16[512,128]{1,0:T(8,128)(2,1)S(1)}, u32[]{:S(2)}, u32[]{:S(2)}) collective-permute-start(bf16[512,128]{1,0:T(8,128)(2,1)S(1)} %add_convert_fusion.near_ref), channel_id=1, source_target_pairs={{0,2},{1,3},{2,0},{3,1},{4,6},{5,7},{6,4},{7,5},{8,10},{9,11},{10,... | collective-permute-start | bytes 393224 | tf_op jit(solution)/shard_map/ppermute | solution.py:299
  19.6 1.5 %collective-permute-start.6 = (bf16[784,128]{1,0:T(8,128)(2,1)S(1)}, bf16[784,128]{1,0:T(8,128)(2,1)S(1)}, u32[]{:S(2)}, u32[]{:S(2)}) collective-permute-start(bf16[784,128]{1,0:T(8,128)(2,1)S(1)} %get-tuple-element.26.own_ref), channel_id=1, source_target_pairs={{0,1},{1,0},{2,3},{3,2},{4,5},{5,4},{6,7},{7,6},{8,9},{9,8},{10,11... | collective-permute-start | bytes 602120 | tf_op jit(solution)/shard_map/ppermute | solution.py:299
  21.2 5.6 %collective-permute-start.9 = (bf16[144,128]{1,0:T(8,128)(2,1)S(1)}, bf16[144,128]{1,0:T(8,128)(2,1)S(1)}, u32[]{:S(2)}, u32[]{:S(2)}) collective-permute-start(bf16[144,128]{1,0:T(8,128)(2,1)S(1)} %stripe.1), channel_id=1, source_target_pairs={{0,8},{4,12},{8,0},{12,4},{1,9},{5,13},{9,1},{13,5},{2,10},{6,14},... | collective-permute-start | bytes 110600 | tf_op jit(solution)/shard_map/ppermute | solution.py:299
  23.8 7.4 %collective-permute-start.7 = (bf16[256,128]{1,0:T(8,128)(2,1)S(1)}, bf16[256,128]{1,0:T(8,128)(2,1)S(1)}, u32[]{:S(2)}, u32[]{:S(2)}) collective-permute-start(bf16[256,128]{1,0:T(8,128)(2,1)S(1)} %get-tuple-element.30), channel_id=1, source_target_pairs={{0,4},{4,0},{8,12},{12,8},{1,5},{5,1},{9,13},{13,9},{2,6},{6,2},{1... | collective-permute-start | bytes 196616 | tf_op jit(solution)/shard_map/ppermute | solution.py:299
  26.0 6.9 %collective-permute-start.8 = (bf16[256,128]{1,0:T(8,128)(2,1)S(1)}, bf16[256,128]{1,0:T(8,128)(2,1)S(1)}, u32[]{:S(2)}, u32[]{:S(2)}) collective-permute-start(bf16[256,128]{1,0:T(8,128)(2,1)S(1)} %get-tuple-element.31), channel_id=1, source_target_pairs={{0,8},{4,12},{8,0},{12,4},{1,9},{5,13},{9,1},{13,5},{2,10},{6,14},... | collective-permute-start | bytes 196616 | tf_op jit(solution)/shard_map/ppermute | solution.py:299
  26.8 4.3 %collective-permute-start.11 = (bf16[144,128]{1,0:T(8,128)(2,1)S(1)}, bf16[144,128]{1,0:T(8,128)(2,1)S(1)}, u32[]{:S(2)}, u32[]{:S(2)}) collective-permute-start(bf16[144,128]{1,0:T(8,128)(2,1)S(1)} %add_convert_fusion.1.pair_ref), channel_id=1, source_target_pairs={{0,4},{4,0},{8,12},{12,8},{1,5},{5,1},{9,13},{13,9},{2,6},{6,2},{1... | collective-permute-start | bytes 110600 | tf_op jit(solution)/shard_map/ppermute | solution.py:299
  27.7 6.2 %collective-permute-start.10 = (bf16[256,128]{1,0:T(8,128)(2,1)S(1)}, bf16[256,128]{1,0:T(8,128)(2,1)S(1)}, u32[]{:S(2)}, u32[]{:S(2)}) collective-permute-start(bf16[256,128]{1,0:T(8,128)(2,1)S(1)} %get-tuple-element.33), channel_id=1, source_target_pairs={{0,12},{4,8},{8,4},{12,0},{1,13},{5,9},{9,5},{13,1},{2,14},{6,10},... | collective-permute-start | bytes 196616 | tf_op jit(solution)/shard_map/ppermute | solution.py:299
  31.1 2.8 %collective-permute-start.12 = (f32[128,128]{1,0:T(8,128)S(1)}, f32[128,128]{1,0:T(8,128)S(1)}, u32[]{:S(2)}, u32[]{:S(2)}) collective-permute-start(f32[128,128]{1,0:T(8,128)S(1)} %convert_add_fusion.half_ref), channel_id=1, source_target_pairs={{0,1},{1,0},{2,3},{3,2},{4,5},{5,4},{6,7},{7,6},{8,9},{9,8},{10,11... | collective-permute-start | bytes 196616 | tf_op jit(solution)/shard_map/ppermute | solution.py:299

commit v8 on v7

--- a/solution.py
+++ b/solution.py
@@ -255,12 +255,37 @@
         part_ref[k] = backward_terms(tile_ref, core, k, own_ref, part_ref.shape[1])
 
 
-def backward_kernel(tile_ref, own_ref, sib_ref, part_ref, keep_ref, send1, send2, send3):
+def turn_kernel(tile_ref, turned_ref):
     core = lax.rem(lax.axis_index("col"), 2)
-    rows = keep_ref.shape[0]
-    for k, out in ((1, send1), (2, send2), (3, send3), (0, keep_ref)):
-        total = part_ref[k] + backward_terms(tile_ref, 1 - core, k, sib_ref, rows)
+    width = turned_ref.shape[1] // 2
+    for x in range(2):
+        row_at = pl.multiple_of((2 * x + 1 - core) * width, width)
+        for c in range(turned_ref.shape[0] // width):
+            lanes = slice(c * width, (c + 1) * width)
+            turned_ref[lanes, x * width : (x + 1) * width] = tile_ref[pl.ds(row_at, width), lanes].T
+
+
+def backward_kernel(offsets, turned_ref, sib_ref, part_ref, *outs):
+    row = lax.axis_index("row")
+    rows = part_ref.shape[1]
+    for k, out in zip(offsets, outs):
+        at = pl.multiple_of(jnp.bitwise_xor(row, k) * rows, rows)
+        total = part_ref[k] + jnp.dot(
+            turned_ref[pl.ds(at, rows), :], sib_ref[pl.ds(0, 2 * rows), :], preferred_element_type=F32
+        )
         out[...] = total.astype(out.dtype)
+
+
+def backward(offsets, turned, sib, part):
+    _, rows, width_in = part.shape
+    return pl.pallas_call(
+        functools.partial(backward_kernel, offsets),
+        in_specs=[WHOLE] * 3,
+        out_specs=[WHOLE] * len(offsets),
+        out_shape=[jax.ShapeDtypeStruct((rows, width_in), BF16 if k else F32) for k in offsets],
+        compiler_params=LIMIT,
+        name="backward",
+    )(turned, sib, part)
 
 
 def stripe_kernel(own_ref, sib_ref, stripe_ref):
@@ -315,7 +340,16 @@
     keep = forward(True, tile, outer, shards)
     sib, cot_far = lax.optimization_barrier((swap(send, "col", 1), cot_far))
     near = (keep + sib.astype(F32)).astype(BF16)
-    far = swap(near, "col", 2)
+    near, tile = lax.optimization_barrier((near, tile))
+    turned = pl.pallas_call(
+        turn_kernel,
+        in_specs=[WHOLE],
+        out_specs=WHOLE,
+        out_shape=jax.ShapeDtypeStruct((ROWS * node_rows, 2 * node_rows), BF16),
+        compiler_params=LIMIT,
+        name="turn",
+    )(tile)
+    far, turned = lax.optimization_barrier((swap(near, "col", 2), turned))
     pre_act, grads = pl.pallas_call(
         layer_kernel,
         in_specs=[WHOLE] * 6,
@@ -347,14 +381,10 @@
         name="stripe",
     )(grads, grads_sib)
     stripe_far = swap(stripe, "row", 2)
-    own, *sends = pl.pallas_call(
-        backward_kernel,
-        in_specs=[WHOLE] * 4,
-        out_specs=[WHOLE] * 4,
-        out_shape=[jax.ShapeDtypeStruct(block.shape, F32)] + [block] * 3,
-        compiler_params=LIMIT,
-        name="backward",
-    )(tile, grads, grads_sib, part)
+    first, second = backward((1, 2), turned, grads_sib, part)
+    third, own = backward((3, 0), turned, grads_sib, part)
+    stripe_far, third = lax.optimization_barrier((stripe_far, third))
+    sends = [first, second, third]
     pair = (stripe.astype(F32) + stripe_far.astype(F32)).astype(BF16)
     pair, sends[2] = lax.optimization_barrier((pair, sends[2]))
     got = [swap(send, "row", k) for k, send in zip((1, 2, 3), sends)]

time: 34.8 us -> 34.7 us (level)
  Pallas kernels: 5.88 us -> 6.25 us
  waiting for transfers between devices: 10 us -> 9.63 us
    ppermute x13, waiting for transfers between devices: 10 us -> 9.63 us  [swap(): return lax.ppermute(array, axis, [(i, i ^ bit) for i in range(size)])]
    pallas_call x1 -> x3, Pallas kernels: 0.51 us -> 0.89 us  [the longest x2 0.57 us: backward(): pl.pallas_call(functools.partial(backward_kernel, offsets), in_specs=[WHO...]
  transfers between devices with their start and end apart: 13 -> 13, of which waited for: 8 -> 8; matrix products, arithmetic and copies ran while one was open for 0% -> 0% of each run, Pallas kernels for 13% -> 14%
where the time goes in v8:
time: 34.7 us; the launch traced here: 34.6 us
  starting transfers between devices  17.1 us (49%)
  waiting for transfers between devices  9.63 us (28%)
  Pallas kernels  6.25 us (18%)
  between operations  1.46 us (4%)
    ppermute x13, starting transfers between devices, swap(): return lax.ppermute(array, axis, [(i, i ^ bit) for i in range(size)])  17.1 us
    ppermute x13, waiting for transfers between devices, swap(): return lax.ppermute(array, axis, [(i, i ^ bit) for i in range(size)])  9.63 us
    pallas_call x1, Pallas kernels, densify(): pl.pallas_call(functools.partial(densify_kernel, chunks, row_blocks, col_...  2.67 us
    pallas_call x2, Pallas kernels, forward(): pl.pallas_call(functools.partial(forward_kernel, mine), in_specs=[WHOLE]...  0.85 us
    pallas_call x1, Pallas kernels, dense_tile(): pl.pallas_call(functools.partial(last_kernel, norm_scale), in_specs=[WHOL...  0.76 us
  transfers between devices with their start and end apart: 13, of which 8 were waited for; matrix products, arithmetic and copies ran while one was open for 0% of the time, Pallas kernels for 14%

profile of v8, /device:TPU:0, one launch (start us, length us, event | category | flops | bytes accessed | tf_op | source)
XLA Modules:
  0.0 34.6 jit_solution(3423855282567179147)
XLA Ops:
  0.6 5.1 %collective-permute-start = (bf16[256,128]{1,0:T(8,128)(2,1)}, bf16[256,128]{1,0:T(8,128)(2,1)S(1)}, u32[]{:S(2)}, u32[]{:S(2)}) collective-permute-start(bf16[256,128]{1,0:T(8,128)(2,1)} %param.8), channel_id=1, source_target_pairs={{0,12},{4,8},{8,4},{12,0},{1,13},{5,9},{9,5},{13,1},{2,14},{6,10},... | collective-permute-start | bytes 196616 | tf_op jit(solution)/shard_map/ppermute | solution.py:324
  5.8 0.6 %collective-permute-start.1 = (bf16[256,128]{1,0:T(8,128)(2,1)}, bf16[256,128]{1,0:T(8,128)(2,1)S(1)}, u32[]{:S(2)}, u32[]{:S(2)}) collective-permute-start(bf16[256,128]{1,0:T(8,128)(2,1)} %param.8), channel_id=1, source_target_pairs={{0,4},{4,0},{8,12},{12,8},{1,5},{5,1},{9,13},{13,9},{2,6},{6,2},{1... | collective-permute-start | bytes 196616 | tf_op jit(solution)/shard_map/ppermute | solution.py:324
  6.4 1.6 %collective-permute-start.4 = (bf16[256,256]{1,0:T(8,128)(2,1)}, bf16[256,256]{1,0:T(8,128)(2,1)S(1)}, u32[]{:S(2)}, u32[]{:S(2)}) collective-permute-start(bf16[256,256]{1,0:T(8,128)(2,1)} %cot_ref.1), channel_id=1, source_target_pairs={{0,2},{1,3},{2,0},{3,1},{4,6},{5,7},{6,4},{7,5},{8,10},{9,11},{10,... | collective-permute-start | bytes 393224 | tf_op jit(solution)/shard_map/ppermute | solution.py:324
  8.7 2.7 %densify.1.tile_ref = bf16[1024,1024]{1,0:T(8,128)(2,1)S(1)} custom-call(s32[1,1]{1,0:T(1,128)} %bitcast.3.count_in, s32[128]{0:T(128)} %rows_in.1, s32[128]{0:T(128)} %cols_in.1, bf16[128,128,128]{2,1,0:T(8,128)(2,1)} %values_ref.1), custom_call_target="tpu_custom_call" | custom-call | flops 2097152 | bytes 4194304 | tf_op jit(solution)/shard_map/densify/pallas_call | solution.py:151
  11.4 0.0 copy-start
  11.4 0.0 copy-start.2
  11.5 0.1 collective-permute-done.2.x2
  11.6 0.4 %forward_sibling.1 = bf16[512,128]{1,0:T(8,128)(2,1)S(1)} custom-call(bf16[1024,1024]{1,0:T(8,128)(2,1)S(1)} %densify.1.tile_ref, bf16[512,128]{1,0:T(8,128)(2,1)S(1)} %constant_dynamic-update-slice_fusion.outer_ref, bf16[256,128]{1,0:T(8,128)(2,1)S(1)} %collective-permute-done.1.x1, bf16[256,128]{1,0:T(8,128)(2,1)S(1)} %collective-permute-done.2.x2), custom_call_target="tpu_custom_call" | custom-call | flops 134217728 | bytes 1048576 | tf_op jit(solution)/shard_map/forward_sibling/pallas_call | solution.py:189
  12.0 0.1 collective-permute-start.3
  12.1 0.4 %forward_mine.1 = f32[512,128]{1,0:T(8,128)S(1)} custom-call(bf16[1024,1024]{1,0:T(8,128)(2,1)S(1)} %densify.1.tile_ref, bf16[512,128]{1,0:T(8,128)(2,1)S(1)} %constant_dynamic-update-slice_fusion.outer_ref, bf16[256,128]{1,0:T(8,128)(2,1)S(1)} %collective-permute-done.1.x1, bf16[256,128]{1,0:T(8,128)(2,1)S(1)} %collective-permute-done.2.x2), custom_call_target="tpu_custom_call" | custom-call | flops 134217728 | bytes 1048576 | tf_op jit(solution)/shard_map/forward_mine/pallas_call | solution.py:189
  12.5 0.9 %collective-permute-done.3 = bf16[512,128]{1,0:T(8,128)(2,1)S(1)} collective-permute-done((bf16[512,128]{1,0:T(8,128)(2,1)S(1)}, bf16[512,128]{1,0:T(8,128)(2,1)S(1)}, u32[]{:S(2)}, u32[]{:S(2)}) %collective-permute-start.3) | collective-permute-done | bytes 131104 | tf_op jit(solution)/shard_map/ppermute | solution.py:324
  13.4 1.6 %collective-permute-start.5 = (bf16[512,128]{1,0:T(8,128)(2,1)S(1)}, bf16[512,128]{1,0:T(8,128)(2,1)S(1)}, u32[]{:S(2)}, u32[]{:S(2)}) collective-permute-start(bf16[512,128]{1,0:T(8,128)(2,1)S(1)} %add_convert_fusion.near_ref), channel_id=1, source_target_pairs={{0,2},{1,3},{2,0},{3,1},{4,6},{5,7},{6,4},{7,5},{8,10},{9,11},{10,... | collective-permute-start | bytes 393224 | tf_op jit(solution)/shard_map/ppermute | solution.py:324
  15.0 0.3 turn.1.turned_ref
  15.3 3.7 %collective-permute-done.5.far_ref = bf16[512,128]{1,0:T(8,128)(2,1)S(1)} collective-permute-done((bf16[512,128]{1,0:T(8,128)(2,1)S(1)}, bf16[512,128]{1,0:T(8,128)(2,1)S(1)}, u32[]{:S(2)}, u32[]{:S(2)}) %collective-permute-start.5) | collective-permute-done | bytes 131104 | tf_op jit(solution)/shard_map/ppermute | solution.py:324
  19.1 0.5 %layer.1 = (f32[256,256]{1,0:T(8,128)S(1)}, bf16[784,128]{1,0:T(8,128)(2,1)S(1)}) custom-call(bf16[512,128]{1,0:T(8,128)(2,1)S(1)} %add_convert_fusion.near_ref, bf16[512,128]{1,0:T(8,128)(2,1)S(1)} %collective-permute-done.5.far_ref, bf16[256,256]{1,0:T(8,128)(2,1)S(1)} %copy-done, bf16[256,256]{1,0:T(8,128)(2,1)S(1)} %collective-permute-done.4.cot_far_ref, ...), custom_call_target="tpu_custom_call" | custom-call | tf_op jit(solution)/shard_map/layer/pallas_call | solution.py:353
  19.6 0.1 collective-permute-start.6
  19.7 0.5 %backward_mine.1.part_ref = f32[4,256,128]{2,1,0:T(8,128)S(1)} custom-call(bf16[1024,1024]{1,0:T(8,128)(2,1)S(1)} %densify.1.tile_ref, bf16[784,128]{1,0:T(8,128)(2,1)S(1)} %get-tuple-element.36.own_ref), custom_call_target="tpu_custom_call" | custom-call | flops 134217728 | bytes 1048576 | tf_op jit(solution)/shard_map/backward_mine/pallas_call | solution.py:365
  20.2 0.9 %collective-permute-done.6.sib_ref = bf16[784,128]{1,0:T(8,128)(2,1)S(1)} collective-permute-done((bf16[784,128]{1,0:T(8,128)(2,1)S(1)}, bf16[784,128]{1,0:T(8,128)(2,1)S(1)}, u32[]{:S(2)}, u32[]{:S(2)}) %collective-permute-start.6) | collective-permute-done | bytes 200736 | tf_op jit(solution)/shard_map/ppermute | solution.py:324
  21.2 2.2 %collective-permute-start.9 = (bf16[144,128]{1,0:T(8,128)(2,1)S(1)}, bf16[144,128]{1,0:T(8,128)(2,1)S(1)}, u32[]{:S(2)}, u32[]{:S(2)}) collective-permute-start(bf16[144,128]{1,0:T(8,128)(2,1)S(1)} %stripe.1), channel_id=1, source_target_pairs={{0,8},{4,12},{8,0},{12,4},{1,9},{5,13},{9,1},{13,5},{2,10},{6,14},... | collective-permute-start | bytes 110600 | tf_op jit(solution)/shard_map/ppermute | solution.py:324
  23.3 0.3 backward.3
  23.6 0.3 backward.2
  23.9 2.0 %collective-permute-start.7 = (bf16[256,128]{1,0:T(8,128)(2,1)S(1)}, bf16[256,128]{1,0:T(8,128)(2,1)S(1)}, u32[]{:S(2)}, u32[]{:S(2)}) collective-permute-start(bf16[256,128]{1,0:T(8,128)(2,1)S(1)} %get-tuple-element.40), channel_id=1, source_target_pairs={{0,4},{4,0},{8,12},{12,8},{1,5},{5,1},{9,13},{13,9},{2,6},{6,2},{1... | collective-permute-start | bytes 196616 | tf_op jit(solution)/shard_map/ppermute | solution.py:324
  25.9 0.1 collective-permute-start.8
  26.1 0.8 %collective-permute-done.9 = bf16[144,128]{1,0:T(8,128)(2,1)S(1)} collective-permute-done((bf16[144,128]{1,0:T(8,128)(2,1)S(1)}, bf16[144,128]{1,0:T(8,128)(2,1)S(1)}, u32[]{:S(2)}, u32[]{:S(2)}) %collective-permute-start.9) | collective-permute-done | bytes 36896 | tf_op jit(solution)/shard_map/ppermute | solution.py:324
  26.9 0.7 %collective-permute-start.11 = (bf16[144,128]{1,0:T(8,128)(2,1)S(1)}, bf16[144,128]{1,0:T(8,128)(2,1)S(1)}, u32[]{:S(2)}, u32[]{:S(2)}) collective-permute-start(bf16[144,128]{1,0:T(8,128)(2,1)S(1)} %add_convert_fusion.1.pair_ref), channel_id=1, source_target_pairs={{0,4},{4,0},{8,12},{12,8},{1,5},{5,1},{9,13},{13,9},{2,6},{6,2},{1... | collective-permute-start | bytes 110600 | tf_op jit(solution)/shard_map/ppermute | solution.py:324
  27.5 0.1 multiply_convert_fusion.act_ref
  27.6 2.9 %collective-permute-start.10 = (bf16[256,128]{1,0:T(8,128)(2,1)S(1)}, bf16[256,128]{1,0:T(8,128)(2,1)S(1)}, u32[]{:S(2)}, u32[]{:S(2)}) collective-permute-start(bf16[256,128]{1,0:T(8,128)(2,1)S(1)} %get-tuple-element.45), channel_id=1, source_target_pairs={{0,12},{4,8},{8,4},{12,0},{1,13},{5,9},{9,5},{13,1},{2,14},{6,10},... | collective-permute-start | bytes 196616 | tf_op jit(solution)/shard_map/ppermute | solution.py:324
  30.6 1.4 %collective-permute-done.11.pair_far_ref = bf16[144,128]{1,0:T(8,128)(2,1)S(1)} collective-permute-done((bf16[144,128]{1,0:T(8,128)(2,1)S(1)}, bf16[144,128]{1,0:T(8,128)(2,1)S(1)}, u32[]{:S(2)}, u32[]{:S(2)}) %collective-permute-start.11) | collective-permute-done | bytes 36896 | tf_op jit(solution)/shard_map/ppermute | solution.py:324
  32.0 0.1 collective-permute-start.12
  32.1 0.8 %collective-permute-done.8.got2 = bf16[256,128]{1,0:T(8,128)(2,1)S(1)} collective-permute-done((bf16[256,128]{1,0:T(8,128)(2,1)S(1)}, bf16[256,128]{1,0:T(8,128)(2,1)S(1)}, u32[]{:S(2)}, u32[]{:S(2)}) %collective-permute-start.8) | collective-permute-done | bytes 65568 | tf_op jit(solution)/shard_map/ppermute | solution.py:324
  32.9 1.0 %collective-permute-done.10.got3 = bf16[256,128]{1,0:T(8,128)(2,1)S(1)} collective-permute-done((bf16[256,128]{1,0:T(8,128)(2,1)S(1)}, bf16[256,128]{1,0:T(8,128)(2,1)S(1)}, u32[]{:S(2)}, u32[]{:S(2)}) %collective-permute-start.10) | collective-permute-done | bytes 65568 | tf_op jit(solution)/shard_map/ppermute | solution.py:324
  33.8 0.8 %last.1 = (bf16[256,128]{1,0:T(8,128)(2,1)}, bf16[256,256]{1,0:T(8,128)(2,1)}, f32[128,256]{1,0:T(8,128)}, f32[1,256]{1,0:T(1,128)}) custom-call(f32[256,128]{1,0:T(8,128)S(1)} %get-tuple-element.39.keep_ref, bf16[256,128]{1,0:T(8,128)(2,1)S(1)} %collective-permute-done.7.got1, bf16[256,128]{1,0:T(8,128)(2,1)S(1)} %collective-permute-done.8.got2, ...), custom_call_target="tpu_custom_call" | custom-call | tf_op jit(solution)/shard_map/last/pallas_call | solution.py:398
  (18 shorter events, 0.1 us)
Async XLA Ops:
  0.6 10.7 %copy-start.3 = (bf16[256,128]{1,0:T(8,128)(2,1)S(1)}, bf16[256,128]{1,0:T(8,128)(2,1)}, u32[]{:S(2)}) copy-start(bf16[256,128]{1,0:T(8,128)(2,1)} %param.8) | copy-start | bytes 196612
  0.6 10.7 %collective-permute-start = (bf16[256,128]{1,0:T(8,128)(2,1)}, bf16[256,128]{1,0:T(8,128)(2,1)S(1)}, u32[]{:S(2)}, u32[]{:S(2)}) collective-permute-start(bf16[256,128]{1,0:T(8,128)(2,1)} %param.8), channel_id=1, source_target_pairs={{0,12},{4,8},{8,4},{12,0},{1,13},{5,9},{9,5},{13,1},{2,14},{6,10},... | collective-permute-start | bytes 196616 | tf_op jit(solution)/shard_map/ppermute | solution.py:324
  5.8 5.8 %collective-permute-start.2 = (bf16[256,128]{1,0:T(8,128)(2,1)}, bf16[256,128]{1,0:T(8,128)(2,1)S(1)}, u32[]{:S(2)}, u32[]{:S(2)}) collective-permute-start(bf16[256,128]{1,0:T(8,128)(2,1)} %param.8), channel_id=1, source_target_pairs={{0,8},{4,12},{8,0},{12,4},{1,9},{5,13},{9,1},{13,5},{2,10},{6,14},... | collective-permute-start | bytes 196616 | tf_op jit(solution)/shard_map/ppermute | solution.py:324
  5.8 5.8 %collective-permute-start.1 = (bf16[256,128]{1,0:T(8,128)(2,1)}, bf16[256,128]{1,0:T(8,128)(2,1)S(1)}, u32[]{:S(2)}, u32[]{:S(2)}) collective-permute-start(bf16[256,128]{1,0:T(8,128)(2,1)} %param.8), channel_id=1, source_target_pairs={{0,4},{4,0},{8,12},{12,8},{1,5},{5,1},{9,13},{13,9},{2,6},{6,2},{1... | collective-permute-start | bytes 196616 | tf_op jit(solution)/shard_map/ppermute | solution.py:324
  6.4 6.1 %collective-permute-start.4 = (bf16[256,256]{1,0:T(8,128)(2,1)}, bf16[256,256]{1,0:T(8,128)(2,1)S(1)}, u32[]{:S(2)}, u32[]{:S(2)}) collective-permute-start(bf16[256,256]{1,0:T(8,128)(2,1)} %cot_ref.1), channel_id=1, source_target_pairs={{0,2},{1,3},{2,0},{3,1},{4,6},{5,7},{6,4},{7,5},{8,10},{9,11},{10,... | collective-permute-start | bytes 393224 | tf_op jit(solution)/shard_map/ppermute | solution.py:324
  11.4 7.7 %copy-start = (bf16[256,256]{1,0:T(8,128)(2,1)S(1)}, bf16[256,256]{1,0:T(8,128)(2,1)}, u32[]{:S(2)}) copy-start(bf16[256,256]{1,0:T(8,128)(2,1)} %cot_ref.1) | copy-start | bytes 393220
  11.4 7.6 %copy-start.1 = (bf16[128,256]{1,0:T(8,128)(2,1)S(1)}, bf16[128,256]{1,0:T(8,128)(2,1)}, u32[]{:S(2)}) copy-start(bf16[128,256]{1,0:T(8,128)(2,1)} %weight_ref.1) | copy-start | bytes 196612
  11.4 7.6 %copy-start.2 = (f32[256]{0:T(256)S(1)}, f32[256]{0:T(256)}, u32[]{:S(2)}) copy-start(f32[256]{0:T(256)} %param.14) | copy-start | bytes 3076
  12.0 1.4 %collective-permute-start.3 = (bf16[512,128]{1,0:T(8,128)(2,1)S(1)}, bf16[512,128]{1,0:T(8,128)(2,1)S(1)}, u32[]{:S(2)}, u32[]{:S(2)}) collective-permute-start(bf16[512,128]{1,0:T(8,128)(2,1)S(1)} %forward_sibling.1), channel_id=1, source_target_pairs={{0,1},{1,0},{2,3},{3,2},{4,5},{5,4},{6,7},{7,6},{8,9},{9,8},{10,11... | collective-permute-start | bytes 393224 | tf_op jit(solution)/shard_map/ppermute | solution.py:324
  13.4 5.6 %collective-permute-start.5 = (bf16[512,128]{1,0:T(8,128)(2,1)S(1)}, bf16[512,128]{1,0:T(8,128)(2,1)S(1)}, u32[]{:S(2)}, u32[]{:S(2)}) collective-permute-start(bf16[512,128]{1,0:T(8,128)(2,1)S(1)} %add_convert_fusion.near_ref), channel_id=1, source_target_pairs={{0,2},{1,3},{2,0},{3,1},{4,6},{5,7},{6,4},{7,5},{8,10},{9,11},{10,... | collective-permute-start | bytes 393224 | tf_op jit(solution)/shard_map/ppermute | solution.py:324
  19.6 1.5 %collective-permute-start.6 = (bf16[784,128]{1,0:T(8,128)(2,1)S(1)}, bf16[784,128]{1,0:T(8,128)(2,1)S(1)}, u32[]{:S(2)}, u32[]{:S(2)}) collective-permute-start(bf16[784,128]{1,0:T(8,128)(2,1)S(1)} %get-tuple-element.36.own_ref), channel_id=1, source_target_pairs={{0,1},{1,0},{2,3},{3,2},{4,5},{5,4},{6,7},{7,6},{8,9},{9,8},{10,11... | collective-permute-start | bytes 602120 | tf_op jit(solution)/shard_map/ppermute | solution.py:324
  21.2 5.7 %collective-permute-start.9 = (bf16[144,128]{1,0:T(8,128)(2,1)S(1)}, bf16[144,128]{1,0:T(8,128)(2,1)S(1)}, u32[]{:S(2)}, u32[]{:S(2)}) collective-permute-start(bf16[144,128]{1,0:T(8,128)(2,1)S(1)} %stripe.1), channel_id=1, source_target_pairs={{0,8},{4,12},{8,0},{12,4},{1,9},{5,13},{9,1},{13,5},{2,10},{6,14},... | collective-permute-start | bytes 110600 | tf_op jit(solution)/shard_map/ppermute | solution.py:324
  23.9 8.2 %collective-permute-start.7 = (bf16[256,128]{1,0:T(8,128)(2,1)S(1)}, bf16[256,128]{1,0:T(8,128)(2,1)S(1)}, u32[]{:S(2)}, u32[]{:S(2)}) collective-permute-start(bf16[256,128]{1,0:T(8,128)(2,1)S(1)} %get-tuple-element.40), channel_id=1, source_target_pairs={{0,4},{4,0},{8,12},{12,8},{1,5},{5,1},{9,13},{13,9},{2,6},{6,2},{1... | collective-permute-start | bytes 196616 | tf_op jit(solution)/shard_map/ppermute | solution.py:324
  25.9 6.9 %collective-permute-start.8 = (bf16[256,128]{1,0:T(8,128)(2,1)S(1)}, bf16[256,128]{1,0:T(8,128)(2,1)S(1)}, u32[]{:S(2)}, u32[]{:S(2)}) collective-permute-start(bf16[256,128]{1,0:T(8,128)(2,1)S(1)} %get-tuple-element.41), channel_id=1, source_target_pairs={{0,8},{4,12},{8,0},{12,4},{1,9},{5,13},{9,1},{13,5},{2,10},{6,14},... | collective-permute-start | bytes 196616 | tf_op jit(solution)/shard_map/ppermute | solution.py:324
  26.9 5.1 %collective-permute-start.11 = (bf16[144,128]{1,0:T(8,128)(2,1)S(1)}, bf16[144,128]{1,0:T(8,128)(2,1)S(1)}, u32[]{:S(2)}, u32[]{:S(2)}) collective-permute-start(bf16[144,128]{1,0:T(8,128)(2,1)S(1)} %add_convert_fusion.1.pair_ref), channel_id=1, source_target_pairs={{0,4},{4,0},{8,12},{12,8},{1,5},{5,1},{9,13},{13,9},{2,6},{6,2},{1... | collective-permute-start | bytes 110600 | tf_op jit(solution)/shard_map/ppermute | solution.py:324
  27.6 6.2 %collective-permute-start.10 = (bf16[256,128]{1,0:T(8,128)(2,1)S(1)}, bf16[256,128]{1,0:T(8,128)(2,1)S(1)}, u32[]{:S(2)}, u32[]{:S(2)}) collective-permute-start(bf16[256,128]{1,0:T(8,128)(2,1)S(1)} %get-tuple-element.45), channel_id=1, source_target_pairs={{0,12},{4,8},{8,4},{12,0},{1,13},{5,9},{9,5},{13,1},{2,14},{6,10},... | collective-permute-start | bytes 196616 | tf_op jit(solution)/shard_map/ppermute | solution.py:324
  32.0 1.9 %collective-permute-start.12 = (f32[128,128]{1,0:T(8,128)S(1)}, f32[128,128]{1,0:T(8,128)S(1)}, u32[]{:S(2)}, u32[]{:S(2)}) collective-permute-start(f32[128,128]{1,0:T(8,128)S(1)} %convert_add_fusion.half_ref), channel_id=1, source_target_pairs={{0,1},{1,0},{2,3},{3,2},{4,5},{5,4},{6,7},{7,6},{8,9},{9,8},{10,11... | collective-permute-start | bytes 196616 | tf_op jit(solution)/shard_map/ppermute | solution.py:324

commit v9 on v8

--- a/solution.py
+++ b/solution.py
@@ -265,27 +265,15 @@
             turned_ref[lanes, x * width : (x + 1) * width] = tile_ref[pl.ds(row_at, width), lanes].T
 
 
-def backward_kernel(offsets, turned_ref, sib_ref, part_ref, *outs):
+def backward_kernel(turned_ref, sib_ref, part_ref, keep_ref, send1, send2, send3):
     row = lax.axis_index("row")
-    rows = part_ref.shape[1]
-    for k, out in zip(offsets, outs):
+    rows = keep_ref.shape[0]
+    for k, out in ((1, send1), (2, send2), (3, send3), (0, keep_ref)):
         at = pl.multiple_of(jnp.bitwise_xor(row, k) * rows, rows)
         total = part_ref[k] + jnp.dot(
             turned_ref[pl.ds(at, rows), :], sib_ref[pl.ds(0, 2 * rows), :], preferred_element_type=F32
         )
         out[...] = total.astype(out.dtype)
-
-
-def backward(offsets, turned, sib, part):
-    _, rows, width_in = part.shape
-    return pl.pallas_call(
-        functools.partial(backward_kernel, offsets),
-        in_specs=[WHOLE] * 3,
-        out_specs=[WHOLE] * len(offsets),
-        out_shape=[jax.ShapeDtypeStruct((rows, width_in), BF16 if k else F32) for k in offsets],
-        compiler_params=LIMIT,
-        name="backward",
-    )(turned, sib, part)
 
 
 def stripe_kernel(own_ref, sib_ref, stripe_ref):
@@ -381,10 +369,14 @@
         name="stripe",
     )(grads, grads_sib)
     stripe_far = swap(stripe, "row", 2)
-    first, second = backward((1, 2), turned, grads_sib, part)
-    third, own = backward((3, 0), turned, grads_sib, part)
-    stripe_far, third = lax.optimization_barrier((stripe_far, third))
-    sends = [first, second, third]
+    own, *sends = pl.pallas_call(
+        backward_kernel,
+        in_specs=[WHOLE] * 3,
+        out_specs=[WHOLE] * 4,
+        out_shape=[jax.ShapeDtypeStruct(block.shape, F32)] + [block] * 3,
+        compiler_params=LIMIT,
+        name="backward",
+    )(turned, grads_sib, part)
     pair = (stripe.astype(F32) + stripe_far.astype(F32)).astype(BF16)
     pair, sends[2] = lax.optimization_barrier((pair, sends[2]))
     got = [swap(send, "row", k) for k, send in zip((1, 2, 3), sends)]

time: 34.7 us -> 34.8 us (level)
  no operation moved by 1% of the time
where the time goes in v9:
time: 34.8 us
  starting transfers between devices  17.2 us (49%)
  waiting for transfers between devices  9.8 us (28%)
  Pallas kernels  6.11 us (18%)
  between operations  1.46 us (4%)
    ppermute x13, starting transfers between devices, swap(): return lax.ppermute(array, axis, [(i, i ^ bit) for i in range(size)])  17.2 us
    ppermute x13, waiting for transfers between devices, swap(): return lax.ppermute(array, axis, [(i, i ^ bit) for i in range(size)])  9.8 us
    pallas_call x1, Pallas kernels, densify(): pl.pallas_call(functools.partial(densify_kernel, chunks, row_blocks, col_...  2.67 us
    pallas_call x2, Pallas kernels, forward(): pl.pallas_call(functools.partial(forward_kernel, mine), in_specs=[WHOLE]...  0.85 us
    pallas_call x1, Pallas kernels, dense_tile(): pl.pallas_call(functools.partial(last_kernel, norm_scale), in_specs=[WHOL...  0.76 us
  transfers between devices with their start and end apart: 13, of which 8 were waited for; matrix products, arithmetic and copies ran while one was open for 0% of the time, Pallas kernels for 14%

profile of v9, /device:TPU:0, one launch (start us, length us, event | category | flops | bytes accessed | tf_op | source)
XLA Modules:
  0.0 34.8 jit_solution(16430990249555312597)
XLA Ops:
  0.6 5.1 %collective-permute-start = (bf16[256,128]{1,0:T(8,128)(2,1)}, bf16[256,128]{1,0:T(8,128)(2,1)S(1)}, u32[]{:S(2)}, u32[]{:S(2)}) collective-permute-start(bf16[256,128]{1,0:T(8,128)(2,1)} %param.8), channel_id=1, source_target_pairs={{0,12},{4,8},{8,4},{12,0},{1,13},{5,9},{9,5},{13,1},{2,14},{6,10},... | collective-permute-start | bytes 196616 | tf_op jit(solution)/shard_map/ppermute | solution.py:312
  5.8 0.6 %collective-permute-start.1 = (bf16[256,128]{1,0:T(8,128)(2,1)}, bf16[256,128]{1,0:T(8,128)(2,1)S(1)}, u32[]{:S(2)}, u32[]{:S(2)}) collective-permute-start(bf16[256,128]{1,0:T(8,128)(2,1)} %param.8), channel_id=1, source_target_pairs={{0,4},{4,0},{8,12},{12,8},{1,5},{5,1},{9,13},{13,9},{2,6},{6,2},{1... | collective-permute-start | bytes 196616 | tf_op jit(solution)/shard_map/ppermute | solution.py:312
  6.4 1.6 %collective-permute-start.4 = (bf16[256,256]{1,0:T(8,128)(2,1)}, bf16[256,256]{1,0:T(8,128)(2,1)S(1)}, u32[]{:S(2)}, u32[]{:S(2)}) collective-permute-start(bf16[256,256]{1,0:T(8,128)(2,1)} %cot_ref.1), channel_id=1, source_target_pairs={{0,2},{1,3},{2,0},{3,1},{4,6},{5,7},{6,4},{7,5},{8,10},{9,11},{10,... | collective-permute-start | bytes 393224 | tf_op jit(solution)/shard_map/ppermute | solution.py:312
  8.7 2.7 %densify.1.tile_ref = bf16[1024,1024]{1,0:T(8,128)(2,1)S(1)} custom-call(s32[1,1]{1,0:T(1,128)} %bitcast.3.count_in, s32[128]{0:T(128)} %rows_in.1, s32[128]{0:T(128)} %cols_in.1, bf16[128,128,128]{2,1,0:T(8,128)(2,1)} %values_ref.1), custom_call_target="tpu_custom_call" | custom-call | flops 2097152 | bytes 4194304 | tf_op jit(solution)/shard_map/densify/pallas_call | solution.py:151
  11.4 0.0 copy-start
  11.4 0.0 copy-start.1
  11.4 0.0 copy-start.2
  11.5 0.1 collective-permute-done.2.x2
  11.6 0.4 %forward_sibling.1 = bf16[512,128]{1,0:T(8,128)(2,1)S(1)} custom-call(bf16[1024,1024]{1,0:T(8,128)(2,1)S(1)} %densify.1.tile_ref, bf16[512,128]{1,0:T(8,128)(2,1)S(1)} %constant_dynamic-update-slice_fusion.outer_ref, bf16[256,128]{1,0:T(8,128)(2,1)S(1)} %collective-permute-done.1.x1, bf16[256,128]{1,0:T(8,128)(2,1)S(1)} %collective-permute-done.2.x2), custom_call_target="tpu_custom_call" | custom-call | flops 134217728 | bytes 1048576 | tf_op jit(solution)/shard_map/forward_sibling/pallas_call | solution.py:189
  12.0 0.1 collective-permute-start.3
  12.1 0.4 %forward_mine.1 = f32[512,128]{1,0:T(8,128)S(1)} custom-call(bf16[1024,1024]{1,0:T(8,128)(2,1)S(1)} %densify.1.tile_ref, bf16[512,128]{1,0:T(8,128)(2,1)S(1)} %constant_dynamic-update-slice_fusion.outer_ref, bf16[256,128]{1,0:T(8,128)(2,1)S(1)} %collective-permute-done.1.x1, bf16[256,128]{1,0:T(8,128)(2,1)S(1)} %collective-permute-done.2.x2), custom_call_target="tpu_custom_call" | custom-call | flops 134217728 | bytes 1048576 | tf_op jit(solution)/shard_map/forward_mine/pallas_call | solution.py:189
  12.5 0.9 %collective-permute-done.3 = bf16[512,128]{1,0:T(8,128)(2,1)S(1)} collective-permute-done((bf16[512,128]{1,0:T(8,128)(2,1)S(1)}, bf16[512,128]{1,0:T(8,128)(2,1)S(1)}, u32[]{:S(2)}, u32[]{:S(2)}) %collective-permute-start.3) | collective-permute-done | bytes 131104 | tf_op jit(solution)/shard_map/ppermute | solution.py:312
  13.4 1.6 %collective-permute-start.5 = (bf16[512,128]{1,0:T(8,128)(2,1)S(1)}, bf16[512,128]{1,0:T(8,128)(2,1)S(1)}, u32[]{:S(2)}, u32[]{:S(2)}) collective-permute-start(bf16[512,128]{1,0:T(8,128)(2,1)S(1)} %add_convert_fusion.near_ref), channel_id=1, source_target_pairs={{0,2},{1,3},{2,0},{3,1},{4,6},{5,7},{6,4},{7,5},{8,10},{9,11},{10,... | collective-permute-start | bytes 393224 | tf_op jit(solution)/shard_map/ppermute | solution.py:312
  15.0 0.3 turn.1.turned_ref
  15.3 3.7 %collective-permute-done.5.far_ref = bf16[512,128]{1,0:T(8,128)(2,1)S(1)} collective-permute-done((bf16[512,128]{1,0:T(8,128)(2,1)S(1)}, bf16[512,128]{1,0:T(8,128)(2,1)S(1)}, u32[]{:S(2)}, u32[]{:S(2)}) %collective-permute-start.5) | collective-permute-done | bytes 131104 | tf_op jit(solution)/shard_map/ppermute | solution.py:312
  19.1 0.5 %layer.1 = (f32[256,256]{1,0:T(8,128)S(1)}, bf16[784,128]{1,0:T(8,128)(2,1)S(1)}) custom-call(bf16[512,128]{1,0:T(8,128)(2,1)S(1)} %add_convert_fusion.near_ref, bf16[512,128]{1,0:T(8,128)(2,1)S(1)} %collective-permute-done.5.far_ref, bf16[256,256]{1,0:T(8,128)(2,1)S(1)} %copy-done, bf16[256,256]{1,0:T(8,128)(2,1)S(1)} %collective-permute-done.4.cot_far_ref, ...), custom_call_target="tpu_custom_call" | custom-call | tf_op jit(solution)/shard_map/layer/pallas_call | solution.py:341
  19.6 0.1 collective-permute-start.6
  19.7 0.5 %backward_mine.1.part_ref = f32[4,256,128]{2,1,0:T(8,128)S(1)} custom-call(bf16[1024,1024]{1,0:T(8,128)(2,1)S(1)} %densify.1.tile_ref, bf16[784,128]{1,0:T(8,128)(2,1)S(1)} %get-tuple-element.34.own_ref), custom_call_target="tpu_custom_call" | custom-call | flops 134217728 | bytes 1048576 | tf_op jit(solution)/shard_map/backward_mine/pallas_call | solution.py:353
  20.2 0.9 %collective-permute-done.6.sib_ref = bf16[784,128]{1,0:T(8,128)(2,1)S(1)} collective-permute-done((bf16[784,128]{1,0:T(8,128)(2,1)S(1)}, bf16[784,128]{1,0:T(8,128)(2,1)S(1)}, u32[]{:S(2)}, u32[]{:S(2)}) %collective-permute-start.6) | collective-permute-done | bytes 200736 | tf_op jit(solution)/shard_map/ppermute | solution.py:312
  21.2 2.1 %collective-permute-start.9 = (bf16[144,128]{1,0:T(8,128)(2,1)S(1)}, bf16[144,128]{1,0:T(8,128)(2,1)S(1)}, u32[]{:S(2)}, u32[]{:S(2)}) collective-permute-start(bf16[144,128]{1,0:T(8,128)(2,1)S(1)} %stripe.1), channel_id=1, source_target_pairs={{0,8},{4,12},{8,0},{12,4},{1,9},{5,13},{9,1},{13,5},{2,10},{6,14},... | collective-permute-start | bytes 110600 | tf_op jit(solution)/shard_map/ppermute | solution.py:312
  23.3 0.4 %backward.1 = (f32[256,128]{1,0:T(8,128)S(1)}, bf16[256,128]{1,0:T(8,128)(2,1)S(1)}, bf16[256,128]{1,0:T(8,128)(2,1)S(1)}, bf16[256,128]{1,0:T(8,128)(2,1)S(1)}) custom-call(bf16[1024,512]{1,0:T(8,128)(2,1)S(1)} %turn.1.turned_ref, bf16[784,128]{1,0:T(8,128)(2,1)S(1)} %collective-permute-done.6.sib_ref, f32[4,256,128]{2,1,0:T(8,128)S(1)} %backward_mine.1.part_ref), custom_call_target="tpu_custom_call" | custom-call | tf_op jit(solution)/shard_map/backward/pallas_call | solution.py:372
  23.7 2.2 %collective-permute-start.7 = (bf16[256,128]{1,0:T(8,128)(2,1)S(1)}, bf16[256,128]{1,0:T(8,128)(2,1)S(1)}, u32[]{:S(2)}, u32[]{:S(2)}) collective-permute-start(bf16[256,128]{1,0:T(8,128)(2,1)S(1)} %get-tuple-element.38), channel_id=1, source_target_pairs={{0,4},{4,0},{8,12},{12,8},{1,5},{5,1},{9,13},{13,9},{2,6},{6,2},{1... | collective-permute-start | bytes 196616 | tf_op jit(solution)/shard_map/ppermute | solution.py:312
  25.9 0.0 collective-permute-start.8
  25.9 0.8 %collective-permute-done.9 = bf16[144,128]{1,0:T(8,128)(2,1)S(1)} collective-permute-done((bf16[144,128]{1,0:T(8,128)(2,1)S(1)}, bf16[144,128]{1,0:T(8,128)(2,1)S(1)}, u32[]{:S(2)}, u32[]{:S(2)}) %collective-permute-start.9) | collective-permute-done | bytes 36896 | tf_op jit(solution)/shard_map/ppermute | solution.py:312
  26.7 1.0 %collective-permute-start.11 = (bf16[144,128]{1,0:T(8,128)(2,1)S(1)}, bf16[144,128]{1,0:T(8,128)(2,1)S(1)}, u32[]{:S(2)}, u32[]{:S(2)}) collective-permute-start(bf16[144,128]{1,0:T(8,128)(2,1)S(1)} %add_convert_fusion.1.pair_ref), channel_id=1, source_target_pairs={{0,4},{4,0},{8,12},{12,8},{1,5},{5,1},{9,13},{13,9},{2,6},{6,2},{1... | collective-permute-start | bytes 110600 | tf_op jit(solution)/shard_map/ppermute | solution.py:312
  27.7 0.1 multiply_convert_fusion.act_ref
  27.8 2.8 %collective-permute-start.10 = (bf16[256,128]{1,0:T(8,128)(2,1)S(1)}, bf16[256,128]{1,0:T(8,128)(2,1)S(1)}, u32[]{:S(2)}, u32[]{:S(2)}) collective-permute-start(bf16[256,128]{1,0:T(8,128)(2,1)S(1)} %get-tuple-element.41), channel_id=1, source_target_pairs={{0,12},{4,8},{8,4},{12,0},{1,13},{5,9},{9,5},{13,1},{2,14},{6,10},... | collective-permute-start | bytes 196616 | tf_op jit(solution)/shard_map/ppermute | solution.py:312
  30.5 0.9 %collective-permute-done.11.pair_far_ref = bf16[144,128]{1,0:T(8,128)(2,1)S(1)} collective-permute-done((bf16[144,128]{1,0:T(8,128)(2,1)S(1)}, bf16[144,128]{1,0:T(8,128)(2,1)S(1)}, u32[]{:S(2)}, u32[]{:S(2)}) %collective-permute-start.11) | collective-permute-done | bytes 36896 | tf_op jit(solution)/shard_map/ppermute | solution.py:312
  31.4 0.1 collective-permute-start.12
  31.5 1.4 %collective-permute-done.8.got2 = bf16[256,128]{1,0:T(8,128)(2,1)S(1)} collective-permute-done((bf16[256,128]{1,0:T(8,128)(2,1)S(1)}, bf16[256,128]{1,0:T(8,128)(2,1)S(1)}, u32[]{:S(2)}, u32[]{:S(2)}) %collective-permute-start.8) | collective-permute-done | bytes 65568 | tf_op jit(solution)/shard_map/ppermute | solution.py:312
  32.8 1.2 %collective-permute-done.10.got3 = bf16[256,128]{1,0:T(8,128)(2,1)S(1)} collective-permute-done((bf16[256,128]{1,0:T(8,128)(2,1)S(1)}, bf16[256,128]{1,0:T(8,128)(2,1)S(1)}, u32[]{:S(2)}, u32[]{:S(2)}) %collective-permute-start.10) | collective-permute-done | bytes 65568 | tf_op jit(solution)/shard_map/ppermute | solution.py:312
  34.0 0.8 %last.1 = (bf16[256,128]{1,0:T(8,128)(2,1)}, bf16[256,256]{1,0:T(8,128)(2,1)}, f32[128,256]{1,0:T(8,128)}, f32[1,256]{1,0:T(1,128)}) custom-call(f32[256,128]{1,0:T(8,128)S(1)} %get-tuple-element.37.keep_ref, bf16[256,128]{1,0:T(8,128)(2,1)S(1)} %collective-permute-done.7.got1, bf16[256,128]{1,0:T(8,128)(2,1)S(1)} %collective-permute-done.8.got2, ...), custom_call_target="tpu_custom_call" | custom-call | tf_op jit(solution)/shard_map/last/pallas_call | solution.py:390
  (17 shorter events, 0.1 us)
Async XLA Ops:
  0.6 10.7 %copy-start.3 = (bf16[256,128]{1,0:T(8,128)(2,1)S(1)}, bf16[256,128]{1,0:T(8,128)(2,1)}, u32[]{:S(2)}) copy-start(bf16[256,128]{1,0:T(8,128)(2,1)} %param.8) | copy-start | bytes 196612
  0.6 10.7 %collective-permute-start = (bf16[256,128]{1,0:T(8,128)(2,1)}, bf16[256,128]{1,0:T(8,128)(2,1)S(1)}, u32[]{:S(2)}, u32[]{:S(2)}) collective-permute-start(bf16[256,128]{1,0:T(8,128)(2,1)} %param.8), channel_id=1, source_target_pairs={{0,12},{4,8},{8,4},{12,0},{1,13},{5,9},{9,5},{13,1},{2,14},{6,10},... | collective-permute-start | bytes 196616 | tf_op jit(solution)/shard_map/ppermute | solution.py:312
  5.8 5.8 %collective-permute-start.2 = (bf16[256,128]{1,0:T(8,128)(2,1)}, bf16[256,128]{1,0:T(8,128)(2,1)S(1)}, u32[]{:S(2)}, u32[]{:S(2)}) collective-permute-start(bf16[256,128]{1,0:T(8,128)(2,1)} %param.8), channel_id=1, source_target_pairs={{0,8},{4,12},{8,0},{12,4},{1,9},{5,13},{9,1},{13,5},{2,10},{6,14},... | collective-permute-start | bytes 196616 | tf_op jit(solution)/shard_map/ppermute | solution.py:312
  5.8 5.8 %collective-permute-start.1 = (bf16[256,128]{1,0:T(8,128)(2,1)}, bf16[256,128]{1,0:T(8,128)(2,1)S(1)}, u32[]{:S(2)}, u32[]{:S(2)}) collective-permute-start(bf16[256,128]{1,0:T(8,128)(2,1)} %param.8), channel_id=1, source_target_pairs={{0,4},{4,0},{8,12},{12,8},{1,5},{5,1},{9,13},{13,9},{2,6},{6,2},{1... | collective-permute-start | bytes 196616 | tf_op jit(solution)/shard_map/ppermute | solution.py:312
  6.4 6.1 %collective-permute-start.4 = (bf16[256,256]{1,0:T(8,128)(2,1)}, bf16[256,256]{1,0:T(8,128)(2,1)S(1)}, u32[]{:S(2)}, u32[]{:S(2)}) collective-permute-start(bf16[256,256]{1,0:T(8,128)(2,1)} %cot_ref.1), channel_id=1, source_target_pairs={{0,2},{1,3},{2,0},{3,1},{4,6},{5,7},{6,4},{7,5},{8,10},{9,11},{10,... | collective-permute-start | bytes 393224 | tf_op jit(solution)/shard_map/ppermute | solution.py:312
  11.4 7.7 %copy-start = (bf16[256,256]{1,0:T(8,128)(2,1)S(1)}, bf16[256,256]{1,0:T(8,128)(2,1)}, u32[]{:S(2)}) copy-start(bf16[256,256]{1,0:T(8,128)(2,1)} %cot_ref.1) | copy-start | bytes 393220
  11.4 7.6 %copy-start.1 = (bf16[128,256]{1,0:T(8,128)(2,1)S(1)}, bf16[128,256]{1,0:T(8,128)(2,1)}, u32[]{:S(2)}) copy-start(bf16[128,256]{1,0:T(8,128)(2,1)} %weight_ref.1) | copy-start | bytes 196612
  11.4 7.6 %copy-start.2 = (f32[256]{0:T(256)S(1)}, f32[256]{0:T(256)}, u32[]{:S(2)}) copy-start(f32[256]{0:T(256)} %param.14) | copy-start | bytes 3076
  12.0 1.4 %collective-permute-start.3 = (bf16[512,128]{1,0:T(8,128)(2,1)S(1)}, bf16[512,128]{1,0:T(8,128)(2,1)S(1)}, u32[]{:S(2)}, u32[]{:S(2)}) collective-permute-start(bf16[512,128]{1,0:T(8,128)(2,1)S(1)} %forward_sibling.1), channel_id=1, source_target_pairs={{0,1},{1,0},{2,3},{3,2},{4,5},{5,4},{6,7},{7,6},{8,9},{9,8},{10,11... | collective-permute-start | bytes 393224 | tf_op jit(solution)/shard_map/ppermute | solution.py:312
  13.4 5.6 %collective-permute-start.5 = (bf16[512,128]{1,0:T(8,128)(2,1)S(1)}, bf16[512,128]{1,0:T(8,128)(2,1)S(1)}, u32[]{:S(2)}, u32[]{:S(2)}) collective-permute-start(bf16[512,128]{1,0:T(8,128)(2,1)S(1)} %add_convert_fusion.near_ref), channel_id=1, source_target_pairs={{0,2},{1,3},{2,0},{3,1},{4,6},{5,7},{6,4},{7,5},{8,10},{9,11},{10,... | collective-permute-start | bytes 393224 | tf_op jit(solution)/shard_map/ppermute | solution.py:312
  19.6 1.5 %collective-permute-start.6 = (bf16[784,128]{1,0:T(8,128)(2,1)S(1)}, bf16[784,128]{1,0:T(8,128)(2,1)S(1)}, u32[]{:S(2)}, u32[]{:S(2)}) collective-permute-start(bf16[784,128]{1,0:T(8,128)(2,1)S(1)} %get-tuple-element.34.own_ref), channel_id=1, source_target_pairs={{0,1},{1,0},{2,3},{3,2},{4,5},{5,4},{6,7},{7,6},{8,9},{9,8},{10,11... | collective-permute-start | bytes 602120 | tf_op jit(solution)/shard_map/ppermute | solution.py:312
  21.2 5.5 %collective-permute-start.9 = (bf16[144,128]{1,0:T(8,128)(2,1)S(1)}, bf16[144,128]{1,0:T(8,128)(2,1)S(1)}, u32[]{:S(2)}, u32[]{:S(2)}) collective-permute-start(bf16[144,128]{1,0:T(8,128)(2,1)S(1)} %stripe.1), channel_id=1, source_target_pairs={{0,8},{4,12},{8,0},{12,4},{1,9},{5,13},{9,1},{13,5},{2,10},{6,14},... | collective-permute-start | bytes 110600 | tf_op jit(solution)/shard_map/ppermute | solution.py:312
  23.7 7.8 %collective-permute-start.7 = (bf16[256,128]{1,0:T(8,128)(2,1)S(1)}, bf16[256,128]{1,0:T(8,128)(2,1)S(1)}, u32[]{:S(2)}, u32[]{:S(2)}) collective-permute-start(bf16[256,128]{1,0:T(8,128)(2,1)S(1)} %get-tuple-element.38), channel_id=1, source_target_pairs={{0,4},{4,0},{8,12},{12,8},{1,5},{5,1},{9,13},{13,9},{2,6},{6,2},{1... | collective-permute-start | bytes 196616 | tf_op jit(solution)/shard_map/ppermute | solution.py:312
  25.9 6.9 %collective-permute-start.8 = (bf16[256,128]{1,0:T(8,128)(2,1)S(1)}, bf16[256,128]{1,0:T(8,128)(2,1)S(1)}, u32[]{:S(2)}, u32[]{:S(2)}) collective-permute-start(bf16[256,128]{1,0:T(8,128)(2,1)S(1)} %get-tuple-element.39), channel_id=1, source_target_pairs={{0,8},{4,12},{8,0},{12,4},{1,9},{5,13},{9,1},{13,5},{2,10},{6,14},... | collective-permute-start | bytes 196616 | tf_op jit(solution)/shard_map/ppermute | solution.py:312
  26.7 4.7 %collective-permute-start.11 = (bf16[144,128]{1,0:T(8,128)(2,1)S(1)}, bf16[144,128]{1,0:T(8,128)(2,1)S(1)}, u32[]{:S(2)}, u32[]{:S(2)}) collective-permute-start(bf16[144,128]{1,0:T(8,128)(2,1)S(1)} %add_convert_fusion.1.pair_ref), channel_id=1, source_target_pairs={{0,4},{4,0},{8,12},{12,8},{1,5},{5,1},{9,13},{13,9},{2,6},{6,2},{1... | collective-permute-start | bytes 110600 | tf_op jit(solution)/shard_map/ppermute | solution.py:312
  27.8 6.2 %collective-permute-start.10 = (bf16[256,128]{1,0:T(8,128)(2,1)S(1)}, bf16[256,128]{1,0:T(8,128)(2,1)S(1)}, u32[]{:S(2)}, u32[]{:S(2)}) collective-permute-start(bf16[256,128]{1,0:T(8,128)(2,1)S(1)} %get-tuple-element.41), channel_id=1, source_target_pairs={{0,12},{4,8},{8,4},{12,0},{1,13},{5,9},{9,5},{13,1},{2,14},{6,10},... | collective-permute-start | bytes 196616 | tf_op jit(solution)/shard_map/ppermute | solution.py:312
  31.4 2.6 %collective-permute-start.12 = (f32[128,128]{1,0:T(8,128)S(1)}, f32[128,128]{1,0:T(8,128)S(1)}, u32[]{:S(2)}, u32[]{:S(2)}) collective-permute-start(f32[128,128]{1,0:T(8,128)S(1)} %convert_add_fusion.half_ref), channel_id=1, source_target_pairs={{0,1},{1,0},{2,3},{3,2},{4,5},{5,4},{6,7},{7,6},{8,9},{9,8},{10,11... | collective-permute-start | bytes 196616 | tf_op jit(solution)/shard_map/ppermute | solution.py:312

commit v10 on v9

--- a/solution.py
+++ b/solution.py
@@ -289,7 +289,7 @@
         ).astype(BF16)
 
 
-def last_kernel(scale, keep_ref, got1, got2, got3, act_ref, pair_ref, pair_far_ref, half_ref, sib_ref,
+def last_kernel(scale, keep_ref, got3, act_ref, pair_ref, pair_far_ref, half_ref, sib_ref,
                 features_ref, hidden_ref, gw_ref, gb_ref):
     core = lax.rem(lax.axis_index("col"), 2)
     width_in, hid = gw_ref.shape
@@ -301,9 +301,7 @@
     both = (pair_ref[block, :].astype(F32) + pair_far_ref[block, :].astype(F32)) * scale
     for j in range(hid // width_in):
         gb_ref[:, j * width_in : (j + 1) * width_in] = both[j : j + 1, :]
-    total = keep_ref[...] + got1[...].astype(F32)
-    total = total + got2[...].astype(F32) + got3[...].astype(F32)
-    features_ref[...] = total.astype(BF16)
+    features_ref[...] = (keep_ref[...] + got3[...].astype(F32)).astype(BF16)
     hidden_ref[...] = act_ref[...]
 
 
@@ -389,7 +387,7 @@
     norm_scale = float(node_rows * ROWS * COLS) ** (-0.5)
     grad_features, hidden, grad_weight, grad_bias = pl.pallas_call(
         functools.partial(last_kernel, norm_scale),
-        in_specs=[WHOLE] * 9,
+        in_specs=[WHOLE] * 7,
         out_specs=[WHOLE] * 4,
         out_shape=[
             block,
@@ -399,7 +397,7 @@
         ],
         compiler_params=LIMIT,
         name="last",
-    )(own, *got, hidden, pair, pair_far, gw_half, gw_sib)
+    )(own + got[0].astype(F32) + got[1].astype(F32), got[2], hidden, pair, pair_far, gw_half, gw_sib)
     return hidden, grad_weight, grad_bias.reshape(hid), grad_features
 
 

time: 34.8 us -> 34.8 us (level)
  no operation moved by 1% of the time
where the time goes in v10:
time: 34.8 us
  starting transfers between devices  17.2 us (49%)
  waiting for transfers between devices  9.77 us (28%)
  Pallas kernels  6.1 us (18%)
  between operations  1.46 us (4%)
    ppermute x13, starting transfers between devices, swap(): return lax.ppermute(array, axis, [(i, i ^ bit) for i in range(size)])  17.2 us
    ppermute x13, waiting for transfers between devices, swap(): return lax.ppermute(array, axis, [(i, i ^ bit) for i in range(size)])  9.77 us
    pallas_call x1, Pallas kernels, densify(): pl.pallas_call(functools.partial(densify_kernel, chunks, row_blocks, col_...  2.67 us
    pallas_call x2, Pallas kernels, forward(): pl.pallas_call(functools.partial(forward_kernel, mine), in_specs=[WHOLE]...  0.85 us
    pallas_call x1, Pallas kernels, dense_tile(): pl.pallas_call(functools.partial(last_kernel, norm_scale), in_specs=[WHOL...  0.76 us
  transfers between devices with their start and end apart: 13, of which 8 were waited for; matrix products, arithmetic and copies ran while one was open for 0% of the time, Pallas kernels for 14%

profile of v10, /device:TPU:0, one launch (start us, length us, event | category | flops | bytes accessed | tf_op | source)
XLA Modules:
  0.0 34.8 jit_solution(1777639560938420445)
XLA Ops:
  0.6 5.1 %collective-permute-start = (bf16[256,128]{1,0:T(8,128)(2,1)}, bf16[256,128]{1,0:T(8,128)(2,1)S(1)}, u32[]{:S(2)}, u32[]{:S(2)}) collective-permute-start(bf16[256,128]{1,0:T(8,128)(2,1)} %param.8), channel_id=1, source_target_pairs={{0,12},{4,8},{8,4},{12,0},{1,13},{5,9},{9,5},{13,1},{2,14},{6,10},... | collective-permute-start | bytes 196616 | tf_op jit(solution)/shard_map/ppermute | solution.py:310
  5.8 0.6 %collective-permute-start.1 = (bf16[256,128]{1,0:T(8,128)(2,1)}, bf16[256,128]{1,0:T(8,128)(2,1)S(1)}, u32[]{:S(2)}, u32[]{:S(2)}) collective-permute-start(bf16[256,128]{1,0:T(8,128)(2,1)} %param.8), channel_id=1, source_target_pairs={{0,4},{4,0},{8,12},{12,8},{1,5},{5,1},{9,13},{13,9},{2,6},{6,2},{1... | collective-permute-start | bytes 196616 | tf_op jit(solution)/shard_map/ppermute | solution.py:310
  6.4 1.6 %collective-permute-start.4 = (bf16[256,256]{1,0:T(8,128)(2,1)}, bf16[256,256]{1,0:T(8,128)(2,1)S(1)}, u32[]{:S(2)}, u32[]{:S(2)}) collective-permute-start(bf16[256,256]{1,0:T(8,128)(2,1)} %cot_ref.1), channel_id=1, source_target_pairs={{0,2},{1,3},{2,0},{3,1},{4,6},{5,7},{6,4},{7,5},{8,10},{9,11},{10,... | collective-permute-start | bytes 393224 | tf_op jit(solution)/shard_map/ppermute | solution.py:310
  8.7 2.7 %densify.1.tile_ref = bf16[1024,1024]{1,0:T(8,128)(2,1)S(1)} custom-call(s32[1,1]{1,0:T(1,128)} %bitcast.3.count_in, s32[128]{0:T(128)} %rows_in.1, s32[128]{0:T(128)} %cols_in.1, bf16[128,128,128]{2,1,0:T(8,128)(2,1)} %values_ref.1), custom_call_target="tpu_custom_call" | custom-call | flops 2097152 | bytes 4194304 | tf_op jit(solution)/shard_map/densify/pallas_call | solution.py:151
  11.4 0.0 copy-start
  11.4 0.0 copy-start.1
  11.4 0.0 copy-start.2
  11.5 0.1 collective-permute-done.2.x2
  11.6 0.4 %forward_sibling.1 = bf16[512,128]{1,0:T(8,128)(2,1)S(1)} custom-call(bf16[1024,1024]{1,0:T(8,128)(2,1)S(1)} %densify.1.tile_ref, bf16[512,128]{1,0:T(8,128)(2,1)S(1)} %constant_dynamic-update-slice_fusion.outer_ref, bf16[256,128]{1,0:T(8,128)(2,1)S(1)} %collective-permute-done.1.x1, bf16[256,128]{1,0:T(8,128)(2,1)S(1)} %collective-permute-done.2.x2), custom_call_target="tpu_custom_call" | custom-call | flops 134217728 | bytes 1048576 | tf_op jit(solution)/shard_map/forward_sibling/pallas_call | solution.py:189
  12.0 0.1 collective-permute-start.3
  12.1 0.4 %forward_mine.1 = f32[512,128]{1,0:T(8,128)S(1)} custom-call(bf16[1024,1024]{1,0:T(8,128)(2,1)S(1)} %densify.1.tile_ref, bf16[512,128]{1,0:T(8,128)(2,1)S(1)} %constant_dynamic-update-slice_fusion.outer_ref, bf16[256,128]{1,0:T(8,128)(2,1)S(1)} %collective-permute-done.1.x1, bf16[256,128]{1,0:T(8,128)(2,1)S(1)} %collective-permute-done.2.x2), custom_call_target="tpu_custom_call" | custom-call | flops 134217728 | bytes 1048576 | tf_op jit(solution)/shard_map/forward_mine/pallas_call | solution.py:189
  12.5 0.9 %collective-permute-done.3 = bf16[512,128]{1,0:T(8,128)(2,1)S(1)} collective-permute-done((bf16[512,128]{1,0:T(8,128)(2,1)S(1)}, bf16[512,128]{1,0:T(8,128)(2,1)S(1)}, u32[]{:S(2)}, u32[]{:S(2)}) %collective-permute-start.3) | collective-permute-done | bytes 131104 | tf_op jit(solution)/shard_map/ppermute | solution.py:310
  13.4 1.6 %collective-permute-start.5 = (bf16[512,128]{1,0:T(8,128)(2,1)S(1)}, bf16[512,128]{1,0:T(8,128)(2,1)S(1)}, u32[]{:S(2)}, u32[]{:S(2)}) collective-permute-start(bf16[512,128]{1,0:T(8,128)(2,1)S(1)} %add_convert_fusion.near_ref), channel_id=1, source_target_pairs={{0,2},{1,3},{2,0},{3,1},{4,6},{5,7},{6,4},{7,5},{8,10},{9,11},{10,... | collective-permute-start | bytes 393224 | tf_op jit(solution)/shard_map/ppermute | solution.py:310
  15.0 0.3 turn.1.turned_ref
  15.3 3.7 %collective-permute-done.5.far_ref = bf16[512,128]{1,0:T(8,128)(2,1)S(1)} collective-permute-done((bf16[512,128]{1,0:T(8,128)(2,1)S(1)}, bf16[512,128]{1,0:T(8,128)(2,1)S(1)}, u32[]{:S(2)}, u32[]{:S(2)}) %collective-permute-start.5) | collective-permute-done | bytes 131104 | tf_op jit(solution)/shard_map/ppermute | solution.py:310
  19.1 0.5 %layer.1 = (f32[256,256]{1,0:T(8,128)S(1)}, bf16[784,128]{1,0:T(8,128)(2,1)S(1)}) custom-call(bf16[512,128]{1,0:T(8,128)(2,1)S(1)} %add_convert_fusion.near_ref, bf16[512,128]{1,0:T(8,128)(2,1)S(1)} %collective-permute-done.5.far_ref, bf16[256,256]{1,0:T(8,128)(2,1)S(1)} %copy-done, bf16[256,256]{1,0:T(8,128)(2,1)S(1)} %collective-permute-done.4.cot_far_ref, ...), custom_call_target="tpu_custom_call" | custom-call | tf_op jit(solution)/shard_map/layer/pallas_call | solution.py:339
  19.6 0.1 collective-permute-start.6
  19.7 0.5 %backward_mine.1.part_ref = f32[4,256,128]{2,1,0:T(8,128)S(1)} custom-call(bf16[1024,1024]{1,0:T(8,128)(2,1)S(1)} %densify.1.tile_ref, bf16[784,128]{1,0:T(8,128)(2,1)S(1)} %get-tuple-element.34.own_ref), custom_call_target="tpu_custom_call" | custom-call | flops 134217728 | bytes 1048576 | tf_op jit(solution)/shard_map/backward_mine/pallas_call | solution.py:351
  20.2 0.9 %collective-permute-done.6.sib_ref = bf16[784,128]{1,0:T(8,128)(2,1)S(1)} collective-permute-done((bf16[784,128]{1,0:T(8,128)(2,1)S(1)}, bf16[784,128]{1,0:T(8,128)(2,1)S(1)}, u32[]{:S(2)}, u32[]{:S(2)}) %collective-permute-start.6) | collective-permute-done | bytes 200736 | tf_op jit(solution)/shard_map/ppermute | solution.py:310
  21.2 2.1 %collective-permute-start.9 = (bf16[144,128]{1,0:T(8,128)(2,1)S(1)}, bf16[144,128]{1,0:T(8,128)(2,1)S(1)}, u32[]{:S(2)}, u32[]{:S(2)}) collective-permute-start(bf16[144,128]{1,0:T(8,128)(2,1)S(1)} %stripe.1), channel_id=1, source_target_pairs={{0,8},{4,12},{8,0},{12,4},{1,9},{5,13},{9,1},{13,5},{2,10},{6,14},... | collective-permute-start | bytes 110600 | tf_op jit(solution)/shard_map/ppermute | solution.py:310
  23.3 0.4 %backward.1 = (f32[256,128]{1,0:T(8,128)S(1)}, bf16[256,128]{1,0:T(8,128)(2,1)S(1)}, bf16[256,128]{1,0:T(8,128)(2,1)S(1)}, bf16[256,128]{1,0:T(8,128)(2,1)S(1)}) custom-call(bf16[1024,512]{1,0:T(8,128)(2,1)S(1)} %turn.1.turned_ref, bf16[784,128]{1,0:T(8,128)(2,1)S(1)} %collective-permute-done.6.sib_ref, f32[4,256,128]{2,1,0:T(8,128)S(1)} %backward_mine.1.part_ref), custom_call_target="tpu_custom_call" | custom-call | tf_op jit(solution)/shard_map/backward/pallas_call | solution.py:370
  23.7 2.2 %collective-permute-start.7 = (bf16[256,128]{1,0:T(8,128)(2,1)S(1)}, bf16[256,128]{1,0:T(8,128)(2,1)S(1)}, u32[]{:S(2)}, u32[]{:S(2)}) collective-permute-start(bf16[256,128]{1,0:T(8,128)(2,1)S(1)} %get-tuple-element.38), channel_id=1, source_target_pairs={{0,4},{4,0},{8,12},{12,8},{1,5},{5,1},{9,13},{13,9},{2,6},{6,2},{1... | collective-permute-start | bytes 196616 | tf_op jit(solution)/shard_map/ppermute | solution.py:310
  25.9 0.0 collective-permute-start.8
  25.9 0.8 %collective-permute-done.9 = bf16[144,128]{1,0:T(8,128)(2,1)S(1)} collective-permute-done((bf16[144,128]{1,0:T(8,128)(2,1)S(1)}, bf16[144,128]{1,0:T(8,128)(2,1)S(1)}, u32[]{:S(2)}, u32[]{:S(2)}) %collective-permute-start.9) | collective-permute-done | bytes 36896 | tf_op jit(solution)/shard_map/ppermute | solution.py:310
  26.7 1.0 %collective-permute-start.11 = (bf16[144,128]{1,0:T(8,128)(2,1)S(1)}, bf16[144,128]{1,0:T(8,128)(2,1)S(1)}, u32[]{:S(2)}, u32[]{:S(2)}) collective-permute-start(bf16[144,128]{1,0:T(8,128)(2,1)S(1)} %add_convert_fusion.1.pair_ref), channel_id=1, source_target_pairs={{0,4},{4,0},{8,12},{12,8},{1,5},{5,1},{9,13},{13,9},{2,6},{6,2},{1... | collective-permute-start | bytes 110600 | tf_op jit(solution)/shard_map/ppermute | solution.py:310
  27.7 0.1 multiply_convert_fusion.act_ref
  27.8 2.8 %collective-permute-start.10 = (bf16[256,128]{1,0:T(8,128)(2,1)S(1)}, bf16[256,128]{1,0:T(8,128)(2,1)S(1)}, u32[]{:S(2)}, u32[]{:S(2)}) collective-permute-start(bf16[256,128]{1,0:T(8,128)(2,1)S(1)} %get-tuple-element.41), channel_id=1, source_target_pairs={{0,12},{4,8},{8,4},{12,0},{1,13},{5,9},{9,5},{13,1},{2,14},{6,10},... | collective-permute-start | bytes 196616 | tf_op jit(solution)/shard_map/ppermute | solution.py:310
  30.5 0.9 %collective-permute-done.11.pair_far_ref = bf16[144,128]{1,0:T(8,128)(2,1)S(1)} collective-permute-done((bf16[144,128]{1,0:T(8,128)(2,1)S(1)}, bf16[144,128]{1,0:T(8,128)(2,1)S(1)}, u32[]{:S(2)}, u32[]{:S(2)}) %collective-permute-start.11) | collective-permute-done | bytes 36896 | tf_op jit(solution)/shard_map/ppermute | solution.py:310
  31.4 0.1 collective-permute-start.12
  31.5 1.4 %collective-permute-done.8 = bf16[256,128]{1,0:T(8,128)(2,1)S(1)} collective-permute-done((bf16[256,128]{1,0:T(8,128)(2,1)S(1)}, bf16[256,128]{1,0:T(8,128)(2,1)S(1)}, u32[]{:S(2)}, u32[]{:S(2)}) %collective-permute-start.8) | collective-permute-done | bytes 65568 | tf_op jit(solution)/shard_map/ppermute | solution.py:310
  32.9 1.1 %collective-permute-done.10.got3 = bf16[256,128]{1,0:T(8,128)(2,1)S(1)} collective-permute-done((bf16[256,128]{1,0:T(8,128)(2,1)S(1)}, bf16[256,128]{1,0:T(8,128)(2,1)S(1)}, u32[]{:S(2)}, u32[]{:S(2)}) %collective-permute-start.10) | collective-permute-done | bytes 65568 | tf_op jit(solution)/shard_map/ppermute | solution.py:310
  34.0 0.8 %last.1 = (bf16[256,128]{1,0:T(8,128)(2,1)}, bf16[256,256]{1,0:T(8,128)(2,1)}, f32[128,256]{1,0:T(8,128)}, f32[1,256]{1,0:T(1,128)}) custom-call(f32[256,128]{1,0:T(8,128)S(1)} %convert_add_fusion.keep_ref, bf16[256,128]{1,0:T(8,128)(2,1)S(1)} %collective-permute-done.10.got3, bf16[256,256]{1,0:T(8,128)(2,1)S(1)} %multiply_convert_fusion.act_ref, ...), custom_call_target="tpu_custom_call" | custom-call | tf_op jit(solution)/shard_map/last/pallas_call | solution.py:388
  (18 shorter events, 0.1 us)
Async XLA Ops:
  0.6 10.7 %copy-start.3 = (bf16[256,128]{1,0:T(8,128)(2,1)S(1)}, bf16[256,128]{1,0:T(8,128)(2,1)}, u32[]{:S(2)}) copy-start(bf16[256,128]{1,0:T(8,128)(2,1)} %param.8) | copy-start | bytes 196612
  0.6 10.7 %collective-permute-start = (bf16[256,128]{1,0:T(8,128)(2,1)}, bf16[256,128]{1,0:T(8,128)(2,1)S(1)}, u32[]{:S(2)}, u32[]{:S(2)}) collective-permute-start(bf16[256,128]{1,0:T(8,128)(2,1)} %param.8), channel_id=1, source_target_pairs={{0,12},{4,8},{8,4},{12,0},{1,13},{5,9},{9,5},{13,1},{2,14},{6,10},... | collective-permute-start | bytes 196616 | tf_op jit(solution)/shard_map/ppermute | solution.py:310
  5.8 5.8 %collective-permute-start.2 = (bf16[256,128]{1,0:T(8,128)(2,1)}, bf16[256,128]{1,0:T(8,128)(2,1)S(1)}, u32[]{:S(2)}, u32[]{:S(2)}) collective-permute-start(bf16[256,128]{1,0:T(8,128)(2,1)} %param.8), channel_id=1, source_target_pairs={{0,8},{4,12},{8,0},{12,4},{1,9},{5,13},{9,1},{13,5},{2,10},{6,14},... | collective-permute-start | bytes 196616 | tf_op jit(solution)/shard_map/ppermute | solution.py:310
  5.8 5.8 %collective-permute-start.1 = (bf16[256,128]{1,0:T(8,128)(2,1)}, bf16[256,128]{1,0:T(8,128)(2,1)S(1)}, u32[]{:S(2)}, u32[]{:S(2)}) collective-permute-start(bf16[256,128]{1,0:T(8,128)(2,1)} %param.8), channel_id=1, source_target_pairs={{0,4},{4,0},{8,12},{12,8},{1,5},{5,1},{9,13},{13,9},{2,6},{6,2},{1... | collective-permute-start | bytes 196616 | tf_op jit(solution)/shard_map/ppermute | solution.py:310
  6.4 6.1 %collective-permute-start.4 = (bf16[256,256]{1,0:T(8,128)(2,1)}, bf16[256,256]{1,0:T(8,128)(2,1)S(1)}, u32[]{:S(2)}, u32[]{:S(2)}) collective-permute-start(bf16[256,256]{1,0:T(8,128)(2,1)} %cot_ref.1), channel_id=1, source_target_pairs={{0,2},{1,3},{2,0},{3,1},{4,6},{5,7},{6,4},{7,5},{8,10},{9,11},{10,... | collective-permute-start | bytes 393224 | tf_op jit(solution)/shard_map/ppermute | solution.py:310
  11.4 7.7 %copy-start = (bf16[256,256]{1,0:T(8,128)(2,1)S(1)}, bf16[256,256]{1,0:T(8,128)(2,1)}, u32[]{:S(2)}) copy-start(bf16[256,256]{1,0:T(8,128)(2,1)} %cot_ref.1) | copy-start | bytes 393220
  11.4 7.6 %copy-start.1 = (bf16[128,256]{1,0:T(8,128)(2,1)S(1)}, bf16[128,256]{1,0:T(8,128)(2,1)}, u32[]{:S(2)}) copy-start(bf16[128,256]{1,0:T(8,128)(2,1)} %weight_ref.1) | copy-start | bytes 196612
  11.4 7.6 %copy-start.2 = (f32[256]{0:T(256)S(1)}, f32[256]{0:T(256)}, u32[]{:S(2)}) copy-start(f32[256]{0:T(256)} %param.14) | copy-start | bytes 3076
  12.0 1.4 %collective-permute-start.3 = (bf16[512,128]{1,0:T(8,128)(2,1)S(1)}, bf16[512,128]{1,0:T(8,128)(2,1)S(1)}, u32[]{:S(2)}, u32[]{:S(2)}) collective-permute-start(bf16[512,128]{1,0:T(8,128)(2,1)S(1)} %forward_sibling.1), channel_id=1, source_target_pairs={{0,1},{1,0},{2,3},{3,2},{4,5},{5,4},{6,7},{7,6},{8,9},{9,8},{10,11... | collective-permute-start | bytes 393224 | tf_op jit(solution)/shard_map/ppermute | solution.py:310
  13.4 5.6 %collective-permute-start.5 = (bf16[512,128]{1,0:T(8,128)(2,1)S(1)}, bf16[512,128]{1,0:T(8,128)(2,1)S(1)}, u32[]{:S(2)}, u32[]{:S(2)}) collective-permute-start(bf16[512,128]{1,0:T(8,128)(2,1)S(1)} %add_convert_fusion.near_ref), channel_id=1, source_target_pairs={{0,2},{1,3},{2,0},{3,1},{4,6},{5,7},{6,4},{7,5},{8,10},{9,11},{10,... | collective-permute-start | bytes 393224 | tf_op jit(solution)/shard_map/ppermute | solution.py:310
  19.6 1.5 %collective-permute-start.6 = (bf16[784,128]{1,0:T(8,128)(2,1)S(1)}, bf16[784,128]{1,0:T(8,128)(2,1)S(1)}, u32[]{:S(2)}, u32[]{:S(2)}) collective-permute-start(bf16[784,128]{1,0:T(8,128)(2,1)S(1)} %get-tuple-element.34.own_ref), channel_id=1, source_target_pairs={{0,1},{1,0},{2,3},{3,2},{4,5},{5,4},{6,7},{7,6},{8,9},{9,8},{10,11... | collective-permute-start | bytes 602120 | tf_op jit(solution)/shard_map/ppermute | solution.py:310
  21.2 5.5 %collective-permute-start.9 = (bf16[144,128]{1,0:T(8,128)(2,1)S(1)}, bf16[144,128]{1,0:T(8,128)(2,1)S(1)}, u32[]{:S(2)}, u32[]{:S(2)}) collective-permute-start(bf16[144,128]{1,0:T(8,128)(2,1)S(1)} %stripe.1), channel_id=1, source_target_pairs={{0,8},{4,12},{8,0},{12,4},{1,9},{5,13},{9,1},{13,5},{2,10},{6,14},... | collective-permute-start | bytes 110600 | tf_op jit(solution)/shard_map/ppermute | solution.py:310
  23.7 7.8 %collective-permute-start.7 = (bf16[256,128]{1,0:T(8,128)(2,1)S(1)}, bf16[256,128]{1,0:T(8,128)(2,1)S(1)}, u32[]{:S(2)}, u32[]{:S(2)}) collective-permute-start(bf16[256,128]{1,0:T(8,128)(2,1)S(1)} %get-tuple-element.38), channel_id=1, source_target_pairs={{0,4},{4,0},{8,12},{12,8},{1,5},{5,1},{9,13},{13,9},{2,6},{6,2},{1... | collective-permute-start | bytes 196616 | tf_op jit(solution)/shard_map/ppermute | solution.py:310
  25.9 6.9 %collective-permute-start.8 = (bf16[256,128]{1,0:T(8,128)(2,1)S(1)}, bf16[256,128]{1,0:T(8,128)(2,1)S(1)}, u32[]{:S(2)}, u32[]{:S(2)}) collective-permute-start(bf16[256,128]{1,0:T(8,128)(2,1)S(1)} %get-tuple-element.39), channel_id=1, source_target_pairs={{0,8},{4,12},{8,0},{12,4},{1,9},{5,13},{9,1},{13,5},{2,10},{6,14},... | collective-permute-start | bytes 196616 | tf_op jit(solution)/shard_map/ppermute | solution.py:310
  26.7 4.7 %collective-permute-start.11 = (bf16[144,128]{1,0:T(8,128)(2,1)S(1)}, bf16[144,128]{1,0:T(8,128)(2,1)S(1)}, u32[]{:S(2)}, u32[]{:S(2)}) collective-permute-start(bf16[144,128]{1,0:T(8,128)(2,1)S(1)} %add_convert_fusion.1.pair_ref), channel_id=1, source_target_pairs={{0,4},{4,0},{8,12},{12,8},{1,5},{5,1},{9,13},{13,9},{2,6},{6,2},{1... | collective-permute-start | bytes 110600 | tf_op jit(solution)/shard_map/ppermute | solution.py:310
  27.8 6.2 %collective-permute-start.10 = (bf16[256,128]{1,0:T(8,128)(2,1)S(1)}, bf16[256,128]{1,0:T(8,128)(2,1)S(1)}, u32[]{:S(2)}, u32[]{:S(2)}) collective-permute-start(bf16[256,128]{1,0:T(8,128)(2,1)S(1)} %get-tuple-element.41), channel_id=1, source_target_pairs={{0,12},{4,8},{8,4},{12,0},{1,13},{5,9},{9,5},{13,1},{2,14},{6,10},... | collective-permute-start | bytes 196616 | tf_op jit(solution)/shard_map/ppermute | solution.py:310
  31.4 2.6 %collective-permute-start.12 = (f32[128,128]{1,0:T(8,128)S(1)}, f32[128,128]{1,0:T(8,128)S(1)}, u32[]{:S(2)}, u32[]{:S(2)}) collective-permute-start(f32[128,128]{1,0:T(8,128)S(1)} %convert_add_fusion.1.half_ref), channel_id=1, source_target_pairs={{0,1},{1,0},{2,3},{3,2},{4,5},{5,4},{6,7},{7,6},{8,9},{9,8},{10,11... | collective-permute-start | bytes 196616 | tf_op jit(solution)/shard_map/ppermute | solution.py:310
